TPU v7x, 32 devices: a whole 2x2x4 slice. The times are simulated.
32 devices in a mesh: seq: 4 (over z), wide: 8 (over y, x, core).
Axes of the slice: x: 2, y: 2, z: 4, core: 2. Of those that a mesh axis runs over, the one named last changes fastest.
Arguments:
- tokens: bfloat16 [4, 1024, 2048], P('seq', 'wide'), may hold values from -6 to 6
- cotangent: bfloat16 [4, 1024, 2048], P('seq', 'wide'), may hold values from -6 to 6
- norm_gains: bfloat16 [2, 2048], P(None, 'wide'), may hold values from 0.5 to 1.5
- in_weight: bfloat16 [2048, 2, 2560], P('wide'), may hold values from -0.125 to 0.125
- conv_weight: bfloat16 [4, 2560], P(None, 'wide'), may hold values from -3 to 3
- conv_bias: bfloat16 [2560], P('wide'), may hold values from -3 to 3
- gate_weights: bfloat16 [2, 10, 256, 256], P(None, None, None, 'wide'), may hold values from -0.375 to 0.375
- gate_biases: bfloat16 [2, 2560], P(None, 'wide'), may hold values from -4 to 4
- decay_param: bfloat16 [2560], P('wide'), as said below
- out_weight: bfloat16 [2560, 2048], P('wide'), may hold values from -0.125 to 0.125
- mlp_in_weight: bfloat16 [2048, 2, 6144], P(None, None, 'wide'), may hold values from -0.125 to 0.125
- mlp_out_weight: bfloat16 [6144, 2048], P('wide'), may hold values from -0.078125 to 0.078125
Outputs:
- output: bfloat16 [4, 1024, 2048], P('seq', 'wide')
- input_grad: float32 [4, 1024, 2048], P('seq', 'wide')
- norm_gains_grad: float32 [2, 2048], P(None, 'wide')
- in_weight_grad: float32 [2048, 2, 2560], P('wide')
- conv_weight_grad: float32 [4, 2560], P(None, 'wide')
- conv_bias_grad: float32 [2560], P('wide')
- gate_weights_grad: float32 [2, 10, 256, 256], P(None, None, None, 'wide')
- gate_biases_grad: float32 [2, 2560], P(None, 'wide')
- decay_param_grad: float32 [2560], P('wide')
- out_weight_grad: float32 [2560, 2048], P('wide')
- mlp_in_weight_grad: float32 [2048, 2, 6144], P(None, None, 'wide')
- mlp_out_weight_grad: float32 [6144, 2048], P('wide')
Inputs may be any that keep to these rules, and one draw needn't show every extreme that they name: softplus(-decay_param) lies between 0.05 / 1024 and 0.03 in every channel.
All inputs are finite; a program needn't handle non-finite values.
Results may differ from a plain program's by a relative error of at most 0.011.
Values may be sent and summed in bfloat16 or wider, within the bound.
No kernel may reach another device: no remote copies, remote signals or barrier semaphores. Data moves between devices by JAX's collectives and lax.ppermute only.
A program may use at most 320 MiB of HBM per device.

v0:
```python
import jax
import jax.numpy as jnp
from jax import lax
from jax.sharding import PartitionSpec as P


def shifted(block, axis, distance):
    devices = range(lax.axis_size(axis))
    route = [(i - distance, i) for i in devices if i - distance in devices]
    return lax.ppermute(block, axis, route)


def rms_scale(values, gain):
    return values * lax.rsqrt(jnp.mean(values * values, axis=-1, keepdims=True) + 1e-06) * gain


def gate_math(gate_pre, conv_values, decay_param):
    recur_gate = jax.nn.sigmoid(gate_pre[0])
    input_gate = jax.nn.sigmoid(gate_pre[1])
    log_decay = -8.0 * recur_gate * jax.nn.softplus(-decay_param)
    inflow = jnp.sqrt(-jnp.expm1(2.0 * log_decay)) * input_gate * conv_values
    return (log_decay, inflow)


def gelu_product(gate_values, other_values):
    return jax.nn.gelu(gate_values) * other_values


def affine_combine(earlier, later):
    return (earlier[0] * later[0], later[0] * earlier[1] + later[1])


def shards(
    tokens,
    cotangent,
    norm_gains,
    in_weight,
    conv_weight,
    conv_bias,
    gate_weights,
    gate_biases,
    decay_param,
    out_weight,
    mlp_in_weight,
    mlp_out_weight,
):
    rows = tokens[0].astype(jnp.float32)
    cot_low = cotangent[0]
    cot_rows = cot_low.astype(jnp.float32)
    tok_rows = rows.shape[0]
    width = rows.shape[1]
    gains_all, in_all, conv_all, cbias_all, gatew_all, gateb_all, decay_all = (
        lax.all_gather(norm_gains, "wide", axis=1, tiled=True),
        lax.all_gather(in_weight, "wide", axis=0, tiled=True),
        lax.all_gather(conv_weight, "wide", axis=1, tiled=True),
        lax.all_gather(conv_bias, "wide", axis=0, tiled=True),
        lax.all_gather(gate_weights, "wide", axis=3, tiled=True),
        lax.all_gather(gate_biases, "wide", axis=1, tiled=True),
        lax.all_gather(decay_param, "wide", axis=0, tiled=True),
    )
    gains_f = gains_all.astype(jnp.float32)
    lru_width = in_all.shape[2]
    heads = gatew_all.shape[1]
    block_width = gatew_all.shape[2]
    taps = conv_all.shape[0]
    normed_f, norm_pull = jax.vjp(rms_scale, rows, gains_f[0])
    normed = normed_f.astype(jnp.bfloat16)
    in_flat = in_all.reshape(width, 2 * lru_width)
    projected = jnp.dot(normed, in_flat, preferred_element_type=jnp.float32)
    branch = projected[:, :lru_width].astype(jnp.bfloat16)
    gate_branch = projected[:, lru_width:]
    previous = shifted(branch[tok_rows - (taps - 1) :], "wide", 1)
    extended = jnp.concatenate([previous, branch], axis=0).astype(jnp.float32)
    conv_f = conv_all.astype(jnp.float32)
    conv_out = cbias_all.astype(jnp.float32)
    for offset in range(taps):
        conv_out = (
            conv_out + conv_f[offset] * extended[taps - 1 - offset : taps - 1 - offset + tok_rows]
        )
    conv_low = conv_out.astype(jnp.bfloat16)
    conv_blocks = conv_low.reshape(tok_rows, heads, block_width)
    gate_pre = (
        jnp.einsum(
            "thc,ghcd->gthd", conv_blocks, gatew_all, preferred_element_type=jnp.float32
        ).reshape(2, tok_rows, lru_width)
        + gateb_all.astype(jnp.float32)[:, None, :]
    )
    (log_decay, inflow), gate_pull = jax.vjp(
        gate_math, gate_pre, conv_low.astype(jnp.float32), decay_all.astype(jnp.float32)
    )
    decay_chan, inflow_chan, branch_chan = (
        lax.all_to_all(log_decay, "wide", split_axis=1, concat_axis=0, tiled=True),
        lax.all_to_all(inflow, "wide", split_axis=1, concat_axis=0, tiled=True),
        lax.all_to_all(gate_branch, "wide", split_axis=1, concat_axis=0, tiled=True),
    )
    factor_chan = jnp.exp(decay_chan)
    state_chan = lax.associative_scan(affine_combine, (factor_chan, inflow_chan), axis=0)[1]
    mixed_chan_f, mix_pull = jax.vjp(gelu_product, branch_chan, state_chan)
    mixed_chan = mixed_chan_f.astype(jnp.bfloat16)
    middle = rows + lax.psum_scatter(
        jnp.dot(mixed_chan, out_weight, preferred_element_type=jnp.float32),
        "wide",
        scatter_dimension=0,
        tiled=True,
    )
    normed_two_f, norm_two_pull = jax.vjp(rms_scale, middle, gains_f[1])
    normed_two = normed_two_f.astype(jnp.bfloat16)
    every_normed, every_cot = (
        lax.all_gather(normed_two, "wide", axis=0, tiled=True),
        lax.all_gather(cot_low, "wide", axis=0, tiled=True),
    )
    hidden_width = mlp_in_weight.shape[2]
    mlp_in_flat = mlp_in_weight.reshape(width, 2 * hidden_width)
    gate_up = jnp.dot(every_normed, mlp_in_flat, preferred_element_type=jnp.float32)
    hidden_f, hidden_pull = jax.vjp(
        gelu_product, gate_up[:, :hidden_width], gate_up[:, hidden_width:]
    )
    hidden = hidden_f.astype(jnp.bfloat16)
    feed = lax.psum_scatter(
        jnp.dot(hidden, mlp_out_weight, preferred_element_type=jnp.float32),
        "wide",
        scatter_dimension=0,
        tiled=True,
    )
    result = (middle + feed).astype(jnp.bfloat16)
    hidden_grad = jnp.dot(every_cot, mlp_out_weight.T, preferred_element_type=jnp.float32)
    mlp_out_grad = jnp.dot(hidden.T, every_cot, preferred_element_type=jnp.float32)
    gate_grad, up_grad = hidden_pull(hidden_grad)
    gate_up_grad = jnp.concatenate([gate_grad, up_grad], axis=1).astype(jnp.bfloat16)
    mlp_in_grad = jnp.dot(every_normed.T, gate_up_grad, preferred_element_type=jnp.float32).reshape(
        width, 2, hidden_width
    )
    normed_two_grad = lax.psum_scatter(
        jnp.dot(gate_up_grad, mlp_in_flat.T, preferred_element_type=jnp.float32),
        "wide",
        scatter_dimension=0,
        tiled=True,
    )
    middle_norm_grad, gain_two_grad = norm_two_pull(normed_two_grad)
    middle_grad = cot_rows + middle_norm_grad
    mix_low = middle_grad.astype(jnp.bfloat16)
    mix_every = lax.all_gather(mix_low, "wide", axis=0, tiled=True)
    out_grad = jnp.dot(mixed_chan.T, mix_every, preferred_element_type=jnp.float32)
    mixed_grad_chan = jnp.dot(mix_every, out_weight.T, preferred_element_type=jnp.float32)
    branch_grad_chan, sgrad_chan = mix_pull(mixed_grad_chan)
    next_factor = jnp.concatenate([factor_chan[1:], jnp.zeros_like(factor_chan[:1])], axis=0)
    carried = lax.associative_scan(affine_combine, (next_factor[::-1], sgrad_chan[::-1]), axis=0)[
        1
    ][::-1]
    prior_state = jnp.concatenate([jnp.zeros_like(state_chan[:1]), state_chan[:-1]], axis=0)
    decay_grad_chan = carried * factor_chan * prior_state
    decay_grad, inflow_grad, gate_branch_grad = (
        lax.all_to_all(decay_grad_chan, "wide", split_axis=0, concat_axis=1, tiled=True),
        lax.all_to_all(carried, "wide", split_axis=0, concat_axis=1, tiled=True),
        lax.all_to_all(branch_grad_chan, "wide", split_axis=0, concat_axis=1, tiled=True),
    )
    pre_grad, conv_grad_local, decay_param_grad = gate_pull((decay_grad, inflow_grad))
    pre_low = pre_grad.astype(jnp.bfloat16)
    gate_bias_grad = jnp.sum(pre_low.astype(jnp.float32), axis=1)
    pre_blocks = pre_low.reshape(2, tok_rows, heads, block_width)
    gate_weight_grad = jnp.einsum(
        "thc,gthd->ghcd", conv_blocks, pre_blocks, preferred_element_type=jnp.float32
    )
    conv_grad = conv_grad_local + jnp.einsum(
        "gthd,ghcd->thc", pre_blocks, gatew_all, preferred_element_type=jnp.float32
    ).reshape(tok_rows, lru_width)
    following = shifted(conv_grad[: taps - 1], "wide", -1)
    grad_extended = jnp.concatenate([conv_grad, following], axis=0)
    branch_grad = jnp.zeros((tok_rows, lru_width), jnp.float32)
    tap_grads = []
    for offset in range(taps):
        branch_grad = branch_grad + conv_f[offset] * grad_extended[offset : offset + tok_rows]
        tap_grads.append(
            jnp.sum(conv_grad * extended[taps - 1 - offset : taps - 1 - offset + tok_rows], axis=0)
        )
    conv_weight_grad = jnp.stack(tap_grads)
    conv_bias_grad = jnp.sum(conv_grad, axis=0)
    projected_low = jnp.concatenate([branch_grad, gate_branch_grad], axis=1).astype(jnp.bfloat16)
    in_full = jnp.dot(normed.T, projected_low, preferred_element_type=jnp.float32).reshape(
        width, 2, lru_width
    )
    normed_grad = jnp.dot(projected_low, in_flat.T, preferred_element_type=jnp.float32)
    rows_norm_grad, gain_one_grad = norm_pull(normed_grad)
    input_grad = middle_grad + rows_norm_grad
    gains_full = jnp.stack([gain_one_grad, gain_two_grad])
    gains_part, in_part, conv_part, cbias_part, gatew_part, gateb_part, decay_part = (
        lax.psum_scatter(gains_full, "wide", scatter_dimension=1, tiled=True),
        lax.psum_scatter(in_full, "wide", scatter_dimension=0, tiled=True),
        lax.psum_scatter(conv_weight_grad, "wide", scatter_dimension=1, tiled=True),
        lax.psum_scatter(conv_bias_grad, "wide", scatter_dimension=0, tiled=True),
        lax.psum_scatter(gate_weight_grad, "wide", scatter_dimension=3, tiled=True),
        lax.psum_scatter(gate_bias_grad, "wide", scatter_dimension=1, tiled=True),
        lax.psum_scatter(decay_param_grad, "wide", scatter_dimension=0, tiled=True),
    )
    totals = lax.psum(
        (
            gains_part,
            in_part,
            conv_part,
            cbias_part,
            gatew_part,
            gateb_part,
            decay_part,
            out_grad,
            mlp_in_grad,
            mlp_out_grad,
        ),
        "seq",
    )
    return (
        result[None],
        input_grad[None],
        totals[0],
        totals[1],
        totals[2],
        totals[3],
        totals[4],
        totals[5],
        totals[6],
        totals[7],
        totals[8],
        totals[9],
    )


def solution(mesh):
    placed = (
        P("seq", "wide", None),
        P("seq", "wide", None),
        P(None, "wide"),
        P("wide", None, None),
        P(None, "wide"),
        P("wide"),
        P(None, None, None, "wide"),
        P(None, "wide"),
        P("wide"),
        P("wide", None),
        P(None, None, "wide"),
        P("wide", None),
    )
    return jax.shard_map(
        shards,
        mesh=mesh,
        in_specs=placed,
        out_specs=(
            P("seq", "wide", None),
            P("seq", "wide", None),
            P(None, "wide"),
            P("wide", None, None),
            P(None, "wide"),
            P("wide"),
            P(None, None, None, "wide"),
            P(None, "wide"),
            P("wide"),
            P("wide", None),
            P(None, None, "wide"),
            P("wide", None),
        ),
        check_vma=False,
    )
```

profile of v0, /device:TPU:0, one launch (start us, length us, event | category | flops | bytes accessed | tf_op | source)
XLA Modules:
  0.0 3139.7 jit_solution(15624747235389135180)
XLA Ops:
  38.4 24.1 all-reduce.51
  63.8 56.8 %all-gather.9.cloned.1.call-done = bf16[2048,2,2560]{2,1,0:T(2,128)(2,1)} async-done(((bf16[256,2,2560]{2,1,0:T(2,128)(2,1)}), bf16[2048,2,2560]{2,1,0:T(2,128)(2,1)}) %all-gather.9.cloned.1.call-update) | async-done | bytes 20971536 | tf_op jit(solution)/shard_map/all_gather | solution.py:54
  209.2 24.5 slice.575
  233.7 24.5 slice.580
  258.2 24.5 slice.576
  289.7 24.5 slice.648
  314.2 24.5 slice.578
  338.7 24.5 slice.577
  696.1 26.4 pad.148
  722.5 26.5 pad.149
  759.5 72.7 %reduce-scatter.15.cloned.1.call-done = f32[128,2048]{1,0:T(8,128)} async-done(((f32[1024,2048]{1,0:T(8,128)}), f32[128,2048]{1,0:T(8,128)}) %reduce-scatter.15.cloned.1.call-update) | async-done | bytes 1048592 | tf_op jit(solution)/shard_map/reduce_scatter | solution.py:100
  843.3 29.4 all-gather.13.cloned.1.call-done
  884.7 26.6 all-gather.17.cloned.1.call-done
  932.9 71.4 %reduce-scatter.19.cloned.1.call-done = f32[128,2048]{1,0:T(8,128)} async-done(((f32[1024,2048]{1,0:T(8,128)}), f32[128,2048]{1,0:T(8,128)}) %reduce-scatter.19.cloned.1.call-update) | async-done | bytes 1048592 | tf_op jit(solution)/shard_map/reduce_scatter | solution.py:133
  1012.0 24.7 slice.663
  1036.6 24.5 slice.656
  1061.1 24.5 slice.654
  1115.8 24.7 slice.660
  1140.5 24.5 slice.658
  1392.6 24.7 slice.732
  1542.1 26.6 pad.168
  1568.7 26.4 pad.169
  1728.3 21.1 fusion.74
  1772.7 20.8 copy.282
  1826.6 170.7 %reduce-scatter.21.cloned.1.call-done = f32[256,2,2560]{2,0,1:T(8,128)} async-done(((f32[2048,2,2560]{2,0,1:T(8,128)}), f32[256,2,2560]{2,0,1:T(8,128)}) %reduce-scatter.21.cloned.1.call-update) | async-done | bytes 5242896 | tf_op jit(solution)/shard_map/reduce_scatter | solution.py:188
  1997.9 23.1 all-reduce.48
  2021.2 16.6 reduce-scatter.29.cloned.1.call-done
  2038.8 73.7 %reduce-scatter.17.cloned.1.call-done = f32[128,2048]{1,0:T(8,128)} async-done(((f32[1024,2048]{1,0:T(8,128)}), f32[128,2048]{1,0:T(8,128)}) %reduce-scatter.17.cloned.1.call-update) | async-done | bytes 1048592 | tf_op jit(solution)/shard_map/reduce_scatter | solution.py:119
  2116.6 35.3 %reduce-scatter.25.cloned.1.call-done = f32[256,2]{1,0:T(8,128)} async-done(((f32[2048,2]{1,0:T(8,128)}), f32[256,2]{1,0:T(8,128)}) %reduce-scatter.25.cloned.1.call-update) | async-done | bytes 2064
  2152.9 40.6 %reduce-scatter.27.cloned.1.call-done = f32[320,4]{1,0:T(8,128)} async-done(((f32[2560,4]{1,0:T(8,128)}), f32[320,4]{1,0:T(8,128)}) %reduce-scatter.27.cloned.1.call-update) | async-done | bytes 5136
  2194.4 20.0 all-reduce.49
  2214.4 892.9 %all-reduce.54.cloned.1.call-done = (f32[256,2,2560]{2,0,1:T(8,128)}, f32[2,10,256,32]{2,3,0,1:T(8,128)}, f32[320,2048]{1,0:T(8,128)}, f32[2048,2,768]{2,1,0:T(2,128)}, f32[768,2048]{1,0:T(8,128)}) async-done(((f32[256,2,2560]{2,0,1:T(8,128)}, f32[2,10,256,32]{2,3,0,1:T(8,128)}, f32[320,2048]{1,0:T(8,128)}, f32[2048,2,768]{2,1,0:T(2,128)}, f32[768,2048]{1,0:T(8,128)}), (f32[256,2,2560]{2,0,1:T(8,128)}, ...) | async-done | bytes 27394064 | tf_op jit(solution)/shard_map/psum | solution.py:195
  (566 shorter events, 1127.1 us)
Async XLA Ops:
  7.2 904.1 %copy-start = (bf16[768,2048]{1,0:T(8,128)(2,1)S(1)}, bf16[768,2048]{1,0:T(8,128)(2,1)}, u32[]{:S(2)}) copy-start(bf16[768,2048]{1,0:T(8,128)(2,1)} %param.23) | copy-start | bytes 9437188
  7.3 113.3 %all-gather.9.cloned.1.call-start = ((), (), s32[]{:S(2)}) async-start(), calls=%async_computation.14 | async-start | bytes 23592960 | tf_op jit(solution)/shard_map/all_gather | solution.py:54
  8.0 145.3 %all-gather.11.cloned.1.call-start = ((), (), s32[]{:S(2)}) async-start(), calls=%async_computation.15 | async-start | bytes 2949120 | tf_op jit(solution)/shard_map/all_gather | solution.py:57
  63.7 71.1 %copy-start.77 = (f32[128]{0:T(128)}, f32[128]{0:T(128)S(1)}, u32[]{:S(2)}) copy-start(f32[128]{0:T(128)S(1)} %fusion.60) | copy-start | bytes 1540
  63.7 71.1 %copy-start.65 = (f32[128]{0:T(128)}, f32[128]{0:T(128)S(1)}, u32[]{:S(2)}) copy-start(f32[128]{0:T(128)S(1)} %fusion.97) | copy-start | bytes 1540
  63.8 71.0 %copy-start.59 = (f32[1,2048]{1,0:T(1,128)}, f32[1,2048]{1,0:T(1,128)S(1)}, u32[]{:S(2)}) copy-start(f32[1,2048]{1,0:T(1,128)S(1)} %get-tuple-element.156) | copy-start | bytes 24580
  144.1 3.6 collective-permute-start
  174.1 23.0 all-to-all-start.2
  197.1 85.6 %all-to-all-start.1 = ((f32[128,8,320]{0,2,1:T(8,128)}), f32[128,8,320]{0,2,1:T(8,128)}, u32[]{:S(2)}, u32[]{:S(2)}) async-start(f32[128,8,320]{0,2,1:T(8,128)} %bitcast.278), calls=%async_computation.1 | async-start | bytes 2621440 | tf_op jit(solution)/shard_map/all_to_all | solution.py:93
  282.7 466.3 %all-to-all-start = ((f32[128,8,320]{0,2,1:T(8,128)}), f32[128,8,320]{0,2,1:T(8,128)}, u32[]{:S(2)}, u32[]{:S(2)}) async-start(f32[128,8,320]{0,2,1:T(8,128)} %bitcast.275), calls=%async_computation | async-start | bytes 2621440 | tf_op jit(solution)/shard_map/all_to_all | solution.py:94
  287.0 545.3 %reduce-scatter.15.cloned.1.call-start = ((), (), s32[]{:S(2)}) async-start(), calls=%async_computation.16 | async-start | bytes 9437184 | tf_op jit(solution)/shard_map/reduce_scatter | solution.py:100
  420.6 33.9 %copy-start.31 = (f32[256,320]{0,1:T(8,128)}, f32[256,320]{0,1:T(8,128)S(1)}, u32[]{:S(2)}) copy-start(f32[256,320]{0,1:T(8,128)S(1)} %get-tuple-element.122) | copy-start | bytes 983044
  759.5 113.2 %all-gather.13.cloned.1.call-start = ((), (), s32[]{:S(2)}) async-start(), calls=%async_computation.17 | async-start | bytes 4718592 | tf_op jit(solution)/shard_map/all_gather | solution.py:109
  833.9 172.9 %copy-start.67 = (f32[128]{0:T(128)}, f32[128]{0:T(128)S(1)}, u32[]{:S(2)}) copy-start(f32[128]{0:T(128)S(1)} %fusion.98) | copy-start | bytes 1540
  835.8 75.5 %all-gather.17.cloned.1.call-start = ((), (), s32[]{:S(2)}) async-start(), calls=%async_computation.23 | async-start | bytes 4718592 | tf_op jit(solution)/shard_map/all_gather | solution.py:110
  836.4 167.9 %reduce-scatter.19.cloned.1.call-start = ((), (), s32[]{:S(2)}) async-start(), calls=%async_computation.19 | async-start | bytes 9437184 | tf_op jit(solution)/shard_map/reduce_scatter | solution.py:133
  932.8 176.9 %all-gather.15.cloned.1.call-start = ((), (), s32[]{:S(2)}) async-start(), calls=%async_computation.20 | async-start | bytes 4718592 | tf_op jit(solution)/shard_map/all_gather | solution.py:142
  1236.7 33.6 %copy-start.32 = (f32[256,320]{0,1:T(8,128)}, f32[256,320]{0,1:T(8,128)S(1)}, u32[]{:S(2)}) copy-start(f32[256,320]{0,1:T(8,128)S(1)} %get-tuple-element.120) | copy-start | bytes 983044
  1614.8 22.5 all-to-all-start.4
  1637.3 22.5 all-to-all-start.3
  1641.6 185.0 %reduce-scatter.23.cloned.1.call-start = ((), (), s32[]{:S(2)}) async-start(), calls=%async_computation.22 | async-start | bytes 5898240 | tf_op jit(solution)/shard_map/reduce_scatter | solution.py:191
  1689.9 27.8 all-to-all-start.5
  1694.1 303.1 %reduce-scatter.21.cloned.1.call-start = ((), (), s32[]{:S(2)}) async-start(), calls=%async_computation.21 | async-start | bytes 47185920 | tf_op jit(solution)/shard_map/reduce_scatter | solution.py:188
  1716.5 3.5 collective-permute-start.1
  1749.5 288.3 %reduce-scatter.29.cloned.1.call-start = ((), (), s32[]{:S(2)}) async-start(), calls=%async_computation.26 | async-start | bytes 1474560
  1751.0 361.5 %reduce-scatter.17.cloned.1.call-start = ((), (), s32[]{:S(2)}) async-start(), calls=%async_computation.18 | async-start | bytes 9437184 | tf_op jit(solution)/shard_map/reduce_scatter | solution.py:119
  1758.7 393.2 %reduce-scatter.25.cloned.1.call-start = ((), (), s32[]{:S(2)}) async-start(), calls=%async_computation.24 | async-start | bytes 1179648
  1819.2 374.2 %reduce-scatter.27.cloned.1.call-start = ((), (), s32[]{:S(2)}) async-start(), calls=%async_computation.25 | async-start | bytes 1474560
  1820.9 1286.4 %all-reduce.54.cloned.1.call-start = ((), (), s32[]{:S(2)}) async-start(), calls=%async_computation.27 | async-start | bytes 54788096 | tf_op jit(solution)/shard_map/psum | solution.py:195
  1997.2 41.5 %copy-start.78 = (f32[128]{0:T(128)S(1)}, f32[128]{0:T(128)}, u32[]{:S(2)}) copy-start(f32[128]{0:T(128)} %copy-done.77) | copy-start | bytes 1540
  1997.2 115.2 %copy-start.68 = (f32[128]{0:T(128)S(1)}, f32[128]{0:T(128)}, u32[]{:S(2)}) copy-start(f32[128]{0:T(128)} %copy-done.67) | copy-start | bytes 1540
  1997.3 115.2 %copy-start.71 = (f32[128]{0:T(128)S(1)}, f32[128]{0:T(128)}, u32[]{:S(2)}) copy-start(f32[128]{0:T(128)} %copy-done.70) | copy-start | bytes 1540
  (74 other events, 535.1 us)
Sparse Core Ops, SparseCore 0:
  10.0 110.5 all-gather.8
  123.0 30.1 all-gather.10
  759.6 72.6 reduce-scatter.14
  835.9 36.6 all-gather.12
  874.5 36.7 all-gather.16
  932.9 71.2 reduce-scatter.18
  1009.2 36.6 all-gather.14
  1677.2 58.2 reduce-scatter.22
  1749.6 247.6 reduce-scatter.20
  2000.3 37.3 reduce-scatter.28
  2041.2 71.2 reduce-scatter.16
  2115.8 36.0 reduce-scatter.24
  2156.1 37.3 reduce-scatter.26
  2197.3 909.9 all-reduce.53
where the time goes:
time: 3160 us; the launch traced here: 3140 us
  waiting for transfers between devices  1530 us (48%)
  local copies, waits for them, and re-layouts  1170 us (37%)
  other arithmetic  166 us (5%)
  matrix products  137 us (4%)
  blocking collectives  94.4 us (3%)
    psum x1, waiting for transfers between devices, shards(): lax.psum((gains_part, in_part, conv_part, cbias_part, gatew_part, gateb_p...  893 us
    slice x60, local copies, waits for them, and re-layouts, shards(): lax.associative_scan(affine_combine, (next_factor[::-1], sgrad_chan[::-1]...  373 us
    slice x56, local copies, waits for them, and re-layouts, shards(): lax.associative_scan(affine_combine, (factor_chan, inflow_chan), axis=0)[1]  342 us
    reduce_scatter x1, waiting for transfers between devices, shards(): lax.psum_scatter(in_full, 'wide', scatter_dimension=0, tiled=True)  171 us
    pad x18, local copies, waits for them, and re-layouts, shards(): lax.associative_scan(affine_combine, (factor_chan, inflow_chan), axis=0)[1]  123 us
    pad x18, local copies, waits for them, and re-layouts, shards(): lax.associative_scan(affine_combine, (next_factor[::-1], sgrad_chan[::-1]...  123 us
    unnamed x17, waiting for transfers between devices  93.8 us
    unnamed x201, local copies, waits for them, and re-layouts  93.5 us
  transfers between devices with their start and end apart: 22, of which 15 were waited for; matrix products, arithmetic and copies ran while one was open for 27% of the time, Pallas kernels for 0%

commit v1 on v0

v1 whole, which is shorter than its diff:
```python
import functools
import math
import jax
import jax.numpy as jnp
from jax import lax
from jax.experimental import pallas as pl
from jax.experimental.pallas import tpu as pltpu
from jax.sharding import PartitionSpec as P

BF16 = jnp.bfloat16
F32 = jnp.float32
SUB = 8
LANES = 128
GELU_A = math.sqrt(2.0 / math.pi)
GELU_B = 0.044715


def gelu_parts(v):
    square = v * v
    th = jnp.tanh(GELU_A * v * (1.0 + GELU_B * square))
    value = 0.5 * v * (1.0 + th)
    slope = 0.5 * (1.0 + th) + 0.5 * v * (1.0 - th * th) * (
        GELU_A * (1.0 + 3.0 * GELU_B * square)
    )
    return value, slope


def minus_expm1(v):
    series = jnp.full_like(v, 1.0 / 40320.0)
    for factorial in (5040.0, 720.0, 120.0, 24.0, 6.0, 2.0, 1.0):
        series = series * v + 1.0 / factorial
    return jnp.where(v > -0.5, -v * series, 1.0 - jnp.exp(v))


def sub_iota(width):
    return lax.broadcasted_iota(jnp.int32, (SUB, width), 0)


def roll_down(v, first):
    return jnp.where(sub_iota(v.shape[1]) == 0, first, pltpu.roll(v, 1, 0))


def roll_up(v, last):
    return jnp.where(sub_iota(v.shape[1]) == SUB - 1, last, pltpu.roll(v, SUB - 1, 0))


def rows8(step):
    return pl.ds(pl.multiple_of(step * SUB, SUB), SUB)


def strided_load(refs, s, steps):
    return jnp.concatenate([r[pl.ds(s, SUB, stride=steps), :] for r in refs], axis=1)


def strided_store(ref, s, steps, v):
    for n in range(ref.shape[0]):
        ref.at[n][pl.ds(s, SUB, stride=steps), :] = v[:, n * LANES : (n + 1) * LANES]


def forward_kernel(*refs, taps, groups):
    branch_refs, gateb_refs = refs[:groups], refs[groups : 2 * groups]
    forward_body(branch_refs, gateb_refs, *refs[2 * groups :], taps=taps)


def forward_body(
    branch_refs,
    gateb_refs,
    chan_ref,
    gw_ref,
    mixed_ref,
    states_ref,
    decay_ref,
    rgate_ref,
    igate_ref,
    scale_ref,
    low_ref,
    brow_ref,
    gperm_ref,
    enter_ref,
    ext,
    pre0,
    pre1,
    prod,
    mix,
    tail,
    carry,
    *,
    taps,
):
    rows, width = states_ref.shape
    steps = rows // SUB
    halo = taps - 1

    @pl.when(pl.program_id(1) == 0)
    def _():
        tail[...] = jnp.zeros_like(tail)
        carry[...] = jnp.zeros_like(carry)

    def load(s, _):
        v = strided_load(branch_refs, s, steps).astype(BF16).astype(F32)
        ext[rows8(s + halo), :] = v
        gperm_ref[rows8(s), :] = strided_load(gateb_refs, s, steps)
        return 0

    lax.fori_loop(0, steps, load, 0, unroll=4)
    for back in range(1, halo + 1):
        v = ext[rows8(halo + steps - back), :]
        ext[rows8(halo - back), :] = roll_down(v, tail[back - 1 : back, :])
        tail[back - 1 : back, :] = v[SUB - 1 : SUB]
    big = 8
    wide = SUB * big

    def block(i):
        return pl.ds(pl.multiple_of(i * wide, wide), wide)

    def conv(i, _):
        out = chan_ref[taps : taps + 1, :]
        for k in range(taps):
            v = ext[pl.ds(pl.multiple_of((i * big + halo - k) * SUB, SUB), wide), :]
            out = out + chan_ref[k : k + 1, :] * v
            if k == 0:
                brow_ref[block(i), :] = v.astype(BF16)
        low_ref[block(i), :] = out.astype(BF16)
        return 0

    lax.fori_loop(0, steps // big, conv, 0)
    low = low_ref[...]
    pre0[...] = jnp.dot(low, gw_ref[0, 0], preferred_element_type=F32)
    pre1[...] = jnp.dot(low, gw_ref[1, 0], preferred_element_type=F32)

    def gates(i, _):
        r = jax.nn.sigmoid(pre0[block(i), :] + chan_ref[taps + 1 : taps + 2, :])
        g = jax.nn.sigmoid(pre1[block(i), :] + chan_ref[taps + 2 : taps + 3, :])
        log_decay = r * chan_ref[taps + 3 : taps + 4, :]
        scale = jnp.sqrt(minus_expm1(2.0 * log_decay))
        rgate_ref[block(i), :] = r
        igate_ref[block(i), :] = g
        scale_ref[block(i), :] = scale
        decay_ref[block(i), :] = jnp.exp(log_decay)
        pre0[block(i), :] = scale * g * low_ref[block(i), :].astype(F32)
        return 0

    lax.fori_loop(0, steps // big, gates, 0)

    def scan(s, hp):
        h, p = hp
        a = decay_ref[rows8(s), :]
        h = a * h + pre0[rows8(s), :]
        p = a * p
        states_ref[rows8(s), :] = h
        prod[rows8(s), :] = p
        return h, p

    zero = jnp.zeros((SUB, width), F32)
    h, p = lax.fori_loop(0, steps, scan, (zero, zero + 1.0), unroll=8)
    for shift in (1, 2, 4):
        keep = sub_iota(width) >= shift
        h = h + p * jnp.where(keep, pltpu.roll(h, shift, 0), 0.0)
        p = p * jnp.where(keep, pltpu.roll(p, shift, 0), 1.0)
    first = carry[0:1, :]
    ends = h + p * first
    enter = roll_down(ends, first)
    enter_ref[...] = enter
    carry[0:1, :] = ends[SUB - 1 : SUB]

    def finish(s, _):
        state = states_ref[rows8(s), :] + prod[rows8(s), :] * enter
        states_ref[rows8(s), :] = state
        value, _ = gelu_parts(gperm_ref[rows8(s), :])
        strided_store(mix, s, steps, value * state)
        return 0

    lax.fori_loop(0, steps, finish, 0, unroll=8)
    for n in range(width // LANES):
        mixed_ref[:, n * LANES : (n + 1) * LANES] = mix[n].astype(BF16)


def recur_forward(projected, chan, gate_w, taps, chunk):
    total, width = projected.shape[0], projected.shape[1] // 2
    head = gate_w.shape[2]
    heads = width // head
    chunks = total // chunk
    rows = lambda j, c: (c, j)
    blk = pl.BlockSpec((chunk, head), rows)
    f32s = jax.ShapeDtypeStruct((total, width), F32)
    b16s = jax.ShapeDtypeStruct((total, width), BF16)
    work = pltpu.VMEM((chunk, head), F32)
    groups = head // LANES
    lane = [
        pl.BlockSpec((chunk, LANES), lambda j, c, n=n: (c, j * groups + n))
        for n in (*range(groups), *range(width // LANES, width // LANES + groups))
    ]
    return pl.pallas_call(
        functools.partial(forward_kernel, taps=taps, groups=groups),
        grid=(heads, chunks),
        in_specs=[
            *lane,
            pl.BlockSpec((chan.shape[0], head), lambda j, c: (0, j)),
            pl.BlockSpec((2, 1, head, head), lambda j, c: (0, j, 0, 0)),
        ],
        out_specs=[blk] * 9 + [pl.BlockSpec((SUB, head), rows)],
        out_shape=[b16s, f32s, f32s, f32s, f32s, f32s, b16s, b16s, f32s]
        + [jax.ShapeDtypeStruct((chunks * SUB, width), F32)],
        scratch_shapes=[
            pltpu.VMEM((chunk + (taps - 1) * SUB, head), F32),
            work,
            work,
            work,
            pltpu.VMEM((groups, chunk, LANES), F32),
            pltpu.VMEM((SUB, head), F32),
            pltpu.VMEM((SUB, head), F32),
        ],
        compiler_params=pltpu.CompilerParams(
            dimension_semantics=("arbitrary", "arbitrary"), vmem_limit_bytes=60 << 20
        ),
        name="recur_forward",
    )(*[projected] * 2 * groups, chan, gate_w)


def backward_kernel(*refs, taps, groups):
    backward_body(refs[:groups], *refs[groups:], taps=taps)


def backward_body(
    mgrad_refs,
    states_ref,
    decay_ref,
    rgate_ref,
    igate_ref,
    scale_ref,
    low_ref,
    brow_ref,
    gperm_ref,
    enter_ref,
    chan_ref,
    gw_ref,
    pgrad_ref,
    gwg_ref,
    sums_ref,
    car,
    prod,
    cgrad,
    lowf,
    gout,
    pre,
    sums,
    tail,
    carry,
    *,
    taps,
):
    rows, width = states_ref.shape
    steps = rows // SUB
    halo = taps - 1
    big = 8
    wide = SUB * big

    @pl.when(pl.program_id(1) == 0)
    def _():
        tail[...] = jnp.zeros_like(tail)
        carry[...] = jnp.zeros_like(carry)
        sums[...] = jnp.zeros_like(sums)
        gwg_ref[...] = jnp.zeros_like(gwg_ref)

    def block(i):
        return pl.ds(pl.multiple_of(i * wide, wide), wide)

    def scan(n, uq):
        u, q = uq
        s = steps - 1 - n
        value, slope = gelu_parts(gperm_ref[rows8(s), :])
        mg = strided_load(mgrad_refs, s, steps)
        strided_store(gout, s, steps, mg * states_ref[rows8(s), :] * slope)
        c = mg * value + u
        car[rows8(s), :] = c
        prod[rows8(s), :] = q
        a = decay_ref[rows8(s), :]
        return a * c, a * q

    zero = jnp.zeros((SUB, width), F32)
    u, q = lax.fori_loop(0, steps, scan, (zero, zero + 1.0), unroll=8)
    for shift in (1, 2, 4):
        keep = sub_iota(width) < SUB - shift
        u = u + q * jnp.where(keep, pltpu.roll(u, SUB - shift, 0), 0.0)
        q = q * jnp.where(keep, pltpu.roll(q, SUB - shift, 0), 1.0)
    last = carry[0:1, :]
    ends = u + q * last
    enter = roll_up(ends, last)
    carry[0:1, :] = ends[0:1]
    for n in range(width // LANES):
        pgrad_ref[1, :, n * LANES : (n + 1) * LANES] = gout[n].astype(BF16)
    neg = chan_ref[taps + 3 : taps + 4, :]
    state_in = enter_ref[...]

    def gates(s, acc):
        sum_r, sum_i, sum_d = acc
        c = car[rows8(s), :] + prod[rows8(s), :] * enter
        before = jnp.where(
            s == 0, state_in, states_ref[rows8(jnp.maximum(s - 1, 0)), :]
        )
        a = decay_ref[rows8(s), :]
        r = rgate_ref[rows8(s), :]
        g = igate_ref[rows8(s), :]
        scale = scale_ref[rows8(s), :]
        low = lowf[rows8(s), :]
        c_low = c * low
        dgrad = c * a * before - c_low * g * (a * a) / scale
        pr = dgrad * neg * r * (1.0 - r)
        pi = c_low * scale * g * (1.0 - g)
        pre[0, rows8(s), :] = pr
        pre[1, rows8(s), :] = pi
        cgrad[rows8(s), :] = c * scale * g
        pr = pr.astype(BF16).astype(F32)
        pi = pi.astype(BF16).astype(F32)
        return sum_r + pr, sum_i + pi, sum_d + dgrad * r

    lowf[...] = low_ref[...].astype(F32)
    sum_r, sum_i, sum_d = lax.fori_loop(0, steps, gates, (zero, zero, zero), unroll=4)
    low = low_ref[...]
    pr = pre[0].astype(BF16)
    pi = pre[1].astype(BF16)
    back = (((1,), (1,)), ((), ()))
    over = (((0,), (0,)), ((), ()))
    gwg_ref[0, 0] += lax.dot_general(low, pr, over, preferred_element_type=F32)
    gwg_ref[1, 0] += lax.dot_general(low, pi, over, preferred_element_type=F32)
    cgrad[pl.ds(0, rows), :] = (
        cgrad[pl.ds(0, rows), :]
        + lax.dot_general(pr, gw_ref[0, 0], back, preferred_element_type=F32)
        + lax.dot_general(pi, gw_ref[1, 0], back, preferred_element_type=F32)
    )
    for ahead in range(halo):
        v = cgrad[rows8(ahead), :]
        cgrad[rows8(steps + ahead), :] = roll_up(v, tail[ahead : ahead + 1, :])
        tail[ahead : ahead + 1, :] = v[0:1]
    car[...] = brow_ref[...].astype(F32)

    def conv(s, acc):
        branch = car[rows8(s), :]
        out = zero
        new = []
        for k in range(taps):
            v = cgrad[rows8(s + k), :]
            out = out + chan_ref[k : k + 1, :] * v
            new.append(acc[k] + v * branch)
            if k == 0:
                new_bias = acc[taps] + v
        strided_store(gout, s, steps, out)
        return (*new, new_bias)

    acc = lax.fori_loop(0, steps, conv, (zero,) * (taps + 1), unroll=4)
    for n in range(width // LANES):
        pgrad_ref[0, :, n * LANES : (n + 1) * LANES] = gout[n].astype(BF16)
    for n, v in enumerate((*acc, sum_r, sum_i, sum_d)):
        sums[n] += v
        sums_ref[n : n + 1, :] = jnp.sum(sums[n], axis=0, keepdims=True)


def recur_backward(mixed_grad, saved, chan, gate_w, taps, chunk):
    total, width = mixed_grad.shape
    head = gate_w.shape[2]
    heads = width // head
    chunks = total // chunk
    rows = lambda j, c: (chunks - 1 - c, j)
    blk = pl.BlockSpec((chunk, head), rows)
    work = pltpu.VMEM((chunk, head), F32)
    gws = pl.BlockSpec((2, 1, head, head), lambda j, c: (0, j, 0, 0))
    groups = head // LANES
    lane = [
        pl.BlockSpec((chunk, LANES), lambda j, c, n=n: (chunks - 1 - c, j * groups + n))
        for n in range(groups)
    ]
    n_sums = -(-(taps + 4) // SUB) * SUB
    return pl.pallas_call(
        functools.partial(backward_kernel, taps=taps, groups=groups),
        grid=(heads, chunks),
        in_specs=lane
        + [blk] * 8
        + [
            pl.BlockSpec((SUB, head), rows),
            pl.BlockSpec((chan.shape[0], head), lambda j, c: (0, j)),
            gws,
        ],
        out_specs=[
            pl.BlockSpec((2, chunk, head), lambda j, c: (0, chunks - 1 - c, j)),
            gws,
            pl.BlockSpec((n_sums, head), lambda j, c: (0, j)),
        ],
        out_shape=[
            jax.ShapeDtypeStruct((2, total, width), BF16),
            jax.ShapeDtypeStruct((2, heads, head, head), F32),
            jax.ShapeDtypeStruct((n_sums, width), F32),
        ],
        scratch_shapes=[
            work,
            work,
            pltpu.VMEM((chunk + (taps - 1) * SUB, head), F32),
            work,
            pltpu.VMEM((groups, chunk, LANES), F32),
            pltpu.VMEM((2, chunk, head), F32),
            pltpu.VMEM((taps + 4, SUB, head), F32),
            pltpu.VMEM((SUB, head), F32),
            pltpu.VMEM((SUB, head), F32),
        ],
        compiler_params=pltpu.CompilerParams(
            dimension_semantics=("arbitrary", "arbitrary"), vmem_limit_bytes=60 << 20
        ),
        name="recur_backward",
    )(*[mixed_grad] * groups, *saved, chan, gate_w)


def bit_list(n):
    return [1 << i for i in range(n.bit_length() - 1)]


def swap(block, axis, bit):
    return lax.ppermute(block, axis, [(i, i ^ bit) for i in range(lax.axis_size(axis))])


def gather_near(block):
    n = lax.axis_size("wide")
    core, *links = bit_list(n)
    half = block.shape[1] // 2
    sides = []
    for part, order in ((block[:, :half], links), (block[:, half:], links[::-1])):
        held = part
        for m, bit in enumerate(order):
            held = jnp.stack([held, swap(held, "wide", bit)], axis=m)
        place = sorted(range(len(order)), key=lambda i: -order[i])
        sides.append(held.transpose(*place, len(order), len(order) + 1))
    both = jnp.concatenate(sides, axis=-1)
    both = jnp.stack([both, swap(both, "wide", core)], axis=-3)
    return both.reshape(n * block.shape[0], block.shape[1])


def scatter_near(parts):
    n = lax.axis_size("wide")
    core, *links = bit_list(n)
    rows, width = parts.shape[0] // n, parts.shape[1]
    held = parts.reshape((2,) * len(links) + (2, rows, width))
    held = held[..., 0, :, :].astype(F32) + swap(
        held[..., 1, :, :].astype(BF16), "wide", core
    ).astype(F32)
    half = width // 2
    sides = []
    for part, order in ((held[..., :half], links), (held[..., half:], links[::-1])):
        axes = links[::-1]
        for bit in order:
            axis = axes.index(bit)
            keep = lax.index_in_dim(part, 0, axis, keepdims=False)
            send = lax.index_in_dim(part, 1, axis, keepdims=False).astype(BF16)
            part = keep + swap(send, "wide", bit).astype(F32)
            axes = axes[:axis] + axes[axis + 1 :]
        sides.append(part)
    return jnp.concatenate(sides, axis=-1)


def reorder(rows):
    n = lax.axis_size("wide")
    here = lax.axis_index("wide")
    size = rows.shape[0] // n
    return jnp.concatenate(
        [lax.dynamic_slice_in_dim(rows, (here ^ r) * size, size) for r in range(n)]
    )


def norm_rows(rows):
    inv = lax.rsqrt(jnp.mean(rows * rows, axis=-1, keepdims=True) + 1e-06)
    return inv, rows * inv


def norm_back(grad, gain, inv, unit):
    scaled = grad * gain
    return inv * (scaled - unit * jnp.mean(scaled * unit, axis=-1, keepdims=True))


def dot(left, right):
    return jnp.dot(left, right, preferred_element_type=F32)


def dot_over(left, right):
    return lax.dot_general(
        left, right, (((0,), (0,)), ((), ())), preferred_element_type=F32
    )


def dot_back(left, right):
    return lax.dot_general(
        left, right, (((1,), (1,)), ((), ())), preferred_element_type=F32
    )


def feed_forward(normed, cot, weight_in, weight_out):
    hidden_width = weight_out.shape[0]
    gate_up = dot(normed, weight_in)
    gate, up = gate_up[:, :hidden_width], gate_up[:, hidden_width:]
    value, slope = gelu_parts(gate)
    hidden_grad = dot_back(cot, weight_out)
    hidden = (value * up).astype(BF16)
    gate_up_grad = jnp.concatenate(
        [
            (hidden_grad * up * slope).astype(BF16),
            (hidden_grad * value).astype(BF16),
        ],
        axis=1,
    )
    return hidden, gate_up_grad


def shards(
    tokens,
    cotangent,
    norm_gains,
    in_weight,
    conv_weight,
    conv_bias,
    gate_weights,
    gate_biases,
    decay_param,
    out_weight,
    mlp_in_weight,
    mlp_out_weight,
):
    n_wide, n_seq = lax.axis_size("wide"), lax.axis_size("seq")
    here = lax.axis_index("wide")
    tok_low, cot_low = tokens[0], cotangent[0]
    size, width = tok_low.shape
    own = out_weight.shape[0]
    lru = own * n_wide
    heads, head = gate_weights.shape[1:3]
    taps = conv_weight.shape[0]
    gain_own = norm_gains.shape[1]

    span = max(
        ((w + 1) * own - 1) // head - w * own // head + 1 for w in range(n_wide)
    )
    firsts = [min(w * own // head, heads - span) for w in range(n_wide)]
    win = span * head
    start = jnp.minimum(here * own // head, heads - span) * head
    offset = here * own - start

    small = lax.all_gather(
        jnp.concatenate(
            [
                norm_gains.reshape(-1),
                conv_weight.reshape(-1),
                conv_bias,
                gate_biases.reshape(-1),
                decay_param,
            ]
        ),
        "wide",
    )
    gains = (
        small[:, : 2 * gain_own]
        .reshape(n_wide, 2, gain_own)
        .transpose(1, 0, 2)
        .reshape(2, width)
        .astype(F32)
    )
    channels = (
        small[:, 2 * gain_own :]
        .reshape(n_wide, taps + 4, own)
        .transpose(1, 0, 2)
        .reshape(taps + 4, lru)
    )
    channels = lax.dynamic_slice_in_dim(channels, start, win, axis=1).astype(F32)
    chan = jnp.concatenate(
        [channels[: taps + 3], -8.0 * jax.nn.softplus(-channels[taps + 3 :])]
    )

    tok_all = lax.all_gather(tok_low, "wide", axis=0, tiled=True)
    in_win = lax.all_to_all(
        jnp.stack(
            [
                jnp.concatenate(
                    [
                        in_weight[:, h, f * head : f * head + win]
                        for h in range(2)
                    ],
                    axis=1,
                )
                for f in firsts
            ]
        ),
        "wide",
        split_axis=0,
        concat_axis=0,
        tiled=True,
    ).reshape(width, 2 * win)
    gate_w = lax.all_to_all(
        jnp.stack([gate_weights[:, f : f + span] for f in firsts]),
        "wide",
        split_axis=0,
        concat_axis=0,
        tiled=True,
    )
    gate_w = jnp.moveaxis(gate_w, 0, 3).reshape(2, span, head, head)

    below = max(w * own - f * head for w, f in enumerate(firsts))
    above = max(f * head + win - (w + 1) * own for w, f in enumerate(firsts))
    if max(below, above) <= own:
        lower = lax.ppermute(
            out_weight[own - below :], "wide", [(i, i + 1) for i in range(n_wide - 1)]
        )
        upper = lax.ppermute(
            out_weight[:above], "wide", [(i + 1, i) for i in range(n_wide - 1)]
        )
        out_win = lax.dynamic_slice_in_dim(
            jnp.concatenate([lower, out_weight, upper]), below - offset, win
        )
    else:
        out_win = lax.dynamic_slice_in_dim(
            lax.all_gather(out_weight, "wide", axis=0, tiled=True), start, win
        )
    out_own = lax.dynamic_update_slice_in_dim(
        jnp.zeros((win, width), BF16), out_weight, offset, 0
    )
    in_own = jnp.concatenate(
        [
            lax.dynamic_slice_in_dim(in_win, h * win + offset, own, axis=1)
            for h in range(2)
        ],
        axis=1,
    )

    cot_near = gather_near(cot_low)
    total = size * n_wide
    recompute = n_seq * total <= 8192 and n_seq & (n_seq - 1) == 0 and n_seq > 1

    def others(rows):
        sent = jnp.concatenate([swap(rows, "seq", d) for d in range(1, n_seq)])
        return lax.all_gather(sent, "wide", axis=0, tiled=True)

    inv_all, unit_all = norm_rows(tok_all.astype(F32))
    normed_all = (unit_all * gains[0]).astype(BF16)
    projected = dot(normed_all, in_win)
    chunk = min(total, 512)
    mixed, *saved = recur_forward(projected, chan, gate_w, taps, chunk)
    mixed_near = reorder(mixed)
    rows = tok_low.astype(F32)
    middle = rows + scatter_near(dot(mixed_near, out_own).astype(BF16))
    inv_two, unit_two = norm_rows(middle)
    normed_two = (unit_two * gains[1]).astype(BF16)

    mlp_in = mlp_in_weight.reshape(width, -1)
    normed_near = gather_near(normed_two)
    hidden, gate_up_grad = feed_forward(normed_near, cot_near, mlp_in, mlp_out_weight)
    mlp_out_grad = dot_over(hidden, cot_near)
    mlp_in_grad = dot_over(normed_near, gate_up_grad)
    normed_two_grad = scatter_near(dot_back(gate_up_grad, mlp_in).astype(BF16))
    feed = scatter_near(dot(hidden, mlp_out_weight).astype(BF16))
    result = (middle + feed).astype(BF16)
    middle_grad = cot_low.astype(F32) + norm_back(
        normed_two_grad, gains[1], inv_two, unit_two
    )
    gain_two_grad = jnp.sum(normed_two_grad * unit_two, axis=0)

    mix_near = gather_near(middle_grad.astype(BF16))
    mixed_grad = reorder(dot_back(mix_near, out_win))
    projected_grad, gate_grad, sums = recur_backward(
        mixed_grad, saved, chan, gate_w, taps, chunk
    )
    out_grad = lax.dynamic_slice_in_dim(
        dot_over(mixed_near, mix_near).astype(BF16), offset, own
    )
    own_grad = jnp.concatenate(
        [
            lax.dynamic_slice_in_dim(projected_grad[h], offset, own, axis=1)
            for h in range(2)
        ],
        axis=1,
    )
    normed_grad_part = dot_back(reorder(own_grad), in_own).astype(BF16)
    in_grad = lax.all_to_all(
        dot_over(normed_all, own_grad).astype(BF16).reshape(n_wide, -1, 2 * own),
        "wide",
        split_axis=0,
        concat_axis=0,
        tiled=True,
    )
    in_grad = jnp.concatenate(
        [
            jnp.moveaxis(in_grad[:, :, h * own : (h + 1) * own], 0, 1).reshape(-1, 1, lru)
            for h in range(2)
        ],
        axis=1,
    )
    part = head // n_wide
    gate_grad = lax.all_to_all(
        jnp.moveaxis(
            gate_grad.astype(BF16).reshape(2, span, head, n_wide, part), 3, 0
        ),
        "wide",
        split_axis=0,
        concat_axis=0,
        tiled=True,
    )
    holders = [
        next(w for w, f in enumerate(firsts) if f <= j < f + span) for j in range(heads)
    ]
    gate_grad = jnp.stack(
        [gate_grad[w, :, j - firsts[w]] for j, w in enumerate(holders)], axis=1
    )
    normed_grad = scatter_near(normed_grad_part)
    inv_one, unit_one = norm_rows(rows)
    input_grad = middle_grad + norm_back(normed_grad, gains[0], inv_one, unit_one)
    gain_one_grad = jnp.sum(normed_grad * unit_one, axis=0)

    gains_grad = lax.psum(jnp.stack([gain_one_grad, gain_two_grad]), ("seq", "wide"))
    gains_grad = lax.dynamic_slice_in_dim(gains_grad, here * gain_own, gain_own, axis=1)
    sums = lax.psum(
        lax.dynamic_slice_in_dim(sums[: taps + 4], offset, own, axis=1), "seq"
    )
    decay_grad = sums[taps + 3] * 8.0 * jax.nn.sigmoid(-decay_param.astype(F32))
    in_grad, out_grad, gate_grad = (
        lax.psum(g, "seq").astype(F32) for g in (in_grad, out_grad, gate_grad)
    )
    if recompute:
        normed_far, cot_far = others(normed_two), others(cot_low)
        hidden_far, gate_up_far = feed_forward(
            normed_far, cot_far, mlp_in, mlp_out_weight
        )
        mlp_out_grad = mlp_out_grad + dot_over(hidden_far, cot_far)
        mlp_in_grad = mlp_in_grad + dot_over(normed_far, gate_up_far)
    else:
        mlp_out_grad, mlp_in_grad = (
            lax.psum(g.astype(BF16), "seq").astype(F32)
            for g in (mlp_out_grad, mlp_in_grad)
        )
    return (
        result[None],
        input_grad[None],
        gains_grad,
        in_grad,
        sums[:taps],
        sums[taps],
        gate_grad,
        sums[taps + 1 : taps + 3],
        decay_grad,
        out_grad,
        mlp_in_grad.reshape(mlp_in_weight.shape),
        mlp_out_grad,
    )


def solution(mesh):
    placed = (
        P("seq", "wide", None),
        P("seq", "wide", None),
        P(None, "wide"),
        P("wide", None, None),
        P(None, "wide"),
        P("wide"),
        P(None, None, None, "wide"),
        P(None, "wide"),
        P("wide"),
        P("wide", None),
        P(None, None, "wide"),
        P("wide", None),
    )
    return jax.shard_map(
        shards,
        mesh=mesh,
        in_specs=placed,
        out_specs=(
            P("seq", "wide", None),
            P("seq", "wide", None),
            P(None, "wide"),
            P("wide", None, None),
            P(None, "wide"),
            P("wide"),
            P(None, None, None, "wide"),
            P(None, "wide"),
            P("wide"),
            P("wide", None),
            P(None, None, "wide"),
            P("wide", None),
        ),
        check_vma=False,
    )
```

time: 3160 us -> 939 us (0.30)
  waiting for transfers between devices: 1530 us -> 286 us
  local copies, waits for them, and re-layouts: 1170 us -> 126 us
  other arithmetic: 166 us -> 56.5 us
  starting transfers between devices: 31 us -> 113 us
  matrix products: 137 us -> 181 us
  Pallas kernels: 0 us -> 31.6 us
    psum x1, waiting for transfers between devices: 893 us -> 0.01 us  [shards(): lax.psum(g, 'seq').astype(F32)]
    slice x124 -> x9, local copies, waits for them, and re-layouts: 724 us -> 20.3 us  [the longest x1 12.1 us: shards(): in_weight[:, h, f * head:f * head + win]]
    reduce_scatter x5 -> x0, waiting for transfers between devices: 389 us -> none  [the longest x1 171 us: shards(): lax.psum_scatter(in_full, 'wide', scatter_dimension=0, tiled=True)]
    pad x36 -> x0, local copies, waits for them, and re-layouts: 247 us -> none  [the longest x18 123 us: shards(): lax.associative_scan(affine_combine, (factor_chan, inflow_chan), axis=0)[1]]
    ppermute x2 -> x43, waiting for transfers between devices: 0.01 us -> 225 us  [the longest x41 225 us: swap(): lax.ppermute(block, axis, [(i, i ^ bit) for i in range(lax.axis_size(axis...]
    unnamed x17 -> x4, waiting for transfers between devices: 93.8 us -> 0.73 us
    all_gather x5 -> x3, waiting for transfers between devices: 113 us -> 33.9 us  [the longest x2 33.9 us: others(): return lax.all_gather(sent, 'wide', axis=0, tiled=True)]
    ppermute x2 -> x43, starting transfers between devices: 3.45 us -> 82.9 us  [the longest x41 77.7 us: swap(): lax.ppermute(block, axis, [(i, i ^ bit) for i in range(lax.axis_size(axis...]
  transfers between devices with their start and end apart: 22 -> 51, of which waited for: 15 -> 32; matrix products, arithmetic and copies ran while one was open for 27% -> 17% of each run, Pallas kernels for 0% -> 0%
where the time goes in v1:
time: 939 us; the launch traced here: 929 us
  waiting for transfers between devices  286 us (30%)
  matrix products  181 us (19%)
  local copies, waits for them, and re-layouts  126 us (13%)
  blocking collectives  119 us (13%)
  starting transfers between devices  113 us (12%)
  other arithmetic  56.5 us (6%)
  Pallas kernels  31.6 us (3%)
  between operations  15.5 us (2%)
    ppermute x41, waiting for transfers between devices, swap(): lax.ppermute(block, axis, [(i, i ^ bit) for i in range(lax.axis_size(axis...  225 us
    dot_general x6, matrix products, dot_over(): lax.dot_general(left, right, (((0,), (0,)), ((), ())), preferred_element_...  79.5 us
    ppermute x41, starting transfers between devices, swap(): lax.ppermute(block, axis, [(i, i ^ bit) for i in range(lax.axis_size(axis...  77.7 us
    unnamed x131, local copies, waits for them, and re-layouts  68.7 us
    dot_general x5, matrix products, dot(): return jnp.dot(left, right, preferred_element_type=F32)  54.5 us
    all_gather x1, blocking collectives, shards(): lax.all_gather(jnp.concatenate([norm_gains.reshape(-1), conv_weight.resha...  52 us
    dot_general x5, matrix products, dot_back(): lax.dot_general(left, right, (((1,), (1,)), ((), ())), preferred_element_...  47.3 us
    psum x1, blocking collectives, shards(): lax.psum(jnp.stack([gain_one_grad, gain_two_grad]), ('seq', 'wide'))  39.9 us
  transfers between devices with their start and end apart: 51, of which 32 were waited for; matrix products, arithmetic and copies ran while one was open for 17% of the time, Pallas kernels for 0%

profile of v1, /device:TPU:0, one launch (start us, length us, event | category | flops | bytes accessed | tf_op | source)
XLA Modules:
  0.0 928.8 jit_solution(9941925659573362290)
XLA Ops:
  25.1 12.1 %fusion.109 = (bf16[256,1,512]{2,1,0:T(2,128)(2,1)S(1)}, bf16[256,1,512]{2,1,0:T(2,128)(2,1)S(1)}, bf16[256,1,512]{2,1,0:T(2,128)(2,1)S(1)}, bf16[256,1,512]{2,1...) fusion(bf16[256,2,2560]{2,1,0:T(2,128)(2,1)} %param.15), kind=kLoop, calls=%fused_computation.322 | loop fusion | bytes 8388608 | tf_op jit(solution)/shard_map/slice | solution.py:577
  50.3 52.0 %all-gather.1 = bf16[24576]{0:T(1024)(128)(2,1)S(1)} all-gather(bf16[3072]{0:T(1024)(128)(2,1)S(1)} %concatenate.123), channel_id=3, replica_groups=mesh['seq'=4,'wide'=8] {'wide'}, dimensions={0}, use_global_device_ids=true | all-gather | bytes 55296 | tf_op jit(solution)/shard_map/all_gather | solution.py:541
  114.5 10.0 %fusion.21.refs_0_.refs_1_.refs_2_.refs_3_ = f32[1024,1024]{1,0:T(8,128)} fusion(bf16[2048,1024]{1,0:T(8,128)(2,1)} %bitcast.28, bf16[1,1024,2048]{2,1,0:T(8,128)(2,1)} %all-gather.10.cloned.1.call-done, f32[2048]{0:T(1024)S(1)} %bitcast.506, f32[1024]{0:T(1024)S(1)} %add_rsqrt_fusion), kind=kOutput, calls=%fused_computation.87 | convolution fusion | flops 4303355904 | bytes 12595200 | tf_op jit(solution)/shard_map/dot_general | solution.py:477
  124.5 15.9 %recur_forward.1 = (bf16[1024,512]{1,0:T(8,128)(2,1)}, f32[1024,512]{1,0:T(8,128)}, f32[1024,512]{1,0:T(8,128)}, f32[1024,512]{1,0:T(8,128)}, f32[1024,512]{1,0:...) custom-call(f32[1024,1024]{1,0:T(8,128)} %fusion.21.refs_0_.refs_1_., ...), custom_call_target="tpu_custom_call" | custom-call | tf_op jit(solution)/shard_map/recur_forward/pallas_call | solution.py:193
  161.8 10.5 %collective-permute-done.1 = bf16[2,128,1024]{2,1,0:T(8,128)(2,1)S(1)} collective-permute-done((bf16[2,128,1024]{2,1,0:T(8,128)(2,1)S(1)}, bf16[2,128,1024]{2,1,0:T(8,128)(2,1)S(1)}, u32[]{:S(2)}, u32[]{:S(2)}) %collective-permute-start.1) | collective-permute-done | bytes 524320 | tf_op jit(solution)/shard_map/ppermute | solution.py:416
  203.8 7.5 collective-permute-done.6
  226.6 8.5 fusion.113
  235.1 8.4 multiply_convert_fusion.5
  243.5 6.9 convolution_convert_fusion
  258.1 12.1 %collective-permute-done.21 = bf16[2,128,1024]{2,1,0:T(8,128)(2,1)S(1)} collective-permute-done((bf16[2,128,1024]{2,1,0:T(8,128)(2,1)S(1)}, bf16[2,128,1024]{2,1,0:T(8,128)(2,1)S(1)}, u32[]{:S(2)}, u32[]{:S(2)}) %collective-permute-start.21) | collective-permute-done | bytes 524320 | tf_op jit(solution)/shard_map/ppermute | solution.py:416
  290.6 9.3 %collective-permute-done.26 = bf16[2,128,1024]{2,1,0:T(8,128)(2,1)S(1)} collective-permute-done((bf16[2,128,1024]{2,1,0:T(8,128)(2,1)S(1)}, bf16[2,128,1024]{2,1,0:T(8,128)(2,1)S(1)}, u32[]{:S(2)}, u32[]{:S(2)}) %collective-permute-start.26) | collective-permute-done | bytes 524320 | tf_op jit(solution)/shard_map/ppermute | solution.py:416
  323.2 15.7 %recur_backward.1 = (bf16[2,1024,512]{2,1,0:T(8,128)(2,1)}, f32[2,2,256,256]{3,2,1,0:T(8,128)}, f32[8,512]{1,0:T(8,128)}) custom-call(f32[1024,512]{1,0:T(8,128)} %dynamic-slice_dynamic-update-slice_fusion.refs_0_.refs_1_, f32[1024,512]{1,0:T(8,128)} %dynamic-slice_dynamic-update-slice_fusion.refs_0_.refs_1_, f32[1024,512]{1,0:T(8,128)} %get-tuple-element.26.refs_2_, ...), custom_call_target="tpu_custom_call" | custom-call | tf_op jit(solution)/shard_map/recur_backward/pallas_call | solution.py:373
  357.7 15.8 %all-to-all-start.3 = ((bf16[8,2,2,256,32]{3,4,2,1,0:T(8,128)(2,1)}), bf16[8,2,2,256,32]{3,4,2,1,0:T(8,128)(2,1)}, u32[]{:S(2)}, u32[]{:S(2)}) async-start(bf16[8,2,2,256,32]{3,4,2,1,0:T(8,128)(2,1)} %copy.165), calls=%async_computation.3 | async-start | bytes 1048576 | tf_op jit(solution)/shard_map/all_to_all | solution.py:689
  398.1 22.0 %all-to-all-done.2 = bf16[8,256,640]{1,2,0:T(8,128)(2,1)} async-done(((bf16[8,256,640]{1,2,0:T(8,128)(2,1)}), bf16[8,256,640]{1,2,0:T(8,128)(2,1)}, u32[]{:S(2)}, u32[]{:S(2)}) %all-to-all-start.2) | async-done | bytes 2621472 | tf_op jit(solution)/shard_map/all_to_all | solution.py:674
  428.6 50.1 %collective-permute-done.38 = bf16[128,2048]{1,0:T(8,128)(2,1)S(1)} collective-permute-done((bf16[128,2048]{1,0:T(8,128)(2,1)}, bf16[128,2048]{1,0:T(8,128)(2,1)S(1)}, u32[]{:S(2)}, u32[]{:S(2)}) %collective-permute-start.38) | collective-permute-done | bytes 524320 | tf_op jit(solution)/shard_map/ppermute | solution.py:416
  478.7 12.4 %collective-permute-done.39 = bf16[128,2048]{1,0:T(8,128)(2,1)S(1)} collective-permute-done((bf16[128,2048]{1,0:T(8,128)(2,1)}, bf16[128,2048]{1,0:T(8,128)(2,1)S(1)}, u32[]{:S(2)}, u32[]{:S(2)}) %collective-permute-start.39) | collective-permute-done | bytes 524320 | tf_op jit(solution)/shard_map/ppermute | solution.py:416
  492.5 33.6 %collective-permute-start.40 = (bf16[128,2048]{1,0:T(8,128)(2,1)}, bf16[128,2048]{1,0:T(8,128)(2,1)S(1)}, u32[]{:S(2)}, u32[]{:S(2)}) collective-permute-start(bf16[128,2048]{1,0:T(8,128)(2,1)} %bitcast.468), channel_id=1, source_target_pairs={{0,8},{8,0},{16,24},{24,16},{1,9},{9,1},{17,25},{25,17},{2,10},{10... | collective-permute-start | bytes 1572872 | tf_op jit(solution)/shard_map/ppermute | solution.py:416
  529.4 31.7 %collective-permute-done.40 = bf16[128,2048]{1,0:T(8,128)(2,1)S(1)} collective-permute-done((bf16[128,2048]{1,0:T(8,128)(2,1)}, bf16[128,2048]{1,0:T(8,128)(2,1)S(1)}, u32[]{:S(2)}, u32[]{:S(2)}) %collective-permute-start.40) | collective-permute-done | bytes 524320 | tf_op jit(solution)/shard_map/ppermute | solution.py:416
  561.1 22.6 %collective-permute-done.41 = bf16[128,2048]{1,0:T(8,128)(2,1)S(1)} collective-permute-done((bf16[128,2048]{1,0:T(8,128)(2,1)}, bf16[128,2048]{1,0:T(8,128)(2,1)S(1)}, u32[]{:S(2)}, u32[]{:S(2)}) %collective-permute-start.41) | collective-permute-done | bytes 524320 | tf_op jit(solution)/shard_map/ppermute | solution.py:416
  608.1 8.2 collective-permute-start.11
  616.3 12.2 %collective-permute-done.11 = bf16[2,128,1024]{2,1,0:T(8,128)(2,1)S(1)} collective-permute-done((bf16[2,128,1024]{2,1,0:T(8,128)(2,1)S(1)}, bf16[2,128,1024]{2,1,0:T(8,128)(2,1)S(1)}, u32[]{:S(2)}, u32[]{:S(2)}) %collective-permute-start.11) | collective-permute-done | bytes 524320 | tf_op jit(solution)/shard_map/ppermute | solution.py:416
  650.8 26.8 %psum.37 = f32[8,320]{1,0:T(8,128)S(1)} all-reduce(f32[8,320]{1,0:T(8,128)S(1)} %constant_dynamic-slice_fusion), channel_id=1, replica_groups=mesh['seq'=4,'wide'=8] {'seq'}, use_global_device_ids=true, to_apply=%region_9.10 | all-reduce | flops 2560 | bytes 20480 | tf_op jit(solution)/shard_map/psum | solution.py:711
  692.9 39.9 %psum.35 = f32[2,2048]{1,0:T(2,128)S(1)} all-reduce(f32[2,2048]{1,0:T(2,128)S(1)} %pad_maximum_fusion.20), channel_id=1, replica_groups=mesh['seq'=4,'wide'=8] {'seq','wide'}, use_global_device_ids=true, to_apply=%region_7.8 | all-reduce | flops 4096 | bytes 32768 | tf_op jit(solution)/shard_map/psum | solution.py:709
  739.6 7.8 copy.175
  750.6 26.4 %fusion.115 = f32[3072,1536]{0,1:T(8,128)} fusion(bf16[3072,2048]{1,0:T(8,128)(2,1)} %all-gather.6.cloned.1.call-done, bf16[2048,1536]{1,0:T(8,128)(2,1)} %bitcast.461), kind=kOutput, calls=%fused_computation.328 | convolution fusion | flops 19327352832 | bytes 37748736 | tf_op jit(solution)/shard_map/dot_general | solution.py:477
  777.0 33.9 %all-gather.8.cloned.1.call-done = bf16[3072,2048]{1,0:T(8,128)(2,1)} async-done(((bf16[384,2048]{1,0:T(8,128)(2,1)}), bf16[3072,2048]{1,0:T(8,128)(2,1)}) %all-gather.8.cloned.1.call-update) | async-done | bytes 12582928 | tf_op jit(solution)/shard_map/all_gather | solution.py:632
  811.0 20.2 %fusion.7 = f32[768,2048]{1,0:T(8,128)} fusion(bf16[3072,2048]{1,0:T(8,128)(2,1)} %all-gather.8.cloned.1.call-done, f32[3072,1536]{0,1:T(8,128)} %fusion.115), kind=kOutput, calls=%fused_computation.15 | convolution fusion | flops 9687269376 | bytes 37748736 | tf_op jit(solution)/shard_map/dot_general | solution.py:481
  831.2 7.5 fusion.112
  838.7 23.8 %multiply_convert_fusion.2 = (bf16[3072,768]{0,1:T(8,128)(2,1)}, bf16[3072,768]{0,1:T(8,128)(2,1)}) fusion(f32[3072,1536]{0,1:T(8,128)} %fusion.115, bf16[3072,2048]{1,0:T(8,128)(2,1)} %all-gather.8.cloned.1.call-done, bf16[768,2048]{1,0:T(8,128)(2,1)S(1)} %copy-done), kind=kOutput, calls=%fused_computation.8 | convolution fusion | flops 9715580928 | bytes 44040192 | tf_op jit(solution)/shard_map/dot_general | solution.py:487
  862.5 26.8 %fusion = f32[2048,1536]{0,1:T(8,128)} fusion(bf16[3072,2048]{1,0:T(8,128)(2,1)} %all-gather.6.cloned.1.call-done, bf16[3072,768]{0,1:T(8,128)(2,1)} %get-tuple-element.85, bf16[3072,768]{0,1:T(8,128)(2,1)} %get-tuple-element.84), kind=kOutput, calls=%fused_computation.2 | convolution fusion | flops 19346227200 | bytes 34603008 | tf_op jit(solution)/shard_map/dot_general | solution.py:481
  889.4 13.2 %convolution_add_fusion = f32[2048,1536]{0,1:T(8,128)} fusion(f32[2048,1536]{0,1:T(8,128)} %fusion, bf16[1024,2048]{1,0:T(8,128)(2,1)S(1)} %bitcast.475, bf16[1024,768]{1,0:T(8,128)(2,1)S(1)} %copy-done.41, bf16[1024,768]{1,0:T(8,128)(2,1)S(1)} %copy-done.39), kind=kOutput, calls=%fused_computation.14 | convolution fusion | flops 6451888128 | bytes 32505856 | tf_op jit(solution)/shard_map/dot_general | solution.py:481
  902.6 19.2 %copy.177 = f32[2048,2,768]{2,1,0:T(2,128)} copy(f32[2048,2,768]{0,2,1:T(8,128)} %bitcast.455) | data formatting | bytes 25165824
  (364 shorter events, 290.0 us)
Async XLA Ops:
  7.2 104.2 %all-gather.10.cloned.1.call-start = ((), (), s32[]{:S(2)}) async-start(), calls=%async_computation.6 | async-start | bytes 4718592 | tf_op jit(solution)/shard_map/all_gather | solution.py:571
  19.9 25.3 %all-to-all-start.1 = ((bf16[8,2,2,256,32]{3,4,2,1,0:T(8,128)(2,1)}), bf16[8,2,2,256,32]{3,4,2,1,0:T(8,128)(2,1)}, u32[]{:S(2)}, u32[]{:S(2)}) async-start(bf16[8,2,2,256,32]{3,4,2,1,0:T(8,128)(2,1)} %constant_dynamic-update-slice_fusion), calls=%async_computation.1 | async-start | bytes 1048576 | tf_op jit(solution)/shard_map/all_to_all | solution.py:590
  45.2 69.2 %all-to-all-start = ((bf16[8,256,1024]{2,1,0:T(8,128)(2,1)}), bf16[8,256,1024]{2,1,0:T(8,128)(2,1)}, u32[]{:S(2)}, u32[]{:S(2)}) async-start(bf16[8,256,1024]{2,1,0:T(8,128)(2,1)} %fusion.59), calls=%async_computation | async-start | bytes 8388608 | tf_op jit(solution)/shard_map/all_to_all | solution.py:572
  157.5 14.8 %collective-permute-start.1 = (bf16[2,128,1024]{2,1,0:T(8,128)(2,1)S(1)}, bf16[2,128,1024]{2,1,0:T(8,128)(2,1)S(1)}, u32[]{:S(2)}, u32[]{:S(2)}) collective-permute-start(bf16[2,128,1024]{2,1,0:T(8,128)(2,1)S(1)} %slice_bitcast_fusion.29), channel_id=1, source_target_pairs={{0,2},{1,3},{2,0},{3,1},{4,6},{5,7},{6,4},{7,5},{8,10},{9,11},{10,... | collective-permute-start | bytes 1572872 | tf_op jit(solution)/shard_map/ppermute | solution.py:416
  158.1 14.8 %collective-permute-start.3 = (bf16[2,128,1024]{2,1,0:T(8,128)(2,1)S(1)}, bf16[2,128,1024]{2,1,0:T(8,128)(2,1)S(1)}, u32[]{:S(2)}, u32[]{:S(2)}) collective-permute-start(bf16[2,128,1024]{2,1,0:T(8,128)(2,1)S(1)} %slice_bitcast_fusion.27), channel_id=1, source_target_pairs={{0,4},{1,5},{2,6},{3,7},{4,0},{5,1},{6,2},{7,3},{8,12},{9,13},{10,... | collective-permute-start | bytes 1572872 | tf_op jit(solution)/shard_map/ppermute | solution.py:416
  159.7 27.3 %collective-permute-start.17 = (bf16[128,1024]{1,0:T(8,128)(2,1)S(1)}, bf16[128,1024]{1,0:T(8,128)(2,1)S(1)}, u32[]{:S(2)}, u32[]{:S(2)}) collective-permute-start(bf16[128,1024]{1,0:T(8,128)(2,1)S(1)} %get-tuple-element.143), channel_id=1, source_target_pairs={{0,4},{1,5},{2,6},{3,7},{4,0},{5,1},{6,2},{7,3},{8,12},{9,13},{10,... | collective-permute-start | bytes 786440 | tf_op jit(solution)/shard_map/ppermute | solution.py:416
  160.3 17.6 %collective-permute-start.15 = (bf16[128,1024]{1,0:T(8,128)(2,1)S(1)}, bf16[128,1024]{1,0:T(8,128)(2,1)S(1)}, u32[]{:S(2)}, u32[]{:S(2)}) collective-permute-start(bf16[128,1024]{1,0:T(8,128)(2,1)S(1)} %get-tuple-element.144), channel_id=1, source_target_pairs={{0,2},{1,3},{2,0},{3,1},{4,6},{5,7},{6,4},{7,5},{8,10},{9,11},{10,... | collective-permute-start | bytes 786440 | tf_op jit(solution)/shard_map/ppermute | solution.py:416
  178.0 24.6 %collective-permute-start.16 = (bf16[2,128,1024]{2,1,0:T(8,128)(2,1)S(1)}, bf16[2,128,1024]{2,1,0:T(8,128)(2,1)S(1)}, u32[]{:S(2)}, u32[]{:S(2)}) collective-permute-start(bf16[2,128,1024]{2,1,0:T(8,128)(2,1)S(1)} %get-tuple-element.140), channel_id=1, source_target_pairs={{0,4},{1,5},{2,6},{3,7},{4,0},{5,1},{6,2},{7,3},{8,12},{9,13},{10,... | collective-permute-start | bytes 1572872 | tf_op jit(solution)/shard_map/ppermute | solution.py:416
  186.3 14.7 %collective-permute-start.7 = (bf16[128,1024]{1,0:T(8,128)(2,1)S(1)}, bf16[128,1024]{1,0:T(8,128)(2,1)S(1)}, u32[]{:S(2)}, u32[]{:S(2)}) collective-permute-start(bf16[128,1024]{1,0:T(8,128)(2,1)S(1)} %get-tuple-element.151), channel_id=1, source_target_pairs={{0,4},{1,5},{2,6},{3,7},{4,0},{5,1},{6,2},{7,3},{8,12},{9,13},{10,... | collective-permute-start | bytes 786440 | tf_op jit(solution)/shard_map/ppermute | solution.py:416
  187.0 16.2 %collective-permute-start.18 = (bf16[2,128,1024]{2,1,0:T(8,128)(2,1)S(1)}, bf16[2,128,1024]{2,1,0:T(8,128)(2,1)S(1)}, u32[]{:S(2)}, u32[]{:S(2)}) collective-permute-start(bf16[2,128,1024]{2,1,0:T(8,128)(2,1)S(1)} %get-tuple-element.146), channel_id=1, source_target_pairs={{0,2},{1,3},{2,0},{3,1},{4,6},{5,7},{6,4},{7,5},{8,10},{9,11},{10,... | collective-permute-start | bytes 1572872 | tf_op jit(solution)/shard_map/ppermute | solution.py:416
  194.2 17.1 %collective-permute-start.6 = (bf16[2,128,1024]{2,1,0:T(8,128)(2,1)S(1)}, bf16[2,128,1024]{2,1,0:T(8,128)(2,1)S(1)}, u32[]{:S(2)}, u32[]{:S(2)}) collective-permute-start(bf16[2,128,1024]{2,1,0:T(8,128)(2,1)S(1)} %get-tuple-element.148), channel_id=1, source_target_pairs={{0,4},{1,5},{2,6},{3,7},{4,0},{5,1},{6,2},{7,3},{8,12},{9,13},{10,... | collective-permute-start | bytes 1572872 | tf_op jit(solution)/shard_map/ppermute | solution.py:416
  201.1 12.8 %collective-permute-start.8 = (bf16[2,128,1024]{2,1,0:T(8,128)(2,1)S(1)}, bf16[2,128,1024]{2,1,0:T(8,128)(2,1)S(1)}, u32[]{:S(2)}, u32[]{:S(2)}) collective-permute-start(bf16[2,128,1024]{2,1,0:T(8,128)(2,1)S(1)} %get-tuple-element.154), channel_id=1, source_target_pairs={{0,2},{1,3},{2,0},{3,1},{4,6},{5,7},{6,4},{7,5},{8,10},{9,11},{10,... | collective-permute-start | bytes 1572872 | tf_op jit(solution)/shard_map/ppermute | solution.py:416
  203.8 15.8 %collective-permute-start.19 = (bf16[2,2,128,2048]{3,2,0,1:T(8,128)(2,1)S(1)}, bf16[2,2,128,2048]{3,2,0,1:T(8,128)(2,1)}, u32[]{:S(2)}, u32[]{:S(2)}) collective-permute-start(bf16[2,2,128,2048]{3,2,0,1:T(8,128)(2,1)S(1)} %get-tuple-element.124), channel_id=1, source_target_pairs={{0,1},{1,0},{2,3},{3,2},{4,5},{5,4},{6,7},{7,6},{8,9},{9,8},{10,11... | collective-permute-start | bytes 6291464 | tf_op jit(solution)/shard_map/ppermute | solution.py:416
  256.0 14.3 %collective-permute-start.21 = (bf16[2,128,1024]{2,1,0:T(8,128)(2,1)S(1)}, bf16[2,128,1024]{2,1,0:T(8,128)(2,1)S(1)}, u32[]{:S(2)}, u32[]{:S(2)}) collective-permute-start(bf16[2,128,1024]{2,1,0:T(8,128)(2,1)S(1)} %slice_bitcast_fusion.21), channel_id=1, source_target_pairs={{0,2},{1,3},{2,0},{3,1},{4,6},{5,7},{6,4},{7,5},{8,10},{9,11},{10,... | collective-permute-start | bytes 1572872 | tf_op jit(solution)/shard_map/ppermute | solution.py:416
  257.4 13.9 %collective-permute-start.23 = (bf16[2,128,1024]{2,1,0:T(8,128)(2,1)S(1)}, bf16[2,128,1024]{2,1,0:T(8,128)(2,1)S(1)}, u32[]{:S(2)}, u32[]{:S(2)}) collective-permute-start(bf16[2,128,1024]{2,1,0:T(8,128)(2,1)S(1)} %slice_bitcast_fusion.19), channel_id=1, source_target_pairs={{0,4},{1,5},{2,6},{3,7},{4,0},{5,1},{6,2},{7,3},{8,12},{9,13},{10,... | collective-permute-start | bytes 1572872 | tf_op jit(solution)/shard_map/ppermute | solution.py:416
  357.7 25.7 %all-to-all-start.3 = ((bf16[8,2,2,256,32]{3,4,2,1,0:T(8,128)(2,1)}), bf16[8,2,2,256,32]{3,4,2,1,0:T(8,128)(2,1)}, u32[]{:S(2)}, u32[]{:S(2)}) async-start(bf16[8,2,2,256,32]{3,4,2,1,0:T(8,128)(2,1)} %copy.165), calls=%async_computation.3 | async-start | bytes 1048576 | tf_op jit(solution)/shard_map/all_to_all | solution.py:689
  383.3 36.7 %all-to-all-start.2 = ((bf16[8,256,640]{1,2,0:T(8,128)(2,1)}), bf16[8,256,640]{1,2,0:T(8,128)(2,1)}, u32[]{:S(2)}, u32[]{:S(2)}) async-start(bf16[8,256,640]{1,2,0:T(8,128)(2,1)} %copy.163), calls=%async_computation.2 | async-start | bytes 5242880 | tf_op jit(solution)/shard_map/all_to_all | solution.py:674
  387.8 350.0 %all-reduce.3.cloned.1.call-start = ((), (), s32[]{:S(2)}) async-start(), calls=%async_computation.7 | async-start | bytes 8519680 | tf_op jit(solution)/shard_map/psum | solution.py:716
  423.7 326.9 %all-gather.6.cloned.1.call-start = ((), (), s32[]{:S(2)}) async-start(), calls=%async_computation.4 | async-start | bytes 14155776 | tf_op jit(solution)/shard_map/all_gather | solution.py:632
  423.8 54.9 %collective-permute-start.38 = (bf16[128,2048]{1,0:T(8,128)(2,1)}, bf16[128,2048]{1,0:T(8,128)(2,1)S(1)}, u32[]{:S(2)}, u32[]{:S(2)}) collective-permute-start(bf16[128,2048]{1,0:T(8,128)(2,1)} %copy-done.27), channel_id=1, source_target_pairs={{0,16},{8,24},{16,0},{24,8},{1,17},{9,25},{17,1},{25,9},{2,18},{10... | collective-permute-start | bytes 1572872 | tf_op jit(solution)/shard_map/ppermute | solution.py:416
  427.1 51.6 %collective-permute-start.37 = (bf16[128,2048]{1,0:T(8,128)(2,1)}, bf16[128,2048]{1,0:T(8,128)(2,1)S(1)}, u32[]{:S(2)}, u32[]{:S(2)}) collective-permute-start(bf16[128,2048]{1,0:T(8,128)(2,1)} %copy-done.27), channel_id=1, source_target_pairs={{0,8},{8,0},{16,24},{24,16},{1,9},{9,1},{17,25},{25,17},{2,10},{10... | collective-permute-start | bytes 1572872 | tf_op jit(solution)/shard_map/ppermute | solution.py:416
  428.6 62.5 %collective-permute-start.39 = (bf16[128,2048]{1,0:T(8,128)(2,1)}, bf16[128,2048]{1,0:T(8,128)(2,1)S(1)}, u32[]{:S(2)}, u32[]{:S(2)}) collective-permute-start(bf16[128,2048]{1,0:T(8,128)(2,1)} %copy-done.27), channel_id=1, source_target_pairs={{0,24},{8,16},{16,8},{24,0},{1,25},{9,17},{17,9},{25,1},{2,26},{10... | collective-permute-start | bytes 1572872 | tf_op jit(solution)/shard_map/ppermute | solution.py:416
  492.4 318.5 %all-gather.8.cloned.1.call-start = ((), (), s32[]{:S(2)}) async-start(), calls=%async_computation.5 | async-start | bytes 14155776 | tf_op jit(solution)/shard_map/all_gather | solution.py:632
  492.5 68.6 %collective-permute-start.40 = (bf16[128,2048]{1,0:T(8,128)(2,1)}, bf16[128,2048]{1,0:T(8,128)(2,1)S(1)}, u32[]{:S(2)}, u32[]{:S(2)}) collective-permute-start(bf16[128,2048]{1,0:T(8,128)(2,1)} %bitcast.468), channel_id=1, source_target_pairs={{0,8},{8,0},{16,24},{24,16},{1,9},{9,1},{17,25},{25,17},{2,10},{10... | collective-permute-start | bytes 1572872 | tf_op jit(solution)/shard_map/ppermute | solution.py:416
  526.1 35.0 %collective-permute-start.42 = (bf16[128,2048]{1,0:T(8,128)(2,1)}, bf16[128,2048]{1,0:T(8,128)(2,1)S(1)}, u32[]{:S(2)}, u32[]{:S(2)}) collective-permute-start(bf16[128,2048]{1,0:T(8,128)(2,1)} %bitcast.469), channel_id=1, source_target_pairs={{0,24},{8,16},{16,8},{24,0},{1,25},{9,17},{17,9},{25,1},{2,26},{10... | collective-permute-start | bytes 1572872 | tf_op jit(solution)/shard_map/ppermute | solution.py:416
  529.4 54.2 %collective-permute-start.41 = (bf16[128,2048]{1,0:T(8,128)(2,1)}, bf16[128,2048]{1,0:T(8,128)(2,1)S(1)}, u32[]{:S(2)}, u32[]{:S(2)}) collective-permute-start(bf16[128,2048]{1,0:T(8,128)(2,1)} %bitcast.470), channel_id=1, source_target_pairs={{0,16},{8,24},{16,0},{24,8},{1,17},{9,25},{17,1},{25,9},{2,18},{10... | collective-permute-start | bytes 1572872 | tf_op jit(solution)/shard_map/ppermute | solution.py:416
  607.0 35.4 %collective-permute-start.32 = (bf16[2,2,128,2048]{3,2,1,0:T(8,128)(2,1)}, bf16[2,2,128,2048]{3,2,1,0:T(8,128)(2,1)}, u32[]{:S(2)}, u32[]{:S(2)}) collective-permute-start(bf16[2,2,128,2048]{3,2,1,0:T(8,128)(2,1)} %slice_bitcast_fusion), channel_id=1, source_target_pairs={{0,1},{1,0},{2,3},{3,2},{4,5},{5,4},{6,7},{7,6},{8,9},{9,8},{10,11... | collective-permute-start | bytes 6291464 | tf_op jit(solution)/shard_map/ppermute | solution.py:416
  608.1 20.4 %collective-permute-start.11 = (bf16[2,128,1024]{2,1,0:T(8,128)(2,1)S(1)}, bf16[2,128,1024]{2,1,0:T(8,128)(2,1)S(1)}, u32[]{:S(2)}, u32[]{:S(2)}) collective-permute-start(bf16[2,128,1024]{2,1,0:T(8,128)(2,1)S(1)} %slice_bitcast_fusion.25), channel_id=1, source_target_pairs={{0,2},{1,3},{2,0},{3,1},{4,6},{5,7},{6,4},{7,5},{8,10},{9,11},{10,... | collective-permute-start | bytes 1572872 | tf_op jit(solution)/shard_map/ppermute | solution.py:416
  616.3 13.7 %collective-permute-start.13 = (bf16[2,128,1024]{2,1,0:T(8,128)(2,1)S(1)}, bf16[2,128,1024]{2,1,0:T(8,128)(2,1)S(1)}, u32[]{:S(2)}, u32[]{:S(2)}) collective-permute-start(bf16[2,128,1024]{2,1,0:T(8,128)(2,1)S(1)} %slice_bitcast_fusion.23), channel_id=1, source_target_pairs={{0,4},{1,5},{2,6},{3,7},{4,0},{5,1},{6,2},{7,3},{8,12},{9,13},{10,... | collective-permute-start | bytes 1572872 | tf_op jit(solution)/shard_map/ppermute | solution.py:416
  634.4 15.4 %collective-permute-start.12 = (bf16[128,1024]{1,0:T(8,128)(2,1)S(1)}, bf16[128,1024]{1,0:T(8,128)(2,1)S(1)}, u32[]{:S(2)}, u32[]{:S(2)}) collective-permute-start(bf16[128,1024]{1,0:T(8,128)(2,1)S(1)} %fusion.62), channel_id=1, source_target_pairs={{0,4},{1,5},{2,6},{3,7},{4,0},{5,1},{6,2},{7,3},{8,12},{9,13},{10,... | collective-permute-start | bytes 786440 | tf_op jit(solution)/shard_map/ppermute | solution.py:416
  648.6 29.6 %collective-permute-start.33 = (bf16[2,128,1024]{2,1,0:T(8,128)(2,1)}, bf16[2,128,1024]{2,1,0:T(8,128)(2,1)}, u32[]{:S(2)}, u32[]{:S(2)}) collective-permute-start(bf16[2,128,1024]{2,1,0:T(8,128)(2,1)} %slice_bitcast_fusion.17), channel_id=1, source_target_pairs={{0,2},{1,3},{2,0},{3,1},{4,6},{5,7},{6,4},{7,5},{8,10},{9,11},{10,... | collective-permute-start | bytes 1572872 | tf_op jit(solution)/shard_map/ppermute | solution.py:416
  649.2 29.0 %collective-permute-start.35 = (bf16[2,128,1024]{2,1,0:T(8,128)(2,1)}, bf16[2,128,1024]{2,1,0:T(8,128)(2,1)}, u32[]{:S(2)}, u32[]{:S(2)}) collective-permute-start(bf16[2,128,1024]{2,1,0:T(8,128)(2,1)} %slice_bitcast_fusion.15), channel_id=1, source_target_pairs={{0,4},{1,5},{2,6},{3,7},{4,0},{5,1},{6,2},{7,3},{8,12},{9,13},{10,... | collective-permute-start | bytes 1572872 | tf_op jit(solution)/shard_map/ppermute | solution.py:416
  (65 other events, 915.8 us)
Sparse Core Ops, SparseCore 0:
  9.9 39.9 all-gather.9
  423.9 230.0 all-reduce.2
  656.1 80.9 all-gather.5
  739.0 71.9 all-gather.7

commit v2 on v1

v2 whole, which is shorter than its diff:
```python
import functools
import math
import jax
import jax.numpy as jnp
from jax import lax
from jax.experimental import pallas as pl
from jax.experimental.pallas import tpu as pltpu
from jax.sharding import PartitionSpec as P

BF16 = jnp.bfloat16
F32 = jnp.float32
SUB = 8
LANES = 128
GELU_A = math.sqrt(2.0 / math.pi)
GELU_B = 0.044715


def dot(left, right):
    return jnp.dot(left, right, preferred_element_type=F32)


def dot_over(left, right):
    return lax.dot_general(
        left, right, (((0,), (0,)), ((), ())), preferred_element_type=F32
    )


def dot_back(left, right):
    return lax.dot_general(
        left, right, (((1,), (1,)), ((), ())), preferred_element_type=F32
    )


def gelu_parts(v):
    square = v * v
    th = jnp.tanh(GELU_A * v * (1.0 + GELU_B * square))
    value = 0.5 * v * (1.0 + th)
    slope = 0.5 * (1.0 + th) + 0.5 * v * (1.0 - th * th) * (
        GELU_A * (1.0 + 3.0 * GELU_B * square)
    )
    return value, slope


def minus_expm1(v):
    series = jnp.full_like(v, 1.0 / 40320.0)
    for factorial in (5040.0, 720.0, 120.0, 24.0, 6.0, 2.0, 1.0):
        series = series * v + 1.0 / factorial
    return jnp.where(v > -0.5, -v * series, 1.0 - jnp.exp(v))


def sub_iota(width):
    return lax.broadcasted_iota(jnp.int32, (SUB, width), 0)


def roll_down(v, first):
    return jnp.where(sub_iota(v.shape[1]) == 0, first, pltpu.roll(v, 1, 0))


def roll_up(v, last):
    return jnp.where(sub_iota(v.shape[1]) == SUB - 1, last, pltpu.roll(v, SUB - 1, 0))


def rows8(step):
    return pl.ds(pl.multiple_of(step * SUB, SUB), SUB)


def strided_load(refs, s, steps):
    return jnp.concatenate([r[pl.ds(s, SUB, stride=steps), :] for r in refs], axis=1)


def strided_store(ref, s, steps, v):
    for n in range(ref.shape[0]):
        ref.at[n][pl.ds(s, SUB, stride=steps), :] = v[:, n * LANES : (n + 1) * LANES]


def forward_kernel(*refs, taps, groups):
    forward_body(refs[:groups], *refs[groups:], taps=taps)


def forward_body(
    branch_refs,
    chan_ref,
    gw_ref,
    states_ref,
    decay_ref,
    rgate_ref,
    igate_ref,
    scale_ref,
    low_ref,
    brow_ref,
    enter_ref,
    ext,
    pre0,
    pre1,
    prod,
    tail,
    carry,
    *,
    taps,
):
    rows, width = states_ref.shape
    steps = rows // SUB
    halo = taps - 1

    @pl.when(pl.program_id(1) == 0)
    def _():
        tail[...] = jnp.zeros_like(tail)
        carry[...] = jnp.zeros_like(carry)

    def load(s, _):
        v = strided_load(branch_refs, s, steps).astype(BF16).astype(F32)
        ext[rows8(s + halo), :] = v
        return 0

    lax.fori_loop(0, steps, load, 0, unroll=4)
    for back in range(1, halo + 1):
        v = ext[rows8(halo + steps - back), :]
        ext[rows8(halo - back), :] = roll_down(v, tail[back - 1 : back, :])
        tail[back - 1 : back, :] = v[SUB - 1 : SUB]
    big = 8
    wide = SUB * big

    def block(i):
        return pl.ds(pl.multiple_of(i * wide, wide), wide)

    def conv(i, _):
        out = chan_ref[taps : taps + 1, :]
        for k in range(taps):
            v = ext[pl.ds(pl.multiple_of((i * big + halo - k) * SUB, SUB), wide), :]
            out = out + chan_ref[k : k + 1, :] * v
            if k == 0:
                brow_ref[block(i), :] = v.astype(BF16)
        low_ref[block(i), :] = out.astype(BF16)
        return 0

    lax.fori_loop(0, steps // big, conv, 0)
    low = low_ref[...]
    pre0[...] = dot_back(low, gw_ref[0, 0])
    pre1[...] = dot_back(low, gw_ref[1, 0])

    def gates(i, _):
        r = jax.nn.sigmoid(pre0[block(i), :] + chan_ref[taps + 1 : taps + 2, :])
        g = jax.nn.sigmoid(pre1[block(i), :] + chan_ref[taps + 2 : taps + 3, :])
        log_decay = r * chan_ref[taps + 3 : taps + 4, :]
        scale = jnp.sqrt(minus_expm1(2.0 * log_decay))
        rgate_ref[block(i), :] = r
        igate_ref[block(i), :] = g
        scale_ref[block(i), :] = scale
        decay_ref[block(i), :] = jnp.exp(log_decay)
        pre0[block(i), :] = scale * g * low_ref[block(i), :].astype(F32)
        return 0

    lax.fori_loop(0, steps // big, gates, 0)

    def scan(s, hp):
        h, p = hp
        a = decay_ref[rows8(s), :]
        h = a * h + pre0[rows8(s), :]
        p = a * p
        states_ref[rows8(s), :] = h
        prod[rows8(s), :] = p
        return h, p

    zero = jnp.zeros((SUB, width), F32)
    h, p = lax.fori_loop(0, steps, scan, (zero, zero + 1.0), unroll=8)
    for shift in (1, 2, 4):
        keep = sub_iota(width) >= shift
        h = h + p * jnp.where(keep, pltpu.roll(h, shift, 0), 0.0)
        p = p * jnp.where(keep, pltpu.roll(p, shift, 0), 1.0)
    first = carry[0:1, :]
    ends = h + p * first
    enter = roll_down(ends, first)
    enter_ref[...] = enter
    carry[0:1, :] = ends[SUB - 1 : SUB]

    def finish(s, _):
        states_ref[rows8(s), :] = states_ref[rows8(s), :] + prod[rows8(s), :] * enter
        return 0

    lax.fori_loop(0, steps, finish, 0, unroll=8)


def mix_kernel(*refs, groups):
    states_ref, mixed_ref, gperm_ref, out = refs[groups:]
    rows, width = states_ref.shape
    steps = rows // SUB

    def body(s, _):
        v = strided_load(refs[:groups], s, steps)
        gperm_ref[rows8(s), :] = v
        strided_store(out, s, steps, gelu_parts(v)[0] * states_ref[rows8(s), :])
        return 0

    lax.fori_loop(0, steps, body, 0, unroll=8)
    for n in range(width // LANES):
        mixed_ref[:, n * LANES : (n + 1) * LANES] = out[n].astype(BF16)


def mix_forward(gate_branch, states, head, chunk):
    total, width = states.shape
    groups = head // LANES
    blk = pl.BlockSpec((chunk, head), lambda j, c: (c, j))
    lane = [
        pl.BlockSpec((chunk, LANES), lambda j, c, n=n: (c, j * groups + n))
        for n in range(groups)
    ]
    return pl.pallas_call(
        functools.partial(mix_kernel, groups=groups),
        grid=(width // head, total // chunk),
        in_specs=lane + [blk],
        out_specs=[blk, blk],
        out_shape=[
            jax.ShapeDtypeStruct((total, width), BF16),
            jax.ShapeDtypeStruct((total, width), F32),
        ],
        scratch_shapes=[pltpu.VMEM((groups, chunk, LANES), F32)],
        compiler_params=pltpu.CompilerParams(
            dimension_semantics=("arbitrary", "arbitrary"), vmem_limit_bytes=60 << 20
        ),
        name="mix_forward",
    )(*[gate_branch] * groups, states)


def recur_forward(projected, chan, gate_w, taps, chunk):
    total, width = projected.shape
    head = gate_w.shape[2]
    heads = width // head
    chunks = total // chunk
    rows = lambda j, c: (c, j)
    blk = pl.BlockSpec((chunk, head), rows)
    f32s = jax.ShapeDtypeStruct((total, width), F32)
    b16s = jax.ShapeDtypeStruct((total, width), BF16)
    work = pltpu.VMEM((chunk, head), F32)
    groups = head // LANES
    lane = [
        pl.BlockSpec((chunk, LANES), lambda j, c, n=n: (c, j * groups + n))
        for n in range(groups)
    ]
    return pl.pallas_call(
        functools.partial(forward_kernel, taps=taps, groups=groups),
        grid=(heads, chunks),
        in_specs=[
            *lane,
            pl.BlockSpec((chan.shape[0], head), lambda j, c: (0, j)),
            pl.BlockSpec((2, 1, head, head), lambda j, c: (0, j, 0, 0)),
        ],
        out_specs=[blk] * 7 + [pl.BlockSpec((SUB, head), rows)],
        out_shape=[f32s, f32s, f32s, f32s, f32s, b16s, b16s]
        + [jax.ShapeDtypeStruct((chunks * SUB, width), F32)],
        scratch_shapes=[
            pltpu.VMEM((chunk + (taps - 1) * SUB, head), F32),
            work,
            work,
            work,
            pltpu.VMEM((SUB, head), F32),
            pltpu.VMEM((SUB, head), F32),
        ],
        compiler_params=pltpu.CompilerParams(
            dimension_semantics=("arbitrary", "arbitrary"), vmem_limit_bytes=60 << 20
        ),
        name="recur_forward",
    )(*[projected] * groups, chan, gate_w)


def gate_back_kernel(*refs, groups):
    mgrad_refs = refs[:groups]
    states_ref, gperm_ref, ggrad_ref, sgrad_ref, out = refs[groups:]
    rows, width = states_ref.shape
    steps = rows // SUB

    def body(s, _):
        value, slope = gelu_parts(gperm_ref[rows8(s), :])
        mg = strided_load(mgrad_refs, s, steps)
        strided_store(out, s, steps, mg * states_ref[rows8(s), :] * slope)
        sgrad_ref[rows8(s), :] = mg * value
        return 0

    lax.fori_loop(0, steps, body, 0, unroll=8)
    for n in range(width // LANES):
        ggrad_ref[:, n * LANES : (n + 1) * LANES] = out[n].astype(BF16)


def gate_backward(mixed_grad, states, gate_rows, head, chunk):
    total, width = mixed_grad.shape
    groups = head // LANES
    blk = pl.BlockSpec((chunk, head), lambda j, c: (c, j))
    lane = [
        pl.BlockSpec((chunk, LANES), lambda j, c, n=n: (c, j * groups + n))
        for n in range(groups)
    ]
    return pl.pallas_call(
        functools.partial(gate_back_kernel, groups=groups),
        grid=(width // head, total // chunk),
        in_specs=lane + [blk, blk],
        out_specs=[blk, blk],
        out_shape=[
            jax.ShapeDtypeStruct((total, width), BF16),
            jax.ShapeDtypeStruct((total, width), F32),
        ],
        scratch_shapes=[pltpu.VMEM((groups, chunk, LANES), F32)],
        compiler_params=pltpu.CompilerParams(
            dimension_semantics=("arbitrary", "arbitrary"), vmem_limit_bytes=60 << 20
        ),
        name="gate_backward",
    )(*[mixed_grad] * groups, states, gate_rows)


def backward_kernel(
    sgrad_ref,
    states_ref,
    decay_ref,
    rgate_ref,
    igate_ref,
    scale_ref,
    low_ref,
    brow_ref,
    enter_ref,
    chan_ref,
    gw_ref,
    pgrad_ref,
    gwg_ref,
    sums_ref,
    car,
    prod,
    cgrad,
    lowf,
    gout,
    pre,
    sums,
    tail,
    carry,
    *,
    taps,
):
    rows, width = states_ref.shape
    steps = rows // SUB
    halo = taps - 1

    @pl.when(pl.program_id(1) == 0)
    def _():
        tail[...] = jnp.zeros_like(tail)
        carry[...] = jnp.zeros_like(carry)
        sums[...] = jnp.zeros_like(sums)
        gwg_ref[...] = jnp.zeros_like(gwg_ref)

    def scan(n, uq):
        u, q = uq
        s = steps - 1 - n
        c = sgrad_ref[rows8(s), :] + u
        car[rows8(s), :] = c
        prod[rows8(s), :] = q
        a = decay_ref[rows8(s), :]
        return a * c, a * q

    zero = jnp.zeros((SUB, width), F32)
    u, q = lax.fori_loop(0, steps, scan, (zero, zero + 1.0), unroll=8)
    for shift in (1, 2, 4):
        keep = sub_iota(width) < SUB - shift
        u = u + q * jnp.where(keep, pltpu.roll(u, SUB - shift, 0), 0.0)
        q = q * jnp.where(keep, pltpu.roll(q, SUB - shift, 0), 1.0)
    last = carry[0:1, :]
    ends = u + q * last
    enter = roll_up(ends, last)
    carry[0:1, :] = ends[0:1]
    neg = chan_ref[taps + 3 : taps + 4, :]
    state_in = enter_ref[...]

    def gates(s, acc):
        sum_r, sum_i, sum_d = acc
        c = car[rows8(s), :] + prod[rows8(s), :] * enter
        before = jnp.where(
            s == 0, state_in, states_ref[rows8(jnp.maximum(s - 1, 0)), :]
        )
        a = decay_ref[rows8(s), :]
        r = rgate_ref[rows8(s), :]
        g = igate_ref[rows8(s), :]
        scale = scale_ref[rows8(s), :]
        low = lowf[rows8(s), :]
        c_low = c * low
        dgrad = c * a * before - c_low * g * (a * a) / scale
        pr = dgrad * neg * r * (1.0 - r)
        pi = c_low * scale * g * (1.0 - g)
        pre[0, rows8(s), :] = pr
        pre[1, rows8(s), :] = pi
        cgrad[rows8(s), :] = c * scale * g
        pr = pr.astype(BF16).astype(F32)
        pi = pi.astype(BF16).astype(F32)
        return sum_r + pr, sum_i + pi, sum_d + dgrad * r

    lowf[...] = low_ref[...].astype(F32)
    sum_r, sum_i, sum_d = lax.fori_loop(0, steps, gates, (zero, zero, zero), unroll=4)
    low = low_ref[...]
    pr = pre[0].astype(BF16)
    pi = pre[1].astype(BF16)
    gwg_ref[0, 0] += dot_over(pr, low)
    gwg_ref[1, 0] += dot_over(pi, low)
    cgrad[pl.ds(0, rows), :] = (
        cgrad[pl.ds(0, rows), :] + dot(pr, gw_ref[0, 0]) + dot(pi, gw_ref[1, 0])
    )
    for ahead in range(halo):
        v = cgrad[rows8(ahead), :]
        cgrad[rows8(steps + ahead), :] = roll_up(v, tail[ahead : ahead + 1, :])
        tail[ahead : ahead + 1, :] = v[0:1]
    car[...] = brow_ref[...].astype(F32)

    def conv(s, acc):
        branch = car[rows8(s), :]
        out = zero
        new = []
        for k in range(taps):
            v = cgrad[rows8(s + k), :]
            out = out + chan_ref[k : k + 1, :] * v
            new.append(acc[k] + v * branch)
            if k == 0:
                new_bias = acc[taps] + v
        strided_store(gout, s, steps, out)
        return (*new, new_bias)

    acc = lax.fori_loop(0, steps, conv, (zero,) * (taps + 1), unroll=4)
    for n in range(width // LANES):
        pgrad_ref[:, n * LANES : (n + 1) * LANES] = gout[n].astype(BF16)
    for n, v in enumerate((*acc, sum_r, sum_i, sum_d)):
        sums[n] += v
        sums_ref[n : n + 1, :] = jnp.sum(sums[n], axis=0, keepdims=True)


def recur_backward(state_grad, saved, chan, gate_w, taps, chunk):
    total, width = state_grad.shape
    head = gate_w.shape[2]
    heads = width // head
    chunks = total // chunk
    rows = lambda j, c: (chunks - 1 - c, j)
    blk = pl.BlockSpec((chunk, head), rows)
    work = pltpu.VMEM((chunk, head), F32)
    gws = pl.BlockSpec((2, 1, head, head), lambda j, c: (0, j, 0, 0))
    groups = head // LANES
    n_sums = -(-(taps + 4) // SUB) * SUB
    return pl.pallas_call(
        functools.partial(backward_kernel, taps=taps),
        grid=(heads, chunks),
        in_specs=[blk] * 8
        + [
            pl.BlockSpec((SUB, head), rows),
            pl.BlockSpec((chan.shape[0], head), lambda j, c: (0, j)),
            gws,
        ],
        out_specs=[
            blk,
            gws,
            pl.BlockSpec((n_sums, head), lambda j, c: (0, j)),
        ],
        out_shape=[
            jax.ShapeDtypeStruct((total, width), BF16),
            jax.ShapeDtypeStruct((2, heads, head, head), F32),
            jax.ShapeDtypeStruct((n_sums, width), F32),
        ],
        scratch_shapes=[
            work,
            work,
            pltpu.VMEM((chunk + (taps - 1) * SUB, head), F32),
            work,
            pltpu.VMEM((groups, chunk, LANES), F32),
            pltpu.VMEM((2, chunk, head), F32),
            pltpu.VMEM((taps + 4, SUB, head), F32),
            pltpu.VMEM((SUB, head), F32),
            pltpu.VMEM((SUB, head), F32),
        ],
        compiler_params=pltpu.CompilerParams(
            dimension_semantics=("arbitrary", "arbitrary"), vmem_limit_bytes=60 << 20
        ),
        name="recur_backward",
    )(state_grad, *saved, chan, gate_w)


def split_kernel(table_ref, src, dst, *, half):
    _, rows, width = dst.shape
    n = pl.num_programs(0)
    first = pl.multiple_of(table_ref[pl.program_id(0)], LANES)
    start = pl.multiple_of(table_ref[n], rows)
    dst[0] = src[pl.ds(start, rows), half, pl.ds(first, width)]


def split_columns(weight, half, firsts, head, span, start, rows):
    total, _, lru = weight.shape
    n = len(firsts)
    table = jnp.stack([jnp.int32(f * head) for f in firsts] + [start])
    return pl.pallas_call(
        functools.partial(split_kernel, half=half),
        grid_spec=pltpu.PrefetchScalarGridSpec(
            num_scalar_prefetch=1,
            grid=(n,),
            in_specs=[pl.BlockSpec((total, 2, lru), lambda w, table: (0, 0, 0))],
            out_specs=pl.BlockSpec((1, rows, span * head), lambda w, table: (w, 0, 0)),
        ),
        out_shape=jax.ShapeDtypeStruct((n, rows, span * head), weight.dtype),
        name="split_columns",
    )(table, weight)


def far_kernel(
    normed_ref,
    cot_ref,
    gate_ref,
    up_ref,
    wout_ref,
    own_gate_ref,
    own_up_ref,
    own_out_ref,
    ggate_ref,
    gup_ref,
    gout_ref,
):
    @pl.when(pl.program_id(0) == 0)
    def _():
        ggate_ref[...] = own_gate_ref[...]
        gup_ref[...] = own_up_ref[...]
        gout_ref[...] = own_out_ref[...]

    normed = normed_ref[...]
    cot = cot_ref[...]
    value, slope = gelu_parts(dot(normed, gate_ref[...]))
    up = dot(normed, up_ref[...])
    grad = dot_back(cot, wout_ref[...])
    gout_ref[...] += dot_over((value * up).astype(BF16), cot)
    ggate_ref[...] += dot_over(normed, (grad * up * slope).astype(BF16))
    gup_ref[...] += dot_over(normed, (grad * value).astype(BF16))


def far_grads(normed, cot, weight_in, weight_out, sums, part, parts):
    total, width = normed.shape
    hidden = weight_out.shape[0] // parts
    rows = min(512, total)
    once = pl.Buffered(1)
    data = pl.BlockSpec((rows, width), lambda i: (i, 0))
    cols = lambda i: (0, part)
    lines = lambda i: (part, 0)
    held = pl.BlockSpec((width, hidden), cols, pipeline_mode=once)
    up = pl.BlockSpec((width, hidden), lambda i: (0, parts + part), pipeline_mode=once)
    held_out = pl.BlockSpec((hidden, width), lines, pipeline_mode=once)
    return pl.pallas_call(
        far_kernel,
        grid=(total // rows,),
        in_specs=[data, data, held, up, held_out, held, held, held_out],
        out_specs=[
            pl.BlockSpec((width, hidden), cols),
            pl.BlockSpec((width, hidden), cols),
            pl.BlockSpec((hidden, width), lines),
        ],
        out_shape=[jax.ShapeDtypeStruct(v.shape, F32) for v in sums],
        input_output_aliases={5: 0, 6: 1, 7: 2},
        cost_estimate=pl.CostEstimate(
            flops=12 * total * width * hidden,
            bytes_accessed=4 * total * width + 30 * width * hidden,
            transcendentals=total * hidden,
        ),
        compiler_params=pltpu.CompilerParams(
            dimension_semantics=("arbitrary",), vmem_limit_bytes=60 << 20
        ),
        name="far_grads",
    )(normed, cot, weight_in, weight_in, weight_out, *sums)


def norm_kernel(src, gain, dst):
    rows = src[0].astype(F32)
    inv = lax.rsqrt(jnp.mean(rows * rows, axis=-1, keepdims=True) + 1e-06)
    dst[...] = (rows * inv * gain[...]).astype(BF16)


def norm_packed(packed, gain, size):
    n, _, width = packed.shape
    return pl.pallas_call(
        norm_kernel,
        grid=(n,),
        in_specs=[
            pl.BlockSpec((1, size, width), lambda w: (w, 0, 0)),
            pl.BlockSpec((1, width), lambda w: (0, 0)),
        ],
        out_specs=pl.BlockSpec((size, width), lambda w: (w, 0)),
        out_shape=jax.ShapeDtypeStruct((n * size, width), BF16),
        name="norm_packed",
    )(packed, gain)


def join_kernel(first, second, joined):
    joined[:, 0, :] = first[...].astype(F32)
    joined[:, 1, :] = second[...].astype(F32)


def join_halves(first, second):
    total, width = first.shape
    rows = math.gcd(total, 512)
    block = pl.BlockSpec((rows, width), lambda i: (i, 0))
    return pl.pallas_call(
        join_kernel,
        grid=(total // rows,),
        in_specs=[block, block],
        out_specs=pl.BlockSpec((rows, 2, width), lambda i: (i, 0, 0)),
        out_shape=jax.ShapeDtypeStruct((total, 2, width), F32),
        compiler_params=pltpu.CompilerParams(vmem_limit_bytes=60 << 20),
        name="join_halves",
    )(first, second)


def bit_list(n):
    return [1 << i for i in range(n.bit_length() - 1)]


def swap(block, axis, bit):
    return lax.ppermute(block, axis, [(i, i ^ bit) for i in range(lax.axis_size(axis))])


def gather_steps(block):
    n = lax.axis_size("wide")
    links = bit_list(n)[1:]
    half = block.shape[1] // 2
    sides = [block[:, :half], block[:, half:]]
    orders = [links, links[::-1]]
    for m, bits in enumerate(zip(*orders)):
        got = yield [swap(side, "wide", bit) for side, bit in zip(sides, bits)]
        sides = [jnp.stack([s, g], axis=m) for s, g in zip(sides, got)]
    for i, order in enumerate(orders):
        place = sorted(range(len(order)), key=lambda k: -order[k])
        sides[i] = sides[i].transpose(*place, len(order), len(order) + 1)
    return jnp.concatenate(sides, axis=-1).reshape(-1, block.shape[1])


def other_core(rows):
    return swap(rows, "wide", 1)


def scatter_steps(keep, send):
    n = lax.axis_size("wide")
    links = bit_list(n)[1:]
    rows, width = keep.shape[0] // (n // 2), keep.shape[1]
    half = width // 2
    got = yield [other_core(send)]
    held = keep + got[0].astype(F32)
    held = held.reshape((2,) * len(links) + (rows, width))
    sides = [held[..., :half], held[..., half:]]
    axes = [links[::-1], links[::-1]]
    for bits in zip(links, links[::-1]):
        kept, sent = [], []
        for i, bit in enumerate(bits):
            axis = axes[i].index(bit)
            kept.append(lax.index_in_dim(sides[i], 0, axis, keepdims=False))
            part = lax.index_in_dim(sides[i], 1, axis, keepdims=False)
            sent.append(swap(part.astype(BF16), "wide", bit))
            axes[i] = axes[i][:axis] + axes[i][axis + 1 :]
        got = yield sent
        sides = [k + g.astype(F32) for k, g in zip(kept, got)]
    return jnp.concatenate(sides, axis=-1)


def run_steps(steps, arrived=None):
    try:
        while True:
            arrived = steps.send(arrived)
    except StopIteration as end:
        return end.value


def tie(value, *before):
    return lax.optimization_barrier((value, *before))[0]


def line_step(part, stage):
    n = lax.axis_size("seq")
    if n < 2 or n % 2:
        return lax.psum(part, "seq") if stage == 1 else part
    here = lax.axis_index("seq")

    def step(pairs):
        got = lax.ppermute(part, "seq", pairs)
        return got, (part.astype(F32) + got.astype(F32)).astype(BF16)

    middle = n // 2
    if stage == 0:
        for k in range(middle - 1):
            part = step([(k, k + 1), (n - 1 - k, n - 2 - k)])[1]
    elif stage == 1:
        part = step([(middle - 1, middle), (middle, middle - 1)])[1]
    else:
        for k in range(middle - 2, -1, -1):
            got = step([(k + 1, k), (n - 2 - k, n - 1 - k)])[0]
            part = jnp.where((here == k) | (here == n - 1 - k), got, part)
    return part


def sum_small(values, axis):
    n = lax.axis_size(axis)
    if n & (n - 1):
        return lax.psum(values, axis)
    length = values.shape[0]
    padded = jnp.pad(values, (0, -length % (SUB * LANES))).reshape(-1, LANES)
    for bit in bit_list(n):
        padded = padded + swap(padded, axis, bit)
    return padded.reshape(-1)[:length]


def exchange(blocks):
    return lax.all_to_all(blocks, "wide", split_axis=0, concat_axis=0, tiled=True)


def near_place(r, n):
    return 2 * (r % (n // 2)) + r // (n // 2)


def move_kernel(table_ref, src, dst):
    dst[...] = src[...]


def move_rows(rows, near):
    n = lax.axis_size("wide")
    here = lax.axis_index("wide")
    size = rows.shape[0] // n
    table = jnp.stack([here ^ near_place(r, n) for r in range(n)]).astype(jnp.int32)
    device = lambda r, table: (table[r], 0)
    place = lambda r, table: (r, 0)
    block = (size, rows.shape[1])
    return pl.pallas_call(
        move_kernel,
        grid_spec=pltpu.PrefetchScalarGridSpec(
            num_scalar_prefetch=1,
            grid=(n,),
            in_specs=[pl.BlockSpec(block, device if near else place)],
            out_specs=pl.BlockSpec(block, place if near else device),
        ),
        out_shape=jax.ShapeDtypeStruct(rows.shape, rows.dtype),
        name="move_rows",
    )(table, rows)


def to_near(rows):
    return move_rows(rows, True)


def from_near(rows):
    return move_rows(rows, False)


def gather_small(block):
    n = lax.axis_size("wide")
    here = lax.axis_index("wide")
    held = block[None]
    for bit in bit_list(n):
        held = jnp.concatenate([held, swap(held, "wide", bit)])
    return jnp.concatenate(
        [lax.dynamic_slice_in_dim(held, here ^ w, 1) for w in range(n)]
    )


def norm_rows(rows):
    inv = lax.rsqrt(jnp.mean(rows * rows, axis=-1, keepdims=True) + 1e-06)
    return inv, rows * inv


def norm_back(grad, gain, inv, unit):
    scaled = grad * gain
    return inv * (scaled - unit * jnp.mean(scaled * unit, axis=-1, keepdims=True))


def feed_forward_back(gate_up, cot, weight_out):
    hidden_width = weight_out.shape[0]
    gate, up = gate_up[:, :hidden_width], gate_up[:, hidden_width:]
    value, slope = gelu_parts(gate)
    hidden_grad = dot_back(cot, weight_out)
    hidden = (value * up).astype(BF16)
    gate_up_grad = jnp.concatenate(
        [
            (hidden_grad * up * slope).astype(BF16),
            (hidden_grad * value).astype(BF16),
        ],
        axis=1,
    )
    return hidden, gate_up_grad


def feed_forward(normed, cot, weight_in, weight_out):
    return feed_forward_back(dot(normed, weight_in), cot, weight_out)


def shards(
    tokens,
    cotangent,
    norm_gains,
    in_weight,
    conv_weight,
    conv_bias,
    gate_weights,
    gate_biases,
    decay_param,
    out_weight,
    mlp_in_weight,
    mlp_out_weight,
):
    n_wide, n_seq = lax.axis_size("wide"), lax.axis_size("seq")
    here = lax.axis_index("wide")
    tok_low, cot_low = tokens[0], cotangent[0]
    size, width = tok_low.shape
    own = out_weight.shape[0]
    lru = own * n_wide
    heads, head = gate_weights.shape[1:3]
    taps = conv_weight.shape[0]
    gain_own = norm_gains.shape[1]
    hidden_units = mlp_out_weight.shape[0]
    part = head // n_wide

    span = max(
        ((w + 1) * own - 1) // head - w * own // head + 1 for w in range(n_wide)
    )
    firsts = [min(w * own // head, heads - span) for w in range(n_wide)]
    win = span * head
    start = jnp.minimum(here * own // head, heads - span) * head
    offset = here * own - start

    total = size * n_wide
    half = total // 2
    recompute = n_seq * total <= 8192 and n_seq & (n_seq - 1) == 0 and n_seq > 1

    def far_rows(rows):
        return [swap(rows, "seq", d) for d in range(1, n_seq)] if recompute else []

    def far_gather(rows):
        return lax.all_gather(jnp.concatenate(rows), "wide", axis=0, tiled=True)

    small = jnp.concatenate(
        [
            norm_gains.reshape(-1),
            conv_weight.reshape(-1),
            conv_bias,
            gate_biases.reshape(-1),
            decay_param,
        ]
    )
    n_small = small.shape[0]
    small = jnp.pad(small, (0, -n_small % (16 * width))).reshape(-1, width)
    gate_rows = heads * part * head // width
    packed = jnp.concatenate(
        [
            tok_low,
            small,
            gate_weights.transpose(0, 1, 3, 2).reshape(2 * gate_rows, width),
        ]
    )
    got = lax.all_gather(packed, "wide")
    gates_all = got[:, -2 * gate_rows :].reshape(n_wide, 2, gate_rows, width)
    gate_rows = gate_rows // heads
    small = got[:, size : -2 * heads * gate_rows].reshape(n_wide, -1)[:, :n_small]

    own_rows = in_weight.shape[0]
    shared = n_seq % 2 == 0 and own_rows % 32 == 0
    row_part = own_rows // 2 if shared else own_rows
    odd = lax.axis_index("seq") % 2

    def fetch(half):
        begin = (odd * row_part if shared else odd * 0).astype(jnp.int32)
        return split_columns(in_weight, half, firsts, head, span, begin, row_part)

    def share(rows):
        return swap(rows, "seq", 1) if shared else ()

    def whole(rows, other):
        if shared:
            even = jnp.where(odd == 0, rows, other)
            rows = jnp.stack([even, jnp.where(odd == 0, other, rows)], axis=1)
        return rows.reshape(width, win)

    branch_mine = exchange(fetch(0))
    gate_mine = exchange(fetch(1))
    branch_other, gate_other = share(branch_mine), share(gate_mine)
    in_branch = whole(branch_mine, branch_other)
    gains = (
        small[:, : 2 * gain_own]
        .reshape(n_wide, 2, gain_own)
        .transpose(1, 0, 2)
        .reshape(2, width)
        .astype(F32)
    )
    channels = (
        small[:, 2 * gain_own :]
        .reshape(n_wide, taps + 4, own)
        .transpose(1, 0, 2)
        .reshape(taps + 4, lru)
    )
    channels = lax.dynamic_slice_in_dim(channels, start, win, axis=1).astype(F32)
    chan = jnp.concatenate(
        [channels[: taps + 3], -8.0 * jax.nn.softplus(-channels[taps + 3 :])]
    )
    normed_all = norm_packed(got, gains[:1], size)
    out_own = lax.dynamic_update_slice_in_dim(
        jnp.zeros((win, width), BF16), out_weight, offset, 0
    )
    mlp_in = mlp_in_weight.reshape(width, -1)

    in_branch, normed_all, chan, gains, out_own, mlp_in, gate_mine, gate_other = (
        lax.optimization_barrier(
            (in_branch, normed_all, chan, gains, out_own, mlp_in, gate_mine, gate_other)
        )
    )

    in_gate = whole(gate_mine, gate_other)

    below = max(w * own - f * head for w, f in enumerate(firsts))
    above = max(f * head + win - (w + 1) * own for w, f in enumerate(firsts))
    if max(below, above) <= own:
        around = [
            lax.ppermute(
                out_weight[own - below :],
                "wide",
                [(i, i + 1) for i in range(n_wide - 1)],
            ),
            out_weight,
            lax.ppermute(
                out_weight[:above], "wide", [(i + 1, i) for i in range(n_wide - 1)]
            ),
        ]
        first_row = below - offset
    else:
        around = [lax.all_gather(out_weight, "wide", axis=0, tiled=True)]
        first_row = start
    cot_sent = far_rows(cot_low)
    cot_all = lax.all_gather(tie(cot_low, in_branch), "wide", axis=0, tiled=True)
    gate_w = (
        lax.dynamic_slice_in_dim(
            gates_all, start // head * gate_rows, span * gate_rows, axis=2
        )
        .reshape(n_wide, 2, span, part, head)
        .transpose(1, 2, 0, 3, 4)
        .reshape(2, span, head, head)
    )
    chunk = min(total, 512)
    states, *saved, enter = recur_forward(
        dot(normed_all, in_branch), chan, gate_w, taps, chunk
    )
    in_gate, states, around = lax.optimization_barrier((in_gate, states, around))
    mixed, gate_rows = mix_forward(dot(normed_all, in_gate), states, head, chunk)
    mixed_near = to_near(mixed)
    out_send = dot(mixed_near[half:], out_own).astype(BF16)
    out_send, mixed_near, cot_all = lax.optimization_barrier(
        (out_send, mixed_near, cot_all)
    )
    rows = tok_low.astype(F32)
    steps = scatter_steps(dot(mixed_near[:half], out_own), out_send)
    way = lax.optimization_barrier(steps.send(None))
    way = steps.send(way)
    in_own = jnp.concatenate(
        [
            lax.dynamic_slice_in_dim(weight, offset, own, axis=1)
            for weight in (in_branch, in_gate)
        ],
        axis=1,
    )
    out_win = lax.dynamic_slice_in_dim(jnp.concatenate(around), first_row, win)
    way, in_own, out_win = lax.optimization_barrier((way, in_own, out_win))
    middle = rows + run_steps(steps, way)
    inv_two, unit_two = norm_rows(middle)
    normed_two = (unit_two * gains[1]).astype(BF16)
    middle, normed_two, inv_two, unit_two, cot_all = lax.optimization_barrier(
        (middle, normed_two, inv_two, unit_two, cot_all)
    )

    steps = gather_steps(normed_two)
    way = steps.send(None)
    sent = far_rows(normed_two)
    cot_near = to_near(cot_all)
    way, cot_near, cot_sent = lax.optimization_barrier((way, cot_near, cot_sent))
    normed_even = run_steps(steps, way)
    normed_even, cot_sent = lax.optimization_barrier((normed_even, cot_sent))
    cot_far = far_gather(cot_sent) if recompute else ()
    normed_near = jnp.concatenate([normed_even, other_core(normed_even)])
    hidden, gate_up_grad = feed_forward(normed_near, cot_near, mlp_in, mlp_out_weight)
    up_send = dot_back(gate_up_grad[half:], mlp_in).astype(BF16)
    (
        up_send,
        hidden,
        gate_up_grad,
        normed_near,
        sent[:1],
    ) = lax.optimization_barrier(
        (
            up_send,
            hidden,
            gate_up_grad,
            normed_near,
            sent[:1],
        )
    )
    steps = scatter_steps(dot_back(gate_up_grad[:half], mlp_in), up_send)
    way = steps.send(None)
    way, gate_up_grad, hidden = lax.optimization_barrier((way, gate_up_grad, hidden))
    way = steps.send(way)
    gate_sum = dot_over(normed_near, gate_up_grad[:, :hidden_units])
    up_sum = dot_over(normed_near, gate_up_grad[:, hidden_units:])
    way, gate_sum, up_sum, hidden = lax.optimization_barrier(
        (way, gate_sum, up_sum, hidden)
    )
    out_sum = dot_over(hidden, cot_near)
    normed_two_grad = run_steps(steps, way)
    middle_grad = cot_low.astype(F32) + norm_back(
        normed_two_grad, gains[1], inv_two, unit_two
    )
    mix_low = middle_grad.astype(BF16)
    gain_two_grad = jnp.sum(normed_two_grad * unit_two, axis=0)
    middle_grad, mix_low, gain_two_grad, out_sum, hidden, cot_far, sent = (
        lax.optimization_barrier(
            (middle_grad, mix_low, gain_two_grad, out_sum, hidden, cot_far, sent)
        )
    )

    normed_far = far_gather(sent) if recompute else ()
    steps = gather_steps(mix_low)
    way = lax.optimization_barrier(steps.send(None))
    way = steps.send(way)
    feed_send = dot(hidden[half:], mlp_out_weight).astype(BF16)
    feed_keep = dot(hidden[:half], mlp_out_weight)
    way, feed_send, feed_keep = lax.optimization_barrier((way, feed_send, feed_keep))
    mix_even = run_steps(steps, way)
    mix_near = jnp.concatenate([mix_even, other_core(mix_even)])
    mix_near = lax.optimization_barrier(mix_near)
    mixed_grad = from_near(dot_back(mix_near, out_win))
    gate_half, state_grad = gate_backward(mixed_grad, states, gate_rows, head, chunk)
    out_grad = lax.dynamic_slice_in_dim(
        dot_over(mixed_near, mix_near).astype(BF16), offset, own
    )

    def in_part(grad):
        return dot_over(normed_all, grad).astype(BF16).reshape(n_wide, -1, own)

    def in_rows(part):
        return jnp.moveaxis(exchange(part), 0, 1).reshape(-1, lru)

    gate_half = lax.dynamic_slice_in_dim(gate_half, offset, own, axis=1)
    gate_part = in_part(gate_half)
    state_grad, gate_part, out_grad = lax.optimization_barrier(
        (state_grad, gate_part, out_grad)
    )
    gate_rows_grad = in_rows(gate_part)
    out_grad = line_step(out_grad, 0)
    branch_half, gate_grad, sums = recur_backward(
        state_grad, (states, *saved, enter), chan, gate_w, taps, chunk
    )
    branch_half = lax.dynamic_slice_in_dim(branch_half, offset, own, axis=1)
    branch_part = in_part(branch_half)
    branch_half, branch_part, gate_grad, sums, gate_rows_grad, normed_far, out_grad = (
        lax.optimization_barrier(
            (branch_half, branch_part, gate_grad, sums, gate_rows_grad, normed_far, out_grad)
        )
    )
    branch_rows_grad = in_rows(branch_part)
    out_grad = line_step(out_grad, 1)
    gate_rows_grad = line_step(gate_rows_grad, 0)
    own_near = to_near(jnp.concatenate([branch_half, gate_half], axis=1))
    normed_send = dot_back(own_near[half:], in_own).astype(BF16)
    normed_keep = dot_back(own_near[:half], in_own)
    normed_send, normed_keep, branch_rows_grad, normed_far = lax.optimization_barrier(
        (normed_send, normed_keep, branch_rows_grad, normed_far)
    )

    parts = hidden_units // 256 if hidden_units % 256 == 0 else 1
    held = (gate_sum, up_sum, out_sum)
    normed_steps = scatter_steps(normed_keep, normed_send)
    feed_steps = scatter_steps(feed_keep, feed_send)

    def far_part(held, done):
        for p in range(done, parts if done == 2 else min(done + 1, parts)):
            if recompute:
                held = far_grads(
                    normed_far, cot_far, mlp_in, mlp_out_weight, held, p, parts
                )
        return held

    way = normed_steps.send(None)
    gate_grad = exchange(
        gate_grad.astype(BF16)
        .reshape(2, span, n_wide, part, head)
        .transpose(2, 0, 1, 3, 4)
    )
    held = far_part(held, 0)
    way, held, out_grad, gate_rows_grad, gate_grad = lax.optimization_barrier(
        (way, held, out_grad, gate_rows_grad, gate_grad)
    )
    way = normed_steps.send(way)
    out_grad = line_step(out_grad, 2)
    gate_rows_grad = line_step(gate_rows_grad, 1)
    branch_rows_grad = line_step(branch_rows_grad, 0)
    holders = [
        next(w for w, f in enumerate(firsts) if f <= j < f + span) for j in range(heads)
    ]
    gate_grad = jnp.stack(
        [gate_grad[w, :, j - firsts[w]] for j, w in enumerate(holders)], axis=1
    )
    held = far_part(held, 1)
    way, held, out_grad, gate_rows_grad, branch_rows_grad, gate_grad, feed_keep = (
        lax.optimization_barrier(
            (way, held, out_grad, gate_rows_grad, branch_rows_grad, gate_grad, feed_keep)
        )
    )
    normed_grad = run_steps(normed_steps, way)
    inv_one, unit_one = norm_rows(rows)
    input_grad = middle_grad + norm_back(normed_grad, gains[0], inv_one, unit_one)
    gain_one_grad = jnp.sum(normed_grad * unit_one, axis=0)
    feed_way = feed_steps.send(None)
    gate_rows_grad = line_step(gate_rows_grad, 2)
    branch_rows_grad = line_step(branch_rows_grad, 1)
    gate_grad = line_step(gate_grad, 0)
    held = far_part(held, 2)
    feed_way, held, gate_rows_grad, branch_rows_grad, gate_grad, gain_one_grad = (
        lax.optimization_barrier(
            (feed_way, held, gate_rows_grad, branch_rows_grad, gate_grad, gain_one_grad)
        )
    )
    feed = run_steps(feed_steps, feed_way)
    result = (middle + feed).astype(BF16)
    branch_rows_grad = line_step(branch_rows_grad, 2)
    gate_grad = line_step(line_step(gate_grad, 1), 2)
    if recompute:
        mlp_in_grad = join_halves(held[0], held[1])
    else:
        mlp_in_grad = jnp.stack(held[:2], axis=1)
    mlp_out_grad = held[2]
    in_grad = join_halves(branch_rows_grad, gate_rows_grad)
    sums = lax.dynamic_slice_in_dim(sums[: taps + 4], offset, own, axis=1)
    gate_grad = gate_grad.astype(F32).transpose(0, 1, 3, 2)
    out_grad = out_grad.astype(F32)

    gains_grad = sum_small(jnp.concatenate([gain_one_grad, gain_two_grad]), "wide")
    gains_grad = lax.dynamic_slice_in_dim(
        gains_grad.reshape(2, width), here * gain_own, gain_own, axis=1
    )
    small = sum_small(
        jnp.concatenate([gains_grad.reshape(-1), sums.reshape(-1)]), "seq"
    )
    gains_grad = small[: 2 * gain_own].reshape(2, gain_own)
    sums = small[2 * gain_own :].reshape(taps + 4, own)
    decay_grad = sums[taps + 3] * 8.0 * jax.nn.sigmoid(-decay_param.astype(F32))
    if not recompute:
        mlp_out_grad, mlp_in_grad = (
            lax.psum(g.astype(BF16), "seq").astype(F32)
            for g in (mlp_out_grad, mlp_in_grad)
        )
    return (
        result[None],
        input_grad[None],
        gains_grad,
        in_grad,
        sums[:taps],
        sums[taps],
        gate_grad,
        sums[taps + 1 : taps + 3],
        decay_grad,
        out_grad,
        mlp_in_grad,
        mlp_out_grad,
    )


def solution(mesh):
    placed = (
        P("seq", "wide", None),
        P("seq", "wide", None),
        P(None, "wide"),
        P("wide", None, None),
        P(None, "wide"),
        P("wide"),
        P(None, None, None, "wide"),
        P(None, "wide"),
        P("wide"),
        P("wide", None),
        P(None, None, "wide"),
        P("wide", None),
    )
    return jax.shard_map(
        shards,
        mesh=mesh,
        in_specs=placed,
        out_specs=(
            P("seq", "wide", None),
            P("seq", "wide", None),
            P(None, "wide"),
            P("wide", None, None),
            P(None, "wide"),
            P("wide"),
            P(None, None, None, "wide"),
            P(None, "wide"),
            P("wide"),
            P("wide", None),
            P(None, None, "wide"),
            P("wide", None),
        ),
        check_vma=False,
    )
```

time: 939 us -> 713 us (0.76)
  waiting for transfers between devices: 286 us -> 126 us
  Pallas kernels: 31.6 us -> 189 us
  blocking collectives: 119 us -> 28.2 us
  matrix products: 181 us -> 94.2 us
  local copies, waits for them, and re-layouts: 126 us -> 74 us
  other arithmetic: 56.5 us -> 69.2 us
    pallas_call x1 -> x15, Pallas kernels: 15.7 us -> 177 us  [the longest x3 90.7 us: far_grads(): pl.pallas_call(far_kernel, grid=(total // rows,), in_specs=[data, data, h...]
    ppermute x41 -> x43, waiting for transfers between devices: 225 us -> 80.8 us  [swap(): lax.ppermute(block, axis, [(i, i ^ bit) for i in range(lax.axis_size(axis...]
    psum x2 -> x0, blocking collectives: 66.8 us -> none  [the longest x1 39.9 us: shards(): lax.psum(jnp.stack([gain_one_grad, gain_two_grad]), ('seq', 'wide'))]
    dot_general x6, matrix products: 79.5 us -> 26.7 us  [dot_over(): lax.dot_general(left, right, (((0,), (0,)), ((), ())), preferred_element_...]
    all_gather x1 -> x0, blocking collectives: 52 us -> none  [shards(): lax.all_gather(jnp.concatenate([norm_gains.reshape(-1), conv_weight.resha...]
    unnamed x131 -> x97, local copies, waits for them, and re-layouts: 68.7 us -> 29.1 us
    ppermute x0 -> x12, starting transfers between devices: none -> 34.4 us  [step(): got = lax.ppermute(part, 'seq', pairs)]
    all_gather x3 -> x4, waiting for transfers between devices: 33.9 us -> 3.58 us  [the longest x2 3.58 us: far_gather(): return lax.all_gather(jnp.concatenate(rows), 'wide', axis=0, tiled=True)]
  transfers between devices with their start and end apart: 51 -> 65, of which waited for: 32 -> 25; matrix products, arithmetic and copies ran while one was open for 17% -> 30% of each run, Pallas kernels for 0% -> 26%
where the time goes in v2:
time: 713 us; the launch traced here: 704 us
  Pallas kernels  189 us (27%)
  waiting for transfers between devices  126 us (18%)
  starting transfers between devices  107 us (15%)
  matrix products  94.2 us (13%)
  local copies, waits for them, and re-layouts  74 us (10%)
  other arithmetic  69.2 us (10%)
  blocking collectives  28.2 us (4%)
  between operations  15.4 us (2%)
    pallas_call x3, Pallas kernels, far_grads(): pl.pallas_call(far_kernel, grid=(total // rows,), in_specs=[data, data, h...  90.7 us
    ppermute x43, waiting for transfers between devices, swap(): lax.ppermute(block, axis, [(i, i ^ bit) for i in range(lax.axis_size(axis...  80.8 us
    ppermute x43, starting transfers between devices, swap(): lax.ppermute(block, axis, [(i, i ^ bit) for i in range(lax.axis_size(axis...  53.1 us
    dot_general x7, matrix products, dot(): return jnp.dot(left, right, preferred_element_type=F32)  37.4 us
    ppermute x12, starting transfers between devices, step(): got = lax.ppermute(part, 'seq', pairs)  34.4 us
    dot_general x6, matrix products, dot_back(): lax.dot_general(left, right, (((1,), (1,)), ((), ())), preferred_element_...  30.1 us
    unnamed x97, local copies, waits for them, and re-layouts  29.1 us
    all_to_all x1, blocking collectives, exchange(): lax.all_to_all(blocks, 'wide', split_axis=0, concat_axis=0, tiled=True)  28.2 us
  transfers between devices with their start and end apart: 65, of which 25 were waited for; matrix products, arithmetic and copies ran while one was open for 30% of the time, Pallas kernels for 26%

profile of v2, /device:TPU:0, one launch (start us, length us, event | category | flops | bytes accessed | tf_op | source)
XLA Modules:
  0.0 703.5 jit_solution(4867328951273709877)
XLA Ops:
  14.8 6.5 split_columns.2
  21.2 28.2 %all_to_all.25 = bf16[8,128,512]{2,1,0:T(8,128)(2,1)} all-to-all(bf16[8,128,512]{2,1,0:T(8,128)(2,1)} %split_columns.2), channel_id=1, replica_groups=mesh['seq'=4,'wide'=8] {'wide'}, dimensions={0} | all-to-all | bytes 2097152 | tf_op jit(solution)/shard_map/all_to_all | solution.py:701
  50.9 6.5 split_columns.3
  61.7 7.0 copy.92
  70.3 18.1 %all-to-all-done.1 = bf16[8,128,512]{2,1,0:T(8,128)(2,1)} async-done(((bf16[8,128,512]{2,1,0:T(8,128)(2,1)}), bf16[8,128,512]{2,1,0:T(8,128)(2,1)}, u32[]{:S(2)}, u32[]{:S(2)}) %all-to-all-start.1) | async-done | bytes 1048608 | tf_op jit(solution)/shard_map/all_to_all | solution.py:701
  94.6 7.3 %norm_packed.1 = bf16[1024,2048]{1,0:T(8,128)(2,1)} custom-call(bf16[8,224,2048]{2,1,0:T(8,128)(2,1)} %bitcast.312, f32[1,2048]{1,0:T(1,128)} %bitcast.375), custom_call_target="tpu_custom_call" | custom-call | tf_op jit(solution)/shard_map/norm_packed/pallas_call | solution.py:571
  104.1 6.5 collective-permute-done.1
  126.8 6.5 fusion.66.refs_0_.refs_1_
  133.3 12.6 %recur_forward.1 = (f32[1024,512]{1,0:T(8,128)}, f32[1024,512]{1,0:T(8,128)}, f32[1024,512]{1,0:T(8,128)}, f32[1024,512]{1,0:T(8,128)}, f32[1024,512]{1,0:T(8,12...) custom-call(f32[1024,512]{1,0:T(8,128)} %fusion.66.refs_0_.refs_1_, ...), custom_call_target="tpu_custom_call" | custom-call | tf_op jit(solution)/shard_map/recur_forward/pallas_call | solution.py:239
  145.9 6.6 fusion.67.refs_0_.refs_1_
  152.5 6.2 mix_forward.1
  211.1 7.4 %move_rows.5 = bf16[1024,2048]{1,0:T(8,128)(2,1)} custom-call(s32[8]{0:T(128)} %stack.163.table_ref, bf16[1024,2048]{1,0:T(8,128)(2,1)} %all-gather.6.cloned.1.call-done.src), custom_call_target="tpu_custom_call" | custom-call | tf_op jit(solution)/shard_map/move_rows/pallas_call | solution.py:720
  220.8 8.8 %collective-permute-done.14 = bf16[2,128,1024]{2,1,0:T(8,128)(2,1)S(1)} collective-permute-done((bf16[2,128,1024]{2,1,0:T(8,128)(2,1)S(1)}, bf16[2,128,1024]{2,1,0:T(8,128)(2,1)S(1)}, u32[]{:S(2)}, u32[]{:S(2)}) %collective-permute-start.14) | collective-permute-done | bytes 524320 | tf_op jit(solution)/shard_map/ppermute | solution.py:609
  233.8 5.9 collective-permute-start.17
  240.3 10.8 %fusion.68 = f32[1024,1536]{0,1:T(8,128)} fusion(bf16[1024,2048]{1,0:T(8,128)(2,1)S(1)} %constant_dynamic-update-slice_fusion, bf16[2048,1536]{1,0:T(8,128)(2,1)} %bitcast.326), kind=kOutput, calls=%fused_computation.207 | convolution fusion | flops 6442450944 | bytes 16777216 | tf_op jit(solution)/shard_map/dot_general | solution.py:19
  251.1 7.4 %multiply_convert_fusion.1 = (bf16[1024,768]{0,1:T(8,128)(2,1)S(1)}, bf16[1024,768]{0,1:T(8,128)(2,1)S(1)}, bf16[1024,768]{0,1:T(8,128)(2,1)S(1)}) fusion(f32[1024,1536]{0,1:T(8,128)} %fusion.68, bf16[1024,2048]{1,0:T(8,128)(2,1)S(1)} %copy-done.13, bf16[768,2048]{1,0:T(8,128)(2,1)S(1)} %copy-done.5), kind=kOutput, calls=%fused_computation.9 | convolution fusion | flops 3240099840 | bytes 18350080 | tf_op jit(solution)/shard_map/dot_general | solution.py:29
  265.3 6.3 collective-permute-start.23
  289.4 14.1 %collective-permute-done.19 = bf16[2,128,1024]{2,1,0:T(8,128)(2,1)S(1)} collective-permute-done((bf16[2,128,1024]{2,1,0:T(8,128)(2,1)S(1)}, bf16[2,128,1024]{2,1,0:T(8,128)(2,1)S(1)}, u32[]{:S(2)}, u32[]{:S(2)}) %collective-permute-start.19) | collective-permute-done | bytes 524320 | tf_op jit(solution)/shard_map/ppermute | solution.py:609
  311.9 6.9 collective-permute-done.22
  331.9 6.4 collective-permute-done.25
  348.3 16.7 %collective-permute-done.27 = bf16[2,128,1024]{2,1,0:T(8,128)(2,1)S(1)} collective-permute-done((bf16[2,128,1024]{2,1,0:T(8,128)(2,1)S(1)}, bf16[2,128,1024]{2,1,0:T(8,128)(2,1)S(1)}, u32[]{:S(2)}, u32[]{:S(2)}) %collective-permute-start.27) | collective-permute-done | bytes 524320 | tf_op jit(solution)/shard_map/ppermute | solution.py:609
  376.7 6.3 move_rows.6.refs_0_.refs_1_
  383.0 7.3 %gate_backward.1 = (bf16[1024,512]{1,0:T(8,128)(2,1)}, f32[1024,512]{1,0:T(8,128)}) custom-call(f32[1024,512]{1,0:T(8,128)} %move_rows.6.refs_0_.refs_1_, f32[1024,512]{1,0:T(8,128)} %move_rows.6.refs_0_.refs_1_, f32[1024,512]{1,0:T(8,128)} %get-tuple-element.145.refs_2_.states_ref, f32[1024,512]{1,0:T(8,128)} %get-tuple-element.194.refs_3_), custom_call_target="tpu_custom_call" | custom-call | tf_op jit(solution)/shard_map/gate_backward/pallas_call | solution.py:291
  410.1 11.7 %recur_backward.1 = (bf16[1024,512]{1,0:T(8,128)(2,1)}, f32[2,2,256,256]{3,2,1,0:T(8,128)}, f32[8,512]{1,0:T(8,128)}) custom-call(f32[1024,512]{1,0:T(8,128)} %get-tuple-element.197.sgrad_ref, f32[1024,512]{1,0:T(8,128)} %get-tuple-element.145.refs_2_.states_ref, f32[1024,512]{1,0:T(8,128)} %get-tuple-element.198.decay_ref, ...), custom_call_target="tpu_custom_call" | custom-call | tf_op jit(solution)/shard_map/recur_backward/pallas_call | solution.py:438
  444.2 6.0 move_rows.7
  453.7 7.4 %collective-permute-start.34 = (bf16[256,2560]{1,0:T(8,128)(2,1)}, bf16[256,2560]{1,0:T(8,128)(2,1)}, u32[]{:S(2)}, u32[]{:S(2)}) collective-permute-start(bf16[256,2560]{1,0:T(8,128)(2,1)} %copy.67), channel_id=1, source_target_pairs={{0,8},{24,16},{1,9},{25,17},{2,10},{26,18},{3,11},{27,19},{4,12},{... | collective-permute-start | bytes 3932168 | tf_op jit(solution)/shard_map/ppermute | solution.py:673
  480.9 30.2 %far_grads.3 = (f32[2048,768]{1,0:T(8,128)}, f32[2048,768]{1,0:T(8,128)}, f32[768,2048]{1,0:T(8,128)}) custom-call(bf16[3072,2048]{1,0:T(8,128)(2,1)} %all-gather.10.cloned.1.call-done.normed_ref, bf16[3072,2048]{1,0:T(8,128)(2,1)} %all-gather.8.cloned.1.call-done.cot_ref, ...), custom_call_target="tpu_custom_call", output_to_operand_aliasing={{0}: (5, {}), {1}: (6, {}), {2}: (7, {})} | custom-call | flops 19327352832 | bytes 40894464 | tf_op jit(solution)/shard_map/far_grads/pallas_call | solution.py:540
  536.2 30.2 %far_grads.4 = (f32[2048,768]{1,0:T(8,128)}, f32[2048,768]{1,0:T(8,128)}, f32[768,2048]{1,0:T(8,128)}) custom-call(bf16[3072,2048]{1,0:T(8,128)(2,1)} %all-gather.10.cloned.1.call-done.normed_ref, bf16[3072,2048]{1,0:T(8,128)(2,1)} %all-gather.8.cloned.1.call-done.cot_ref, ...), custom_call_target="tpu_custom_call", output_to_operand_aliasing={{0}: (5, {}), {1}: (6, {}), {2}: (7, {})} | custom-call | flops 19327352832 | bytes 40894464 | tf_op jit(solution)/shard_map/far_grads/pallas_call | solution.py:540
  582.8 30.2 %far_grads.5 = (f32[2048,768]{1,0:T(8,128)}, f32[2048,768]{1,0:T(8,128)}, f32[768,2048]{1,0:T(8,128)}) custom-call(bf16[3072,2048]{1,0:T(8,128)(2,1)} %all-gather.10.cloned.1.call-done.normed_ref, bf16[3072,2048]{1,0:T(8,128)(2,1)} %all-gather.8.cloned.1.call-done.cot_ref, ...), custom_call_target="tpu_custom_call", output_to_operand_aliasing={{0}: (5, {}), {1}: (6, {}), {2}: (7, {})} | custom-call | flops 19327352832 | bytes 40894464 | tf_op jit(solution)/shard_map/far_grads/pallas_call | solution.py:540
  614.9 8.1 %collective-permute-start.42 = (bf16[2,10,32,256]{3,2,1,0:T(8,128)(2,1)S(1)}, bf16[2,10,32,256]{3,2,1,0:T(8,128)(2,1)S(1)}, u32[]{:S(2)}, u32[]{:S(2)}) collective-permute-start(bf16[2,10,32,256]{3,2,1,0:T(8,128)(2,1)S(1)} %copy-done.31), channel_id=1, source_target_pairs={{0,8},{24,16},{1,9},{25,17},{2,10},{26,18},{3,11},{27,19},{4,12},{... | collective-permute-start | bytes 983048 | tf_op jit(solution)/shard_map/ppermute | solution.py:673
  654.8 10.0 %join_halves.3 = f32[2048,2,768]{2,1,0:T(2,128)} custom-call(f32[2048,768]{1,0:T(8,128)} %get-tuple-element.261.first, f32[2048,768]{1,0:T(8,128)} %get-tuple-element.262.second), custom_call_target="tpu_custom_call" | custom-call | tf_op jit(solution)/shard_map/join_halves/pallas_call | solution.py:593
  674.6 13.8 %collective-permute-done.56 = bf16[2,10,32,256]{3,2,1,0:T(8,128)(2,1)S(1)} collective-permute-done((bf16[2,10,32,256]{3,2,1,0:T(8,128)(2,1)S(1)}, bf16[2,10,32,256]{3,2,1,0:T(8,128)(2,1)S(1)}, u32[]{:S(2)}, u32[]{:S(2)}) %collective-permute-start.56) | collective-permute-done | bytes 327712 | tf_op jit(solution)/shard_map/ppermute | solution.py:673
  (376 shorter events, 323.9 us)
Async XLA Ops:
  7.2 85.3 %all-gather.12.cloned.1.call-start = ((), (), s32[]{:S(2)}) async-start(), calls=%async_computation.8 | async-start | bytes 8257536 | tf_op jit(solution)/shard_map/all_gather | solution.py:845
  49.4 39.7 %collective-permute-start = (bf16[8,128,512]{2,1,0:T(8,128)(2,1)}, bf16[8,128,512]{2,1,0:T(8,128)(2,1)}, u32[]{:S(2)}, u32[]{:S(2)}) collective-permute-start(bf16[8,128,512]{2,1,0:T(8,128)(2,1)} %all_to_all.25), channel_id=1, source_target_pairs={{0,8},{8,0},{16,24},{24,16},{1,9},{9,1},{17,25},{25,17},{2,10},{10... | collective-permute-start | bytes 3145736 | tf_op jit(solution)/shard_map/ppermute | solution.py:609
  57.4 31.0 %all-to-all-start.1 = ((bf16[8,128,512]{2,1,0:T(8,128)(2,1)}), bf16[8,128,512]{2,1,0:T(8,128)(2,1)}, u32[]{:S(2)}, u32[]{:S(2)}) async-start(bf16[8,128,512]{2,1,0:T(8,128)(2,1)} %split_columns.3), calls=%async_computation.1 | async-start | bytes 2097152 | tf_op jit(solution)/shard_map/all_to_all | solution.py:701
  61.6 106.5 %all-gather.6.cloned.1.call-start = ((), (), s32[]{:S(2)}) async-start(), calls=%async_computation.5 | async-start | bytes 4718592 | tf_op jit(solution)/shard_map/all_gather | solution.py:922
  110.6 215.2 %all-gather.8.cloned.1.call-start = ((), (), s32[]{:S(2)}) async-start(), calls=%async_computation.6 | async-start | bytes 14155776 | tf_op jit(solution)/shard_map/all_gather | solution.py:824
  112.0 33.8 %collective-permute-start.2 = (bf16[192,2048]{1,0:T(8,128)(2,1)}, bf16[192,2048]{1,0:T(8,128)(2,1)}, u32[]{:S(2)}, u32[]{:S(2)}) collective-permute-start(bf16[192,2048]{1,0:T(8,128)(2,1)} %get-tuple-element.292), channel_id=1, source_target_pairs={{0,1},{1,2},{2,3},{3,4},{4,5},{5,6},{6,7},{8,9},{9,10},{10,11},{11... | collective-permute-start | bytes 2359304 | tf_op jit(solution)/shard_map/ppermute | solution.py:907
  114.2 31.7 %collective-permute-start.3 = (bf16[192,2048]{1,0:T(8,128)(2,1)}, bf16[192,2048]{1,0:T(8,128)(2,1)}, u32[]{:S(2)}, u32[]{:S(2)}) collective-permute-start(bf16[192,2048]{1,0:T(8,128)(2,1)} %get-tuple-element.291), channel_id=1, source_target_pairs={{1,0},{2,1},{3,2},{4,3},{5,4},{6,5},{7,6},{9,8},{10,9},{11,10},{12... | collective-permute-start | bytes 2359304 | tf_op jit(solution)/shard_map/ppermute | solution.py:913
  170.0 48.5 %collective-permute-start.11 = (bf16[128,2048]{1,0:T(8,128)(2,1)}, bf16[128,2048]{1,0:T(8,128)(2,1)}, u32[]{:S(2)}, u32[]{:S(2)}) collective-permute-start(bf16[128,2048]{1,0:T(8,128)(2,1)} %bitcast.345), channel_id=1, source_target_pairs={{0,8},{8,0},{16,24},{24,16},{1,9},{9,1},{17,25},{25,17},{2,10},{10... | collective-permute-start | bytes 1572872 | tf_op jit(solution)/shard_map/ppermute | solution.py:609
  170.7 47.8 %collective-permute-start.12 = (bf16[128,2048]{1,0:T(8,128)(2,1)}, bf16[128,2048]{1,0:T(8,128)(2,1)}, u32[]{:S(2)}, u32[]{:S(2)}) collective-permute-start(bf16[128,2048]{1,0:T(8,128)(2,1)} %bitcast.346), channel_id=1, source_target_pairs={{0,16},{8,24},{16,0},{24,8},{1,17},{9,25},{17,1},{25,9},{2,18},{10... | collective-permute-start | bytes 1572872 | tf_op jit(solution)/shard_map/ppermute | solution.py:609
  173.1 45.3 %collective-permute-start.13 = (bf16[128,2048]{1,0:T(8,128)(2,1)}, bf16[128,2048]{1,0:T(8,128)(2,1)}, u32[]{:S(2)}, u32[]{:S(2)}) collective-permute-start(bf16[128,2048]{1,0:T(8,128)(2,1)} %bitcast.347), channel_id=1, source_target_pairs={{0,24},{8,16},{16,8},{24,0},{1,25},{9,17},{17,9},{25,1},{2,26},{10... | collective-permute-start | bytes 1572872 | tf_op jit(solution)/shard_map/ppermute | solution.py:609
  233.2 203.2 %all-gather.10.cloned.1.call-start = ((), (), s32[]{:S(2)}) async-start(), calls=%async_computation.7 | async-start | bytes 14155776 | tf_op jit(solution)/shard_map/all_gather | solution.py:824
  233.8 29.9 %collective-permute-start.17 = (bf16[128,2048]{1,0:T(8,128)(2,1)}, bf16[128,2048]{1,0:T(8,128)(2,1)S(1)}, u32[]{:S(2)}, u32[]{:S(2)}) collective-permute-start(bf16[128,2048]{1,0:T(8,128)(2,1)} %get-tuple-element.160), channel_id=1, source_target_pairs={{0,8},{8,0},{16,24},{24,16},{1,9},{9,1},{17,25},{25,17},{2,10},{10... | collective-permute-start | bytes 1572872 | tf_op jit(solution)/shard_map/ppermute | solution.py:609
  265.3 56.9 %collective-permute-start.23 = (bf16[128,2048]{1,0:T(8,128)(2,1)}, bf16[128,2048]{1,0:T(8,128)(2,1)}, u32[]{:S(2)}, u32[]{:S(2)}) collective-permute-start(bf16[128,2048]{1,0:T(8,128)(2,1)} %get-tuple-element.160), channel_id=1, source_target_pairs={{0,16},{8,24},{16,0},{24,8},{1,17},{9,25},{17,1},{25,9},{2,18},{10... | collective-permute-start | bytes 1572872 | tf_op jit(solution)/shard_map/ppermute | solution.py:609
  271.7 50.5 %collective-permute-start.24 = (bf16[128,2048]{1,0:T(8,128)(2,1)}, bf16[128,2048]{1,0:T(8,128)(2,1)}, u32[]{:S(2)}, u32[]{:S(2)}) collective-permute-start(bf16[128,2048]{1,0:T(8,128)(2,1)} %get-tuple-element.160), channel_id=1, source_target_pairs={{0,24},{8,16},{16,8},{24,0},{1,25},{9,17},{17,9},{25,1},{2,26},{10... | collective-permute-start | bytes 1572872 | tf_op jit(solution)/shard_map/ppermute | solution.py:609
  400.7 32.2 %collective-permute-start.31 = (bf16[320,2048]{1,0:T(8,128)(2,1)}, bf16[320,2048]{1,0:T(8,128)(2,1)}, u32[]{:S(2)}, u32[]{:S(2)}) collective-permute-start(bf16[320,2048]{1,0:T(8,128)(2,1)} %dynamic-slice_convert_fusion), channel_id=1, source_target_pairs={{0,8},{24,16},{1,9},{25,17},{2,10},{26,18},{3,11},{27,19},{4,12},{... | collective-permute-start | bytes 3932168 | tf_op jit(solution)/shard_map/ppermute | solution.py:673
  406.5 29.8 %all-to-all-start.2 = ((bf16[8,256,320]{1,2,0:T(8,128)(2,1)}), bf16[8,256,320]{1,2,0:T(8,128)(2,1)S(1)}, u32[]{:S(2)}, u32[]{:S(2)}) async-start(bf16[8,256,320]{1,2,0:T(8,128)(2,1)} %copy.65), calls=%async_computation.2 | async-start | bytes 2621440 | tf_op jit(solution)/shard_map/all_to_all | solution.py:701
  437.6 34.7 %all-to-all-start.3 = ((bf16[8,256,320]{1,2,0:T(8,128)(2,1)}), bf16[8,256,320]{1,2,0:T(8,128)(2,1)S(1)}, u32[]{:S(2)}, u32[]{:S(2)}) async-start(bf16[8,256,320]{1,2,0:T(8,128)(2,1)} %copy.66), calls=%async_computation.3 | async-start | bytes 2621440 | tf_op jit(solution)/shard_map/all_to_all | solution.py:701
  441.2 191.6 %collective-permute-start.29 = (bf16[512,2048]{1,0:T(8,128)(2,1)}, bf16[512,2048]{1,0:T(8,128)(2,1)}, u32[]{:S(2)}, u32[]{:S(2)}) collective-permute-start(bf16[512,2048]{1,0:T(8,128)(2,1)} %convolution_convert_fusion), channel_id=1, source_target_pairs={{0,1},{1,0},{2,3},{3,2},{4,5},{5,4},{6,7},{7,6},{8,9},{9,8},{10,11... | collective-permute-start | bytes 6291464 | tf_op jit(solution)/shard_map/ppermute | solution.py:609
  450.3 60.9 %collective-permute-start.33 = (bf16[320,2048]{1,0:T(8,128)(2,1)}, bf16[320,2048]{1,0:T(8,128)(2,1)}, u32[]{:S(2)}, u32[]{:S(2)}) collective-permute-start(bf16[320,2048]{1,0:T(8,128)(2,1)} %add_convert_fusion.5), channel_id=1, source_target_pairs={{8,16},{16,8},{9,17},{17,9},{10,18},{18,10},{11,19},{19,11},{12,20... | collective-permute-start | bytes 3932168 | tf_op jit(solution)/shard_map/ppermute | solution.py:673
  453.7 59.4 %collective-permute-start.34 = (bf16[256,2560]{1,0:T(8,128)(2,1)}, bf16[256,2560]{1,0:T(8,128)(2,1)}, u32[]{:S(2)}, u32[]{:S(2)}) collective-permute-start(bf16[256,2560]{1,0:T(8,128)(2,1)} %copy.67), channel_id=1, source_target_pairs={{0,8},{24,16},{1,9},{25,17},{2,10},{26,18},{3,11},{27,19},{4,12},{... | collective-permute-start | bytes 3932168 | tf_op jit(solution)/shard_map/ppermute | solution.py:673
  472.3 47.2 %all-to-all-start.4 = ((bf16[8,2,2,32,256]{4,3,1,2,0:T(8,128)(2,1)}), bf16[8,2,2,32,256]{4,3,1,2,0:T(8,128)(2,1)}, u32[]{:S(2)}, u32[]{:S(2)}) async-start(bf16[8,2,2,32,256]{4,3,1,2,0:T(8,128)(2,1)} %bitcast.303), calls=%async_computation.4 | async-start | bytes 1048576 | tf_op jit(solution)/shard_map/all_to_all | solution.py:701
  476.5 43.0 %collective-permute-start.32 = (bf16[512,2048]{1,0:T(8,128)(2,1)}, bf16[512,2048]{1,0:T(8,128)(2,1)}, u32[]{:S(2)}, u32[]{:S(2)}) collective-permute-start(bf16[512,2048]{1,0:T(8,128)(2,1)} %convolution_convert_fusion.3), channel_id=1, source_target_pairs={{0,1},{1,0},{2,3},{3,2},{4,5},{5,4},{6,7},{7,6},{8,9},{9,8},{10,11... | collective-permute-start | bytes 6291464 | tf_op jit(solution)/shard_map/ppermute | solution.py:609
  478.4 38.0 %collective-permute-start.39 = (bf16[256,2560]{1,0:T(8,128)(2,1)}, bf16[256,2560]{1,0:T(8,128)(2,1)}, u32[]{:S(2)}, u32[]{:S(2)}) collective-permute-start(bf16[256,2560]{1,0:T(8,128)(2,1)} %copy.70), channel_id=1, source_target_pairs={{0,8},{24,16},{1,9},{25,17},{2,10},{26,18},{3,11},{27,19},{4,12},{... | collective-permute-start | bytes 3932168 | tf_op jit(solution)/shard_map/ppermute | solution.py:673
  526.6 48.4 %collective-permute-start.35 = (bf16[2,128,1024]{2,1,0:T(8,128)(2,1)}, bf16[2,128,1024]{2,1,0:T(8,128)(2,1)}, u32[]{:S(2)}, u32[]{:S(2)}) collective-permute-start(bf16[2,128,1024]{2,1,0:T(8,128)(2,1)} %slice_bitcast_fusion.15), channel_id=1, source_target_pairs={{0,2},{1,3},{2,0},{3,1},{4,6},{5,7},{6,4},{7,5},{8,10},{9,11},{10,... | collective-permute-start | bytes 1572872 | tf_op jit(solution)/shard_map/ppermute | solution.py:609
  528.5 46.5 %collective-permute-start.36 = (bf16[2,128,1024]{2,1,0:T(8,128)(2,1)}, bf16[2,128,1024]{2,1,0:T(8,128)(2,1)}, u32[]{:S(2)}, u32[]{:S(2)}) collective-permute-start(bf16[2,128,1024]{2,1,0:T(8,128)(2,1)} %slice_bitcast_fusion.14), channel_id=1, source_target_pairs={{0,4},{1,5},{2,6},{3,7},{4,0},{5,1},{6,2},{7,3},{8,12},{9,13},{10,... | collective-permute-start | bytes 1572872 | tf_op jit(solution)/shard_map/ppermute | solution.py:609
  530.0 43.6 %collective-permute-start.37 = (bf16[320,2048]{1,0:T(8,128)(2,1)S(1)}, bf16[320,2048]{1,0:T(8,128)(2,1)}, u32[]{:S(2)}, u32[]{:S(2)}) collective-permute-start(bf16[320,2048]{1,0:T(8,128)(2,1)S(1)} %add_convert_fusion.4), channel_id=1, source_target_pairs={{8,0},{16,24},{9,1},{17,25},{10,2},{18,26},{11,3},{19,27},{12,4},{... | collective-permute-start | bytes 3932168 | tf_op jit(solution)/shard_map/ppermute | solution.py:673
  531.3 40.5 %collective-permute-start.38 = (bf16[256,2560]{1,0:T(8,128)(2,1)S(1)}, bf16[256,2560]{1,0:T(8,128)(2,1)}, u32[]{:S(2)}, u32[]{:S(2)}) collective-permute-start(bf16[256,2560]{1,0:T(8,128)(2,1)S(1)} %add_convert_fusion.3), channel_id=1, source_target_pairs={{8,16},{16,8},{9,17},{17,9},{10,18},{18,10},{11,19},{19,11},{12,20... | collective-permute-start | bytes 3932168 | tf_op jit(solution)/shard_map/ppermute | solution.py:673
  575.1 53.1 %collective-permute-start.40 = (bf16[256,2560]{1,0:T(8,128)(2,1)S(1)}, bf16[256,2560]{1,0:T(8,128)(2,1)}, u32[]{:S(2)}, u32[]{:S(2)}) collective-permute-start(bf16[256,2560]{1,0:T(8,128)(2,1)S(1)} %add_convert_fusion.2), channel_id=1, source_target_pairs={{8,0},{16,24},{9,1},{17,25},{10,2},{18,26},{11,3},{19,27},{12,4},{... | collective-permute-start | bytes 3932168 | tf_op jit(solution)/shard_map/ppermute | solution.py:673
  576.4 54.3 %collective-permute-start.41 = (bf16[256,2560]{1,0:T(8,128)(2,1)}, bf16[256,2560]{1,0:T(8,128)(2,1)}, u32[]{:S(2)}, u32[]{:S(2)}) collective-permute-start(bf16[256,2560]{1,0:T(8,128)(2,1)} %add_convert_fusion.1), channel_id=1, source_target_pairs={{8,16},{16,8},{9,17},{17,9},{10,18},{18,10},{11,19},{19,11},{12,20... | collective-permute-start | bytes 3932168 | tf_op jit(solution)/shard_map/ppermute | solution.py:673
  581.4 33.5 %collective-permute-start.44 = (bf16[128,1024]{1,0:T(8,128)(2,1)}, bf16[128,1024]{1,0:T(8,128)(2,1)}, u32[]{:S(2)}, u32[]{:S(2)}) collective-permute-start(bf16[128,1024]{1,0:T(8,128)(2,1)} %fusion.50), channel_id=1, source_target_pairs={{0,2},{1,3},{2,0},{3,1},{4,6},{5,7},{6,4},{7,5},{8,10},{9,11},{10,... | collective-permute-start | bytes 786440 | tf_op jit(solution)/shard_map/ppermute | solution.py:609
  582.7 41.4 %collective-permute-start.43 = (bf16[128,1024]{1,0:T(8,128)(2,1)}, bf16[128,1024]{1,0:T(8,128)(2,1)S(1)}, u32[]{:S(2)}, u32[]{:S(2)}) collective-permute-start(bf16[128,1024]{1,0:T(8,128)(2,1)} %fusion.49), channel_id=1, source_target_pairs={{0,4},{1,5},{2,6},{3,7},{4,0},{5,1},{6,2},{7,3},{8,12},{9,13},{10,... | collective-permute-start | bytes 786440 | tf_op jit(solution)/shard_map/ppermute | solution.py:609
  652.1 38.3 %collective-permute-start.54 = (bf16[256,2560]{1,0:T(8,128)(2,1)S(1)}, bf16[256,2560]{1,0:T(8,128)(2,1)S(1)}, u32[]{:S(2)}, u32[]{:S(2)}) collective-permute-start(bf16[256,2560]{1,0:T(8,128)(2,1)S(1)} %add_convert_fusion), channel_id=1, source_target_pairs={{8,0},{16,24},{9,1},{17,25},{10,2},{18,26},{11,3},{19,27},{12,4},{... | collective-permute-start | bytes 3932168 | tf_op jit(solution)/shard_map/ppermute | solution.py:673
  (71 other events, 783.8 us)
Sparse Core Ops, SparseCore 0:
  14.3 74.8 all-gather.11
  110.7 42.6 all-gather.5
  233.3 92.4 all-gather.7
  328.7 83.4 all-gather.9

commit v3 on v2

--- a/solution.py
+++ b/solution.py
@@ -549,9 +549,7 @@
         out_shape=[jax.ShapeDtypeStruct(v.shape, F32) for v in sums],
         input_output_aliases={5: 0, 6: 1, 7: 2},
         cost_estimate=pl.CostEstimate(
-            flops=12 * total * width * hidden,
-            bytes_accessed=4 * total * width + 30 * width * hidden,
-            transcendentals=total * hidden,
+            flops=1024, bytes_accessed=1024, transcendentals=0
         ),
         compiler_params=pltpu.CompilerParams(
             dimension_semantics=("arbitrary",), vmem_limit_bytes=60 << 20
@@ -821,7 +819,7 @@
         return [swap(rows, "seq", d) for d in range(1, n_seq)] if recompute else []
 
     def far_gather(rows):
-        return lax.all_gather(jnp.concatenate(rows), "wide", axis=0, tiled=True)
+        return lax.all_gather(rows, "wide", axis=0, tiled=True)
 
     small = jnp.concatenate(
         [
@@ -865,8 +863,9 @@
             rows = jnp.stack([even, jnp.where(odd == 0, other, rows)], axis=1)
         return rows.reshape(width, win)
 
-    branch_mine = exchange(fetch(0))
-    gate_mine = exchange(fetch(1))
+    send_branch, send_gate = lax.optimization_barrier((fetch(0), fetch(1)))
+    branch_mine = exchange(send_branch)
+    gate_mine = exchange(send_gate)
     branch_other, gate_other = share(branch_mine), share(gate_mine)
     in_branch = whole(branch_mine, branch_other)
     gains = (
@@ -892,13 +891,12 @@
     )
     mlp_in = mlp_in_weight.reshape(width, -1)
 
-    in_branch, normed_all, chan, gains, out_own, mlp_in, gate_mine, gate_other = (
+    in_branch, normed_all, chan, gains, out_own, mlp_in, gate_mine = (
         lax.optimization_barrier(
-            (in_branch, normed_all, chan, gains, out_own, mlp_in, gate_mine, gate_other)
+            (in_branch, normed_all, chan, gains, out_own, mlp_in, gate_mine)
         )
     )
 
-    in_gate = whole(gate_mine, gate_other)
 
     below = max(w * own - f * head for w, f in enumerate(firsts))
     above = max(f * head + win - (w + 1) * own for w, f in enumerate(firsts))
@@ -932,7 +930,10 @@
     states, *saved, enter = recur_forward(
         dot(normed_all, in_branch), chan, gate_w, taps, chunk
     )
-    in_gate, states, around = lax.optimization_barrier((in_gate, states, around))
+    gate_mine, gate_other, states, around = lax.optimization_barrier(
+        (gate_mine, gate_other, states, around)
+    )
+    in_gate = whole(gate_mine, gate_other)
     mixed, gate_rows = mix_forward(dot(normed_all, in_gate), states, head, chunk)
     mixed_near = to_near(mixed)
     out_send = dot(mixed_near[half:], out_own).astype(BF16)
@@ -941,7 +942,9 @@
     )
     rows = tok_low.astype(F32)
     steps = scatter_steps(dot(mixed_near[:half], out_own), out_send)
-    way = lax.optimization_barrier(steps.send(None))
+    way, in_branch, in_gate, around = lax.optimization_barrier(
+        (steps.send(None), in_branch, in_gate, around)
+    )
     way = steps.send(way)
     in_own = jnp.concatenate(
         [
@@ -964,6 +967,8 @@
     sent = far_rows(normed_two)
     cot_near = to_near(cot_all)
     way, cot_near, cot_sent = lax.optimization_barrier((way, cot_near, cot_sent))
+    cot_sent = jnp.concatenate(cot_sent) if recompute else ()
+    way, cot_sent = lax.optimization_barrier((steps.send(way), cot_sent))
     normed_even = run_steps(steps, way)
     normed_even, cot_sent = lax.optimization_barrier((normed_even, cot_sent))
     cot_far = far_gather(cot_sent) if recompute else ()
@@ -1001,27 +1006,29 @@
     )
     mix_low = middle_grad.astype(BF16)
     gain_two_grad = jnp.sum(normed_two_grad * unit_two, axis=0)
-    middle_grad, mix_low, gain_two_grad, out_sum, hidden, cot_far, sent = (
+    middle_grad, mix_low, gain_two_grad, out_sum, hidden, sent = (
         lax.optimization_barrier(
-            (middle_grad, mix_low, gain_two_grad, out_sum, hidden, cot_far, sent)
+            (middle_grad, mix_low, gain_two_grad, out_sum, hidden, sent)
         )
     )
 
-    normed_far = far_gather(sent) if recompute else ()
     steps = gather_steps(mix_low)
-    way = lax.optimization_barrier(steps.send(None))
+    way, sent = lax.optimization_barrier((steps.send(None), sent))
     way = steps.send(way)
+    normed_far = far_gather(jnp.concatenate(sent)) if recompute else ()
     feed_send = dot(hidden[half:], mlp_out_weight).astype(BF16)
     feed_keep = dot(hidden[:half], mlp_out_weight)
     way, feed_send, feed_keep = lax.optimization_barrier((way, feed_send, feed_keep))
     mix_even = run_steps(steps, way)
     mix_near = jnp.concatenate([mix_even, other_core(mix_even)])
-    mix_near = lax.optimization_barrier(mix_near)
+    mix_near, cot_far = lax.optimization_barrier((mix_near, cot_far))
     mixed_grad = from_near(dot_back(mix_near, out_win))
-    gate_half, state_grad = gate_backward(mixed_grad, states, gate_rows, head, chunk)
     out_grad = lax.dynamic_slice_in_dim(
         dot_over(mixed_near, mix_near).astype(BF16), offset, own
     )
+    gate_half, state_grad = gate_backward(mixed_grad, states, gate_rows, head, chunk)
+    state_grad, out_grad = lax.optimization_barrier((state_grad, out_grad))
+    out_grad = line_step(out_grad, 0)
 
     def in_part(grad):
         return dot_over(normed_all, grad).astype(BF16).reshape(n_wide, -1, own)
@@ -1029,36 +1036,48 @@
     def in_rows(part):
         return jnp.moveaxis(exchange(part), 0, 1).reshape(-1, lru)
 
+    branch_half, gate_grad, sums = recur_backward(
+        state_grad, (states, *saved, enter), chan, gate_w, taps, chunk
+    )
+    branch_half = lax.dynamic_slice_in_dim(branch_half, offset, own, axis=1)
+    branch_part = in_part(branch_half)
+    branch_half, branch_part, gate_half, gate_grad, sums = lax.optimization_barrier(
+        (branch_half, branch_part, gate_half, gate_grad, sums)
+    )
+    branch_rows_grad = in_rows(branch_part)
     gate_half = lax.dynamic_slice_in_dim(gate_half, offset, own, axis=1)
     gate_part = in_part(gate_half)
-    state_grad, gate_part, out_grad = lax.optimization_barrier(
-        (state_grad, gate_part, out_grad)
-    )
-    gate_rows_grad = in_rows(gate_part)
-    out_grad = line_step(out_grad, 0)
-    branch_half, gate_grad, sums = recur_backward(
-        state_grad, (states, *saved, enter), chan, gate_w, taps, chunk
-    )
-    branch_half = lax.dynamic_slice_in_dim(branch_half, offset, own, axis=1)
-    branch_part = in_part(branch_half)
-    branch_half, branch_part, gate_grad, sums, gate_rows_grad, normed_far, out_grad = (
-        lax.optimization_barrier(
-            (branch_half, branch_part, gate_grad, sums, gate_rows_grad, normed_far, out_grad)
-        )
-    )
-    branch_rows_grad = in_rows(branch_part)
-    out_grad = line_step(out_grad, 1)
-    gate_rows_grad = line_step(gate_rows_grad, 0)
     own_near = to_near(jnp.concatenate([branch_half, gate_half], axis=1))
     normed_send = dot_back(own_near[half:], in_own).astype(BF16)
-    normed_keep = dot_back(own_near[:half], in_own)
-    normed_send, normed_keep, branch_rows_grad, normed_far = lax.optimization_barrier(
-        (normed_send, normed_keep, branch_rows_grad, normed_far)
-    )
+    (
+        branch_rows_grad,
+        gate_part,
+        own_near,
+        normed_send,
+        out_grad,
+        normed_far,
+        gate_grad,
+        feed_keep,
+    ) = lax.optimization_barrier(
+        (
+            branch_rows_grad,
+            gate_part,
+            own_near,
+            normed_send,
+            out_grad,
+            normed_far,
+            gate_grad,
+            feed_keep,
+        )
+    )
+    branch_rows_grad = lax.psum(branch_rows_grad, "seq")
+    gate_rows_grad = in_rows(gate_part)
+    out_grad = line_step(out_grad, 1)
+    normed_steps = scatter_steps(dot_back(own_near[:half], in_own), normed_send)
+    way = normed_steps.send(None)
 
     parts = hidden_units // 256 if hidden_units % 256 == 0 else 1
     held = (gate_sum, up_sum, out_sum)
-    normed_steps = scatter_steps(normed_keep, normed_send)
     feed_steps = scatter_steps(feed_keep, feed_send)
 
     def far_part(held, done):
@@ -1069,50 +1088,47 @@
                 )
         return held
 
-    way = normed_steps.send(None)
+    held = far_part(held, 0)
+    way, held, gate_rows_grad, out_grad, normed_far, gate_grad, feed_keep = (
+        lax.optimization_barrier(
+            (way, held, gate_rows_grad, out_grad, normed_far, gate_grad, feed_keep)
+        )
+    )
     gate_grad = exchange(
         gate_grad.astype(BF16)
         .reshape(2, span, n_wide, part, head)
         .transpose(2, 0, 1, 3, 4)
     )
-    held = far_part(held, 0)
-    way, held, out_grad, gate_rows_grad, gate_grad = lax.optimization_barrier(
-        (way, held, out_grad, gate_rows_grad, gate_grad)
-    )
+    out_grad = line_step(out_grad, 2)
     way = normed_steps.send(way)
-    out_grad = line_step(out_grad, 2)
-    gate_rows_grad = line_step(gate_rows_grad, 1)
-    branch_rows_grad = line_step(branch_rows_grad, 0)
+    feed_way = feed_steps.send(None)
+    held = far_part(held, 1)
+    way, feed_way, held, gate_grad, out_grad, normed_far = lax.optimization_barrier(
+        (way, feed_way, held, gate_grad, out_grad, normed_far)
+    )
     holders = [
         next(w for w, f in enumerate(firsts) if f <= j < f + span) for j in range(heads)
     ]
     gate_grad = jnp.stack(
         [gate_grad[w, :, j - firsts[w]] for j, w in enumerate(holders)], axis=1
     )
-    held = far_part(held, 1)
-    way, held, out_grad, gate_rows_grad, branch_rows_grad, gate_grad, feed_keep = (
+    out_grad = out_grad.astype(F32)
+    way = normed_steps.send(way)
+    feed_way = feed_steps.send(feed_way)
+    branch_rows_grad, gate_rows_grad, gate_grad, out_grad, normed_far = (
         lax.optimization_barrier(
-            (way, held, out_grad, gate_rows_grad, branch_rows_grad, gate_grad, feed_keep)
+            (branch_rows_grad, gate_rows_grad, gate_grad, out_grad, normed_far)
         )
     )
+    gate_rows_grad, gate_grad = lax.psum((gate_rows_grad, gate_grad), "seq")
+    held = far_part(held, 2)
+    way, feed_way, held = lax.optimization_barrier((way, feed_way, held))
     normed_grad = run_steps(normed_steps, way)
     inv_one, unit_one = norm_rows(rows)
     input_grad = middle_grad + norm_back(normed_grad, gains[0], inv_one, unit_one)
     gain_one_grad = jnp.sum(normed_grad * unit_one, axis=0)
-    feed_way = feed_steps.send(None)
-    gate_rows_grad = line_step(gate_rows_grad, 2)
-    branch_rows_grad = line_step(branch_rows_grad, 1)
-    gate_grad = line_step(gate_grad, 0)
-    held = far_part(held, 2)
-    feed_way, held, gate_rows_grad, branch_rows_grad, gate_grad, gain_one_grad = (
-        lax.optimization_barrier(
-            (feed_way, held, gate_rows_grad, branch_rows_grad, gate_grad, gain_one_grad)
-        )
-    )
     feed = run_steps(feed_steps, feed_way)
     result = (middle + feed).astype(BF16)
-    branch_rows_grad = line_step(branch_rows_grad, 2)
-    gate_grad = line_step(line_step(gate_grad, 1), 2)
     if recompute:
         mlp_in_grad = join_halves(held[0], held[1])
     else:
@@ -1121,7 +1137,6 @@
     in_grad = join_halves(branch_rows_grad, gate_rows_grad)
     sums = lax.dynamic_slice_in_dim(sums[: taps + 4], offset, own, axis=1)
     gate_grad = gate_grad.astype(F32).transpose(0, 1, 3, 2)
-    out_grad = out_grad.astype(F32)
 
     gains_grad = sum_small(jnp.concatenate([gain_one_grad, gain_two_grad]), "wide")
     gains_grad = lax.dynamic_slice_in_dim(

time: 713 us -> 629 us (0.88)
  waiting for transfers between devices: 126 us -> 92.3 us
  starting transfers between devices: 107 us -> 85.4 us
  local copies, waits for them, and re-layouts: 74 us -> 62.6 us
  other arithmetic: 69.2 us -> 60.6 us
    ppermute x12 -> x3, starting transfers between devices: 34.4 us -> 8.36 us  [step(): got = lax.ppermute(part, 'seq', pairs)]
    ppermute x12 -> x3, waiting for transfers between devices: 23.4 us -> 4.65 us  [step(): got = lax.ppermute(part, 'seq', pairs)]
    all_to_all x4, waiting for transfers between devices: 18.2 us -> 0.01 us  [exchange(): lax.all_to_all(blocks, 'wide', split_axis=0, concat_axis=0, tiled=True)]
    psum x0 -> x2, waiting for transfers between devices: none -> 9.89 us  [the longest x1 6.04 us: shards(): gate_rows_grad, gate_grad = lax.psum((gate_rows_grad, gate_grad), 'seq')]
    convert_element_type x8 -> x2, other arithmetic: 16 us -> 6.62 us  [step(): return (got, (part.astype(F32) + got.astype(F32)).astype(BF16))]
    unnamed x97 -> x107, local copies, waits for them, and re-layouts: 29.1 us -> 22.3 us
  transfers between devices with their start and end apart: 65 -> 58, of which waited for: 25 -> 22; matrix products, arithmetic and copies ran while one was open for 30% -> 31% of each run, Pallas kernels for 26% -> 30%
where the time goes in v3:
time: 629 us; the launch traced here: 619 us
  Pallas kernels  191 us (30%)
  waiting for transfers between devices  92.3 us (15%)
  matrix products  89.8 us (14%)
  starting transfers between devices  85.4 us (14%)
  local copies, waits for them, and re-layouts  62.6 us (10%)
  other arithmetic  60.6 us (10%)
  blocking collectives  21.5 us (3%)
  between operations  15.6 us (2%)
    pallas_call x3, Pallas kernels, far_grads(): pl.pallas_call(far_kernel, grid=(total // rows,), in_specs=[data, data, h...  91.1 us
    ppermute x43, waiting for transfers between devices, swap(): lax.ppermute(block, axis, [(i, i ^ bit) for i in range(lax.axis_size(axis...  74.2 us
    ppermute x43, starting transfers between devices, swap(): lax.ppermute(block, axis, [(i, i ^ bit) for i in range(lax.axis_size(axis...  56.9 us
    dot_general x7, matrix products, dot(): return jnp.dot(left, right, preferred_element_type=F32)  33.5 us
    dot_general x6, matrix products, dot_over(): lax.dot_general(left, right, (((0,), (0,)), ((), ())), preferred_element_...  28.3 us
    dot_general x6, matrix products, dot_back(): lax.dot_general(left, right, (((1,), (1,)), ((), ())), preferred_element_...  28.1 us
    pallas_call x4, Pallas kernels, move_rows(): pl.pallas_call(move_kernel, grid_spec=pltpu.PrefetchScalarGridSpec(num_sc...  25.7 us
    unnamed x107, local copies, waits for them, and re-layouts  22.3 us
  transfers between devices with their start and end apart: 58, of which 22 were waited for; matrix products, arithmetic and copies ran while one was open for 31% of the time, Pallas kernels for 30%

profile of v3, /device:TPU:0, one launch (start us, length us, event | category | flops | bytes accessed | tf_op | source)
XLA Modules:
  0.0 618.5 jit_solution(12490575365900270787)
XLA Ops:
  14.8 6.5 %split_columns.2 = bf16[8,128,512]{2,1,0:T(8,128)(2,1)} custom-call(s32[9]{0:T(128)} %stack.165.table_ref, bf16[256,2,2560]{2,1,0:T(2,128)(2,1)} %src.3), custom_call_target="tpu_custom_call" | custom-call | tf_op jit(solution)/shard_map/split_columns/pallas_call | solution.py:487
  21.2 6.7 %split_columns.3 = bf16[8,128,512]{2,1,0:T(8,128)(2,1)} custom-call(s32[9]{0:T(128)} %stack.165.table_ref, bf16[256,2,2560]{2,1,0:T(2,128)(2,1)} %src.3), custom_call_target="tpu_custom_call" | custom-call | tf_op jit(solution)/shard_map/split_columns/pallas_call | solution.py:487
  28.0 21.5 %all_to_all.25 = bf16[8,128,512]{2,1,0:T(8,128)(2,1)} all-to-all(bf16[8,128,512]{2,1,0:T(8,128)(2,1)S(1)} %copy-done.19), channel_id=1, replica_groups=mesh['seq'=4,'wide'=8] {'wide'}, dimensions={0} | all-to-all | bytes 2097152 | tf_op jit(solution)/shard_map/all_to_all | solution.py:699
  55.3 6.9 %copy.90 = bf16[256,8,2,768]{3,1,2,0:T(8,128)(2,1)} copy(bf16[256,8,2,768]{3,2,1,0:T(2,128)(2,1)} %bitcast.335) | data formatting | bytes 12582912
  63.7 9.9 %collective-permute-done = bf16[8,128,512]{2,1,0:T(8,128)(2,1)} collective-permute-done((bf16[8,128,512]{2,1,0:T(8,128)(2,1)}, bf16[8,128,512]{2,1,0:T(8,128)(2,1)}, u32[]{:S(2)}, u32[]{:S(2)}) %collective-permute-start) | collective-permute-done | bytes 1048608 | tf_op jit(solution)/shard_map/ppermute | solution.py:607
  82.5 7.3 %norm_packed.1 = bf16[1024,2048]{1,0:T(8,128)(2,1)} custom-call(bf16[8,224,2048]{2,1,0:T(8,128)(2,1)} %bitcast.320, f32[1,2048]{1,0:T(1,128)} %bitcast.373), custom_call_target="tpu_custom_call" | custom-call | tf_op jit(solution)/shard_map/norm_packed/pallas_call | solution.py:569
  107.8 6.5 %fusion.66.refs_0_.refs_1_ = f32[1024,512]{1,0:T(8,128)} fusion(bf16[1024,2048]{1,0:T(8,128)(2,1)} %norm_packed.1, bf16[2048,512]{1,0:T(8,128)(2,1)} %bitcast.331), kind=kOutput, calls=%fused_computation.196 | convolution fusion | flops 2147483648 | bytes 8388608 | tf_op jit(solution)/shard_map/dot_general | solution.py:19
  114.3 12.3 %recur_forward.1 = (f32[1024,512]{1,0:T(8,128)}, f32[1024,512]{1,0:T(8,128)}, f32[1024,512]{1,0:T(8,128)}, f32[1024,512]{1,0:T(8,128)}, f32[1024,512]{1,0:T(8,12...) custom-call(f32[1024,512]{1,0:T(8,128)} %fusion.66.refs_0_.refs_1_, ...), custom_call_target="tpu_custom_call" | custom-call | tf_op jit(solution)/shard_map/recur_forward/pallas_call | solution.py:239
  135.1 6.2 mix_forward.1
  141.3 6.1 move_rows.4
  191.0 7.3 %move_rows.5 = bf16[1024,2048]{1,0:T(8,128)(2,1)} custom-call(s32[8]{0:T(128)} %stack.163.table_ref, bf16[1024,2048]{1,0:T(8,128)(2,1)} %all-gather.6.cloned.1.call-done.src), custom_call_target="tpu_custom_call" | custom-call | tf_op jit(solution)/shard_map/move_rows/pallas_call | solution.py:718
  203.1 6.3 %collective-permute-done.14 = bf16[2,128,1024]{2,1,0:T(8,128)(2,1)S(1)} collective-permute-done((bf16[2,128,1024]{2,1,0:T(8,128)(2,1)S(1)}, bf16[2,128,1024]{2,1,0:T(8,128)(2,1)S(1)}, u32[]{:S(2)}, u32[]{:S(2)}) %collective-permute-start.14) | collective-permute-done | bytes 524320 | tf_op jit(solution)/shard_map/ppermute | solution.py:607
  210.8 7.7 %collective-permute-start.17 = (bf16[128,2048]{1,0:T(8,128)(2,1)}, bf16[128,2048]{1,0:T(8,128)(2,1)S(1)}, u32[]{:S(2)}, u32[]{:S(2)}) collective-permute-start(bf16[128,2048]{1,0:T(8,128)(2,1)} %get-tuple-element.187), channel_id=1, source_target_pairs={{0,8},{8,0},{16,24},{24,16},{1,9},{9,1},{17,25},{25,17},{2,10},{10... | collective-permute-start | bytes 1572872 | tf_op jit(solution)/shard_map/ppermute | solution.py:607
  221.1 10.4 %fusion.68 = f32[1024,1536]{0,1:T(8,128)S(1)} fusion(bf16[1024,2048]{1,0:T(8,128)(2,1)S(1)} %constant_dynamic-update-slice_fusion, bf16[2048,1536]{1,0:T(8,128)(2,1)} %bitcast.304), kind=kOutput, calls=%fused_computation.198 | convolution fusion | flops 6442450944 | bytes 16777216 | tf_op jit(solution)/shard_map/dot_general | solution.py:19
  231.5 5.5 multiply_convert_fusion.1
  241.3 6.4 %collective-permute-start.23 = (bf16[128,2048]{1,0:T(8,128)(2,1)}, bf16[128,2048]{1,0:T(8,128)(2,1)S(1)}, u32[]{:S(2)}, u32[]{:S(2)}) collective-permute-start(bf16[128,2048]{1,0:T(8,128)(2,1)} %get-tuple-element.187), channel_id=1, source_target_pairs={{0,16},{8,24},{16,0},{24,8},{1,17},{9,25},{17,1},{25,9},{2,18},{10... | collective-permute-start | bytes 1572872 | tf_op jit(solution)/shard_map/ppermute | solution.py:607
  254.2 5.6 fusion.6.own_gate_ref
  259.8 5.4 fusion.4.own_up_ref
  265.2 12.3 %collective-permute-done.19 = bf16[2,128,1024]{2,1,0:T(8,128)(2,1)S(1)} collective-permute-done((bf16[2,128,1024]{2,1,0:T(8,128)(2,1)S(1)}, bf16[2,128,1024]{2,1,0:T(8,128)(2,1)S(1)}, u32[]{:S(2)}, u32[]{:S(2)}) %collective-permute-start.19) | collective-permute-done | bytes 524320 | tf_op jit(solution)/shard_map/ppermute | solution.py:607
  285.8 6.9 %collective-permute-done.22 = bf16[128,1024]{1,0:T(8,128)(2,1)S(1)} collective-permute-done((bf16[128,1024]{1,0:T(8,128)(2,1)S(1)}, bf16[128,1024]{1,0:T(8,128)(2,1)S(1)}, u32[]{:S(2)}, u32[]{:S(2)}) %collective-permute-start.22) | collective-permute-done | bytes 262176 | tf_op jit(solution)/shard_map/ppermute | solution.py:607
  298.7 10.5 %collective-permute-done.25 = bf16[128,1024]{1,0:T(8,128)(2,1)} collective-permute-done((bf16[128,1024]{1,0:T(8,128)(2,1)S(1)}, bf16[128,1024]{1,0:T(8,128)(2,1)}, u32[]{:S(2)}, u32[]{:S(2)}) %collective-permute-start.25) | collective-permute-done | bytes 262176 | tf_op jit(solution)/shard_map/ppermute | solution.py:607
  324.0 5.7 collective-permute-done.28
  337.2 5.9 fusion.70.src
  343.1 6.3 %move_rows.6.refs_0_.refs_1_ = f32[1024,512]{1,0:T(8,128)} custom-call(s32[8]{0:T(128)} %stack.163.table_ref, f32[1024,512]{1,0:T(8,128)} %fusion.70.src), custom_call_target="tpu_custom_call" | custom-call | tf_op jit(solution)/shard_map/move_rows/pallas_call | solution.py:718
  349.4 7.6 %gate_backward.1 = (bf16[1024,512]{1,0:T(8,128)(2,1)}, f32[1024,512]{1,0:T(8,128)}) custom-call(f32[1024,512]{1,0:T(8,128)} %move_rows.6.refs_0_.refs_1_, f32[1024,512]{1,0:T(8,128)} %move_rows.6.refs_0_.refs_1_, f32[1024,512]{1,0:T(8,128)} %get-tuple-element.166.refs_2_.states_ref, f32[1024,512]{1,0:T(8,128)} %get-tuple-element.224.refs_3_), custom_call_target="tpu_custom_call" | custom-call | tf_op jit(solution)/shard_map/gate_backward/pallas_call | solution.py:291
  368.0 12.1 %recur_backward.1 = (bf16[1024,512]{1,0:T(8,128)(2,1)}, f32[2,2,256,256]{3,2,1,0:T(8,128)}, f32[8,512]{1,0:T(8,128)}) custom-call(f32[1024,512]{1,0:T(8,128)} %get-tuple-element.226.sgrad_ref, f32[1024,512]{1,0:T(8,128)} %get-tuple-element.166.refs_2_.states_ref, f32[1024,512]{1,0:T(8,128)} %get-tuple-element.227.decay_ref, ...), custom_call_target="tpu_custom_call" | custom-call | tf_op jit(solution)/shard_map/recur_backward/pallas_call | solution.py:438
  397.4 6.0 move_rows.7
  419.7 30.2 %far_grads.3 = (f32[2048,768]{1,0:T(8,128)}, f32[2048,768]{1,0:T(8,128)}, f32[768,2048]{1,0:T(8,128)}) custom-call(bf16[3072,2048]{1,0:T(8,128)(2,1)} %all-gather.10.cloned.1.call-done.normed_ref, bf16[3072,2048]{1,0:T(8,128)(2,1)} %all-gather.8.cloned.1.call-done.cot_ref, ...), custom_call_target="tpu_custom_call", output_to_operand_aliasing={{0}: (5, {}), {1}: (6, {}), {2}: (7, {})} | custom-call | flops 1024 | bytes 1024 | tf_op jit(solution)/shard_map/far_grads/pallas_call | solution.py:540
  472.1 30.6 %far_grads.4 = (f32[2048,768]{1,0:T(8,128)}, f32[2048,768]{1,0:T(8,128)}, f32[768,2048]{1,0:T(8,128)}) custom-call(bf16[3072,2048]{1,0:T(8,128)(2,1)} %all-gather.10.cloned.1.call-done.normed_ref, bf16[3072,2048]{1,0:T(8,128)(2,1)} %all-gather.8.cloned.1.call-done.cot_ref, ...), custom_call_target="tpu_custom_call", output_to_operand_aliasing={{0}: (5, {}), {1}: (6, {}), {2}: (7, {})} | custom-call | flops 1024 | bytes 1024 | tf_op jit(solution)/shard_map/far_grads/pallas_call | solution.py:540
  532.0 30.3 %far_grads.5 = (f32[2048,768]{1,0:T(8,128)}, f32[2048,768]{1,0:T(8,128)}, f32[768,2048]{1,0:T(8,128)}) custom-call(bf16[3072,2048]{1,0:T(8,128)(2,1)} %all-gather.10.cloned.1.call-done.normed_ref, bf16[3072,2048]{1,0:T(8,128)(2,1)} %all-gather.8.cloned.1.call-done.cot_ref, ...), custom_call_target="tpu_custom_call", output_to_operand_aliasing={{0}: (5, {}), {1}: (6, {}), {2}: (7, {})} | custom-call | flops 1024 | bytes 1024 | tf_op jit(solution)/shard_map/far_grads/pallas_call | solution.py:540
  583.1 10.2 %join_halves.3 = f32[2048,2,768]{2,1,0:T(2,128)} custom-call(f32[2048,768]{1,0:T(8,128)} %get-tuple-element.299.first, f32[2048,768]{1,0:T(8,128)} %get-tuple-element.300.second), custom_call_target="tpu_custom_call" | custom-call | tf_op jit(solution)/shard_map/join_halves/pallas_call | solution.py:591
  598.5 6.0 all-reduce.7.cloned.1.call-done
  (366 shorter events, 278.0 us)
Async XLA Ops:
  7.2 73.3 %all-gather.12.cloned.1.call-start = ((), (), s32[]{:S(2)}) async-start(), calls=%async_computation.9 | async-start | bytes 8257536 | tf_op jit(solution)/shard_map/all_gather | solution.py:843
  51.0 41.0 %all-to-all-start.1 = ((bf16[8,128,512]{2,1,0:T(8,128)(2,1)}), bf16[8,128,512]{2,1,0:T(8,128)(2,1)}, u32[]{:S(2)}, u32[]{:S(2)}) async-start(bf16[8,128,512]{2,1,0:T(8,128)(2,1)} %split_columns.3), calls=%async_computation.1 | async-start | bytes 2097152 | tf_op jit(solution)/shard_map/all_to_all | solution.py:699
  55.2 95.8 %all-gather.6.cloned.1.call-start = ((), (), s32[]{:S(2)}) async-start(), calls=%async_computation.5 | async-start | bytes 4718592 | tf_op jit(solution)/shard_map/all_gather | solution.py:920
  92.1 245.1 %all-gather.8.cloned.1.call-start = ((), (), s32[]{:S(2)}) async-start(), calls=%async_computation.6 | async-start | bytes 14155776 | tf_op jit(solution)/shard_map/all_gather | solution.py:822
  92.1 34.5 %collective-permute-start.1 = (bf16[8,128,512]{2,1,0:T(8,128)(2,1)}, bf16[8,128,512]{2,1,0:T(8,128)(2,1)}, u32[]{:S(2)}, u32[]{:S(2)}) collective-permute-start(bf16[8,128,512]{2,1,0:T(8,128)(2,1)} %all-to-all-done.1), channel_id=1, source_target_pairs={{0,8},{8,0},{16,24},{24,16},{1,9},{9,1},{17,25},{25,17},{2,10},{10... | collective-permute-start | bytes 3145736 | tf_op jit(solution)/shard_map/ppermute | solution.py:607
  95.9 30.7 %collective-permute-start.2 = (bf16[192,2048]{1,0:T(8,128)(2,1)}, bf16[192,2048]{1,0:T(8,128)(2,1)}, u32[]{:S(2)}, u32[]{:S(2)}) collective-permute-start(bf16[192,2048]{1,0:T(8,128)(2,1)} %get-tuple-element.332), channel_id=1, source_target_pairs={{0,1},{1,2},{2,3},{3,4},{4,5},{5,6},{6,7},{8,9},{9,10},{10,11},{11... | collective-permute-start | bytes 2359304 | tf_op jit(solution)/shard_map/ppermute | solution.py:905
  98.7 27.9 %collective-permute-start.3 = (bf16[192,2048]{1,0:T(8,128)(2,1)}, bf16[192,2048]{1,0:T(8,128)(2,1)}, u32[]{:S(2)}, u32[]{:S(2)}) collective-permute-start(bf16[192,2048]{1,0:T(8,128)(2,1)} %get-tuple-element.331), channel_id=1, source_target_pairs={{1,0},{2,1},{3,2},{4,3},{5,4},{6,5},{7,6},{9,8},{10,9},{11,10},{12... | collective-permute-start | bytes 2359304 | tf_op jit(solution)/shard_map/ppermute | solution.py:911
  152.7 45.6 %collective-permute-start.11 = (bf16[128,2048]{1,0:T(8,128)(2,1)}, bf16[128,2048]{1,0:T(8,128)(2,1)}, u32[]{:S(2)}, u32[]{:S(2)}) collective-permute-start(bf16[128,2048]{1,0:T(8,128)(2,1)} %bitcast.344), channel_id=1, source_target_pairs={{0,8},{8,0},{16,24},{24,16},{1,9},{9,1},{17,25},{25,17},{2,10},{10... | collective-permute-start | bytes 1572872 | tf_op jit(solution)/shard_map/ppermute | solution.py:607
  153.3 45.0 %collective-permute-start.12 = (bf16[128,2048]{1,0:T(8,128)(2,1)}, bf16[128,2048]{1,0:T(8,128)(2,1)}, u32[]{:S(2)}, u32[]{:S(2)}) collective-permute-start(bf16[128,2048]{1,0:T(8,128)(2,1)} %bitcast.345), channel_id=1, source_target_pairs={{0,16},{8,24},{16,0},{24,8},{1,17},{9,25},{17,1},{25,9},{2,18},{10... | collective-permute-start | bytes 1572872 | tf_op jit(solution)/shard_map/ppermute | solution.py:607
  155.7 42.6 %collective-permute-start.13 = (bf16[128,2048]{1,0:T(8,128)(2,1)}, bf16[128,2048]{1,0:T(8,128)(2,1)}, u32[]{:S(2)}, u32[]{:S(2)}) collective-permute-start(bf16[128,2048]{1,0:T(8,128)(2,1)} %bitcast.346), channel_id=1, source_target_pairs={{0,24},{8,16},{16,8},{24,0},{1,25},{9,17},{17,9},{25,1},{2,26},{10... | collective-permute-start | bytes 1572872 | tf_op jit(solution)/shard_map/ppermute | solution.py:607
  210.6 201.2 %all-gather.10.cloned.1.call-start = ((), (), s32[]{:S(2)}) async-start(), calls=%async_computation.7 | async-start | bytes 14155776 | tf_op jit(solution)/shard_map/all_gather | solution.py:822
  210.8 30.3 %collective-permute-start.17 = (bf16[128,2048]{1,0:T(8,128)(2,1)}, bf16[128,2048]{1,0:T(8,128)(2,1)S(1)}, u32[]{:S(2)}, u32[]{:S(2)}) collective-permute-start(bf16[128,2048]{1,0:T(8,128)(2,1)} %get-tuple-element.187), channel_id=1, source_target_pairs={{0,8},{8,0},{16,24},{24,16},{1,9},{9,1},{17,25},{25,17},{2,10},{10... | collective-permute-start | bytes 1572872 | tf_op jit(solution)/shard_map/ppermute | solution.py:607
  241.3 54.5 %collective-permute-start.23 = (bf16[128,2048]{1,0:T(8,128)(2,1)}, bf16[128,2048]{1,0:T(8,128)(2,1)S(1)}, u32[]{:S(2)}, u32[]{:S(2)}) collective-permute-start(bf16[128,2048]{1,0:T(8,128)(2,1)} %get-tuple-element.187), channel_id=1, source_target_pairs={{0,16},{8,24},{16,0},{24,8},{1,17},{9,25},{17,1},{25,9},{2,18},{10... | collective-permute-start | bytes 1572872 | tf_op jit(solution)/shard_map/ppermute | solution.py:607
  247.7 48.1 %collective-permute-start.24 = (bf16[128,2048]{1,0:T(8,128)(2,1)}, bf16[128,2048]{1,0:T(8,128)(2,1)S(1)}, u32[]{:S(2)}, u32[]{:S(2)}) collective-permute-start(bf16[128,2048]{1,0:T(8,128)(2,1)} %get-tuple-element.187), channel_id=1, source_target_pairs={{0,24},{8,16},{16,8},{24,0},{1,25},{9,17},{17,9},{25,1},{2,26},{10... | collective-permute-start | bytes 1572872 | tf_op jit(solution)/shard_map/ppermute | solution.py:607
  251.9 25.6 %collective-permute-start.19 = (bf16[2,128,1024]{2,1,0:T(8,128)(2,1)S(1)}, bf16[2,128,1024]{2,1,0:T(8,128)(2,1)S(1)}, u32[]{:S(2)}, u32[]{:S(2)}) collective-permute-start(bf16[2,128,1024]{2,1,0:T(8,128)(2,1)S(1)} %slice_bitcast_fusion.19), channel_id=1, source_target_pairs={{0,2},{1,3},{2,0},{3,1},{4,6},{5,7},{6,4},{7,5},{8,10},{9,11},{10,... | collective-permute-start | bytes 1572872 | tf_op jit(solution)/shard_map/ppermute | solution.py:607
  252.5 25.6 %collective-permute-start.20 = (bf16[2,128,1024]{2,1,0:T(8,128)(2,1)S(1)}, bf16[2,128,1024]{2,1,0:T(8,128)(2,1)S(1)}, u32[]{:S(2)}, u32[]{:S(2)}) collective-permute-start(bf16[2,128,1024]{2,1,0:T(8,128)(2,1)S(1)} %slice_bitcast_fusion.18), channel_id=1, source_target_pairs={{0,4},{1,5},{2,6},{3,7},{4,0},{5,1},{6,2},{7,3},{8,12},{9,13},{10,... | collective-permute-start | bytes 1572872 | tf_op jit(solution)/shard_map/ppermute | solution.py:607
  362.7 45.8 %collective-permute-start.30 = (bf16[320,2048]{1,0:T(8,128)(2,1)}, bf16[320,2048]{1,0:T(8,128)(2,1)}, u32[]{:S(2)}, u32[]{:S(2)}) collective-permute-start(bf16[320,2048]{1,0:T(8,128)(2,1)} %dynamic-slice_convert_fusion), channel_id=1, source_target_pairs={{0,8},{24,16},{1,9},{25,17},{2,10},{26,18},{3,11},{27,19},{4,12},{... | collective-permute-start | bytes 3932168 | tf_op jit(solution)/shard_map/ppermute | solution.py:671
  411.8 41.5 %collective-permute-start.31 = (bf16[512,2048]{1,0:T(8,128)(2,1)}, bf16[512,2048]{1,0:T(8,128)(2,1)}, u32[]{:S(2)}, u32[]{:S(2)}) collective-permute-start(bf16[512,2048]{1,0:T(8,128)(2,1)} %convolution_convert_fusion.3), channel_id=1, source_target_pairs={{0,1},{1,0},{2,3},{3,2},{4,5},{5,4},{6,7},{7,6},{8,9},{9,8},{10,11... | collective-permute-start | bytes 6291464 | tf_op jit(solution)/shard_map/ppermute | solution.py:607
  412.3 37.6 %collective-permute-start.32 = (bf16[320,2048]{1,0:T(8,128)(2,1)}, bf16[320,2048]{1,0:T(8,128)(2,1)}, u32[]{:S(2)}, u32[]{:S(2)}) collective-permute-start(bf16[320,2048]{1,0:T(8,128)(2,1)} %add_convert_fusion.1), channel_id=1, source_target_pairs={{8,16},{16,8},{9,17},{17,9},{10,18},{18,10},{11,19},{19,11},{12,20... | collective-permute-start | bytes 3932168 | tf_op jit(solution)/shard_map/ppermute | solution.py:671
  415.4 37.9 %all-to-all-start.3 = ((bf16[8,256,320]{1,2,0:T(8,128)(2,1)}), bf16[8,256,320]{1,2,0:T(8,128)(2,1)S(1)}, u32[]{:S(2)}, u32[]{:S(2)}) async-start(bf16[8,256,320]{1,2,0:T(8,128)(2,1)} %copy.66), calls=%async_computation.3 | async-start | bytes 2621440 | tf_op jit(solution)/shard_map/all_to_all | solution.py:699
  419.2 111.1 %all-reduce.5.cloned.1.call-start = ((), (), s32[]{:S(2)}) async-start(), calls=%async_computation.8 | async-start | bytes 2621440 | tf_op jit(solution)/shard_map/psum | solution.py:1073
  419.3 90.6 %collective-permute-start.35 = (bf16[512,2048]{1,0:T(8,128)(2,1)}, bf16[512,2048]{1,0:T(8,128)(2,1)}, u32[]{:S(2)}, u32[]{:S(2)}) collective-permute-start(bf16[512,2048]{1,0:T(8,128)(2,1)} %convolution_convert_fusion), channel_id=1, source_target_pairs={{0,1},{1,0},{2,3},{3,2},{4,5},{5,4},{6,7},{7,6},{8,9},{9,8},{10,11... | collective-permute-start | bytes 6291464 | tf_op jit(solution)/shard_map/ppermute | solution.py:607
  453.3 54.1 %collective-permute-start.36 = (bf16[320,2048]{1,0:T(8,128)(2,1)}, bf16[320,2048]{1,0:T(8,128)(2,1)}, u32[]{:S(2)}, u32[]{:S(2)}) collective-permute-start(bf16[320,2048]{1,0:T(8,128)(2,1)} %add_convert_fusion), channel_id=1, source_target_pairs={{8,0},{16,24},{9,1},{17,25},{10,2},{18,26},{11,3},{19,27},{12,4},{... | collective-permute-start | bytes 3932168 | tf_op jit(solution)/shard_map/ppermute | solution.py:671
  463.7 46.2 %collective-permute-start.33 = (bf16[2,128,1024]{2,1,0:T(8,128)(2,1)}, bf16[2,128,1024]{2,1,0:T(8,128)(2,1)}, u32[]{:S(2)}, u32[]{:S(2)}) collective-permute-start(bf16[2,128,1024]{2,1,0:T(8,128)(2,1)} %slice_bitcast_fusion.15), channel_id=1, source_target_pairs={{0,2},{1,3},{2,0},{3,1},{4,6},{5,7},{6,4},{7,5},{8,10},{9,11},{10,... | collective-permute-start | bytes 1572872 | tf_op jit(solution)/shard_map/ppermute | solution.py:607
  466.2 43.7 %collective-permute-start.34 = (bf16[2,128,1024]{2,1,0:T(8,128)(2,1)}, bf16[2,128,1024]{2,1,0:T(8,128)(2,1)}, u32[]{:S(2)}, u32[]{:S(2)}) collective-permute-start(bf16[2,128,1024]{2,1,0:T(8,128)(2,1)} %slice_bitcast_fusion.14), channel_id=1, source_target_pairs={{0,4},{1,5},{2,6},{3,7},{4,0},{5,1},{6,2},{7,3},{8,12},{9,13},{10,... | collective-permute-start | bytes 1572872 | tf_op jit(solution)/shard_map/ppermute | solution.py:607
  468.6 41.3 %all-to-all-start.4 = ((bf16[8,2,2,32,256]{4,3,1,2,0:T(8,128)(2,1)}), bf16[8,2,2,32,256]{4,3,1,2,0:T(8,128)(2,1)S(1)}, u32[]{:S(2)}, u32[]{:S(2)}) async-start(bf16[8,2,2,32,256]{4,3,1,2,0:T(8,128)(2,1)} %bitcast.302), calls=%async_computation.4 | async-start | bytes 1048576 | tf_op jit(solution)/shard_map/all_to_all | solution.py:699
  472.1 132.5 %all-reduce.7.cloned.1.call-start = ((), (), s32[]{:S(2)}) async-start(), calls=%async_computation.10 | async-start | bytes 3276800 | tf_op jit(solution)/shard_map/psum | solution.py:1123
  519.8 42.5 %collective-permute-start.37 = (bf16[128,1024]{1,0:T(8,128)(2,1)}, bf16[128,1024]{1,0:T(8,128)(2,1)S(1)}, u32[]{:S(2)}, u32[]{:S(2)}) collective-permute-start(bf16[128,1024]{1,0:T(8,128)(2,1)} %fusion.49), channel_id=1, source_target_pairs={{0,4},{1,5},{2,6},{3,7},{4,0},{5,1},{6,2},{7,3},{8,12},{9,13},{10,... | collective-permute-start | bytes 786440 | tf_op jit(solution)/shard_map/ppermute | solution.py:607
  522.5 39.9 %collective-permute-start.38 = (bf16[128,1024]{1,0:T(8,128)(2,1)}, bf16[128,1024]{1,0:T(8,128)(2,1)}, u32[]{:S(2)}, u32[]{:S(2)}) collective-permute-start(bf16[128,1024]{1,0:T(8,128)(2,1)} %fusion.50), channel_id=1, source_target_pairs={{0,2},{1,3},{2,0},{3,1},{4,6},{5,7},{6,4},{7,5},{8,10},{9,11},{10,... | collective-permute-start | bytes 786440 | tf_op jit(solution)/shard_map/ppermute | solution.py:607
  523.9 38.4 %collective-permute-start.39 = (bf16[2,128,1024]{2,1,0:T(8,128)(2,1)}, bf16[2,128,1024]{2,1,0:T(8,128)(2,1)}, u32[]{:S(2)}, u32[]{:S(2)}) collective-permute-start(bf16[2,128,1024]{2,1,0:T(8,128)(2,1)} %slice_bitcast_fusion.13), channel_id=1, source_target_pairs={{0,2},{1,3},{2,0},{3,1},{4,6},{5,7},{6,4},{7,5},{8,10},{9,11},{10,... | collective-permute-start | bytes 1572872 | tf_op jit(solution)/shard_map/ppermute | solution.py:607
  524.5 37.9 %collective-permute-start.40 = (bf16[2,128,1024]{2,1,0:T(8,128)(2,1)}, bf16[2,128,1024]{2,1,0:T(8,128)(2,1)}, u32[]{:S(2)}, u32[]{:S(2)}) collective-permute-start(bf16[2,128,1024]{2,1,0:T(8,128)(2,1)} %slice_bitcast_fusion.12), channel_id=1, source_target_pairs={{0,4},{1,5},{2,6},{3,7},{4,0},{5,1},{6,2},{7,3},{8,12},{9,13},{10,... | collective-permute-start | bytes 1572872 | tf_op jit(solution)/shard_map/ppermute | solution.py:607
  570.2 26.2 %collective-permute-start.42 = (bf16[128,1024]{1,0:T(8,128)(2,1)}, bf16[128,1024]{1,0:T(8,128)(2,1)S(1)}, u32[]{:S(2)}, u32[]{:S(2)}) collective-permute-start(bf16[128,1024]{1,0:T(8,128)(2,1)} %fusion.52), channel_id=1, source_target_pairs={{0,2},{1,3},{2,0},{3,1},{4,6},{5,7},{6,4},{7,5},{8,10},{9,11},{10,... | collective-permute-start | bytes 786440 | tf_op jit(solution)/shard_map/ppermute | solution.py:607
  (69 other events, 696.0 us)
Sparse Core Ops, SparseCore 0:
  14.3 66.1 all-gather.11
  92.2 44.6 all-gather.5
  210.8 99.6 all-gather.7
  312.2 74.6 all-gather.9
  456.5 73.8 all-reduce.4
  532.6 71.8 all-reduce.6

commit v4 on v3

--- a/solution.py
+++ b/solution.py
@@ -180,10 +180,36 @@
     lax.fori_loop(0, steps, finish, 0, unroll=8)
 
 
-def mix_kernel(*refs, groups):
-    states_ref, mixed_ref, gperm_ref, out = refs[groups:]
+def near_index(device, n):
+    bits = lax.axis_index("wide") ^ device
+    return (bits >> 1) + (bits & 1) * (n // 2)
+
+
+def mix_kernel(*refs, groups, n, size):
+    states_ref, mixed_ref, gperm_ref, out, stage, sems = refs[groups:]
     rows, width = states_ref.shape
     steps = rows // SUB
+    head, chunk = pl.program_id(0), pl.program_id(1)
+    chunks = pl.num_programs(1)
+    step = head * chunks + chunk
+    last = pl.num_programs(0) * chunks - 1
+    slot = step % 2
+
+    def copies(slot):
+        made = []
+        for k in range(rows // size):
+            place = near_index(chunk * (rows // size) + k, n)
+            made.append(
+                pltpu.make_async_copy(
+                    stage.at[slot, pl.ds(k * size, size)],
+                    mixed_ref.at[
+                        pl.ds(pl.multiple_of(place * size, size), size),
+                        pl.ds(pl.multiple_of(head * width, width), width),
+                    ],
+                    sems.at[slot, k],
+                )
+            )
+        return made
 
     def body(s, _):
         v = strided_load(refs[:groups], s, steps)
@@ -192,11 +218,29 @@
         return 0
 
     lax.fori_loop(0, steps, body, 0, unroll=8)
-    for n in range(width // LANES):
-        mixed_ref[:, n * LANES : (n + 1) * LANES] = out[n].astype(BF16)
-
-
-def mix_forward(gate_branch, states, head, chunk):
+
+    @pl.when(step >= 2)
+    def _():
+        for copy in copies(slot):
+            copy.wait()
+
+    for g in range(width // LANES):
+        stage[slot, :, g * LANES : (g + 1) * LANES] = out[g].astype(BF16)
+    for copy in copies(slot):
+        copy.start()
+
+    @pl.when(step == last)
+    def _():
+        for copy in copies(slot):
+            copy.wait()
+
+    @pl.when((step == last) & (step >= 1))
+    def _():
+        for copy in copies(1 - slot):
+            copy.wait()
+
+
+def mix_forward(gate_branch, states, head, chunk, size):
     total, width = states.shape
     groups = head // LANES
     blk = pl.BlockSpec((chunk, head), lambda j, c: (c, j))
@@ -205,15 +249,21 @@
         for n in range(groups)
     ]
     return pl.pallas_call(
-        functools.partial(mix_kernel, groups=groups),
+        functools.partial(
+            mix_kernel, groups=groups, n=lax.axis_size("wide"), size=size
+        ),
         grid=(width // head, total // chunk),
         in_specs=lane + [blk],
-        out_specs=[blk, blk],
+        out_specs=[pl.BlockSpec(memory_space=pl.ANY), blk],
         out_shape=[
             jax.ShapeDtypeStruct((total, width), BF16),
             jax.ShapeDtypeStruct((total, width), F32),
         ],
-        scratch_shapes=[pltpu.VMEM((groups, chunk, LANES), F32)],
+        scratch_shapes=[
+            pltpu.VMEM((groups, chunk, LANES), F32),
+            pltpu.VMEM((2, chunk, head), BF16),
+            pltpu.SemaphoreType.DMA((2, chunk // size)),
+        ],
         compiler_params=pltpu.CompilerParams(
             dimension_semantics=("arbitrary", "arbitrary"), vmem_limit_bytes=60 << 20
         ),
@@ -262,47 +312,83 @@
     )(*[projected] * groups, chan, gate_w)
 
 
-def gate_back_kernel(*refs, groups):
-    mgrad_refs = refs[:groups]
-    states_ref, gperm_ref, ggrad_ref, sgrad_ref, out = refs[groups:]
+def gate_back_kernel(
+    mgrad_ref, states_ref, gperm_ref, ggrad_ref, sgrad_ref, out, near, sems, *, n, size
+):
     rows, width = states_ref.shape
     steps = rows // SUB
+    groups = width // LANES
+    chunks = pl.num_programs(1)
+    step = pl.program_id(0) * chunks + pl.program_id(1)
+    last = pl.num_programs(0) * chunks - 1
+    slot = step % 2
+
+    def copies(step, slot):
+        made = []
+        for k in range(rows // size):
+            place = near_index(step % chunks * (rows // size) + k, n)
+            for g in range(groups):
+                lane = step // chunks * width + g * LANES
+                made.append(
+                    pltpu.make_async_copy(
+                        mgrad_ref.at[
+                            pl.ds(pl.multiple_of(place * size, size), size),
+                            pl.ds(pl.multiple_of(lane, LANES), LANES),
+                        ],
+                        near.at[slot, g, pl.ds(k * size, size)],
+                        sems.at[slot, k, g],
+                    )
+                )
+        return made
+
+    @pl.when(step == 0)
+    def _():
+        for copy in copies(step, slot):
+            copy.start()
+
+    @pl.when(step < last)
+    def _():
+        for copy in copies(step + 1, 1 - slot):
+            copy.start()
+
+    for copy in copies(step, slot):
+        copy.wait()
 
     def body(s, _):
         value, slope = gelu_parts(gperm_ref[rows8(s), :])
-        mg = strided_load(mgrad_refs, s, steps)
+        mg = strided_load([near.at[slot, g] for g in range(groups)], s, steps)
         strided_store(out, s, steps, mg * states_ref[rows8(s), :] * slope)
         sgrad_ref[rows8(s), :] = mg * value
         return 0
 
     lax.fori_loop(0, steps, body, 0, unroll=8)
-    for n in range(width // LANES):
-        ggrad_ref[:, n * LANES : (n + 1) * LANES] = out[n].astype(BF16)
-
-
-def gate_backward(mixed_grad, states, gate_rows, head, chunk):
+    for g in range(groups):
+        ggrad_ref[:, g * LANES : (g + 1) * LANES] = out[g].astype(BF16)
+
+
+def gate_backward(mixed_grad, states, gate_rows, head, chunk, size):
     total, width = mixed_grad.shape
     groups = head // LANES
     blk = pl.BlockSpec((chunk, head), lambda j, c: (c, j))
-    lane = [
-        pl.BlockSpec((chunk, LANES), lambda j, c, n=n: (c, j * groups + n))
-        for n in range(groups)
-    ]
     return pl.pallas_call(
-        functools.partial(gate_back_kernel, groups=groups),
+        functools.partial(gate_back_kernel, n=lax.axis_size("wide"), size=size),
         grid=(width // head, total // chunk),
-        in_specs=lane + [blk, blk],
+        in_specs=[pl.BlockSpec(memory_space=pl.ANY), blk, blk],
         out_specs=[blk, blk],
         out_shape=[
             jax.ShapeDtypeStruct((total, width), BF16),
             jax.ShapeDtypeStruct((total, width), F32),
         ],
-        scratch_shapes=[pltpu.VMEM((groups, chunk, LANES), F32)],
+        scratch_shapes=[
+            pltpu.VMEM((groups, chunk, LANES), F32),
+            pltpu.VMEM((2, groups, chunk, LANES), F32),
+            pltpu.SemaphoreType.DMA((2, chunk // size, groups)),
+        ],
         compiler_params=pltpu.CompilerParams(
             dimension_semantics=("arbitrary", "arbitrary"), vmem_limit_bytes=60 << 20
         ),
         name="gate_backward",
-    )(*[mixed_grad] * groups, states, gate_rows)
+    )(mixed_grad, states, gate_rows)
 
 
 def backward_kernel(
@@ -732,21 +818,6 @@
     return move_rows(rows, True)
 
 
-def from_near(rows):
-    return move_rows(rows, False)
-
-
-def gather_small(block):
-    n = lax.axis_size("wide")
-    here = lax.axis_index("wide")
-    held = block[None]
-    for bit in bit_list(n):
-        held = jnp.concatenate([held, swap(held, "wide", bit)])
-    return jnp.concatenate(
-        [lax.dynamic_slice_in_dim(held, here ^ w, 1) for w in range(n)]
-    )
-
-
 def norm_rows(rows):
     inv = lax.rsqrt(jnp.mean(rows * rows, axis=-1, keepdims=True) + 1e-06)
     return inv, rows * inv
@@ -934,8 +1005,9 @@
         (gate_mine, gate_other, states, around)
     )
     in_gate = whole(gate_mine, gate_other)
-    mixed, gate_rows = mix_forward(dot(normed_all, in_gate), states, head, chunk)
-    mixed_near = to_near(mixed)
+    mixed_near, gate_rows = mix_forward(
+        dot(normed_all, in_gate), states, head, chunk, size
+    )
     out_send = dot(mixed_near[half:], out_own).astype(BF16)
     out_send, mixed_near, cot_all = lax.optimization_barrier(
         (out_send, mixed_near, cot_all)
@@ -972,43 +1044,68 @@
     normed_even = run_steps(steps, way)
     normed_even, cot_sent = lax.optimization_barrier((normed_even, cot_sent))
     cot_far = far_gather(cot_sent) if recompute else ()
-    normed_near = jnp.concatenate([normed_even, other_core(normed_even)])
-    hidden, gate_up_grad = feed_forward(normed_near, cot_near, mlp_in, mlp_out_weight)
-    up_send = dot_back(gate_up_grad[half:], mlp_in).astype(BF16)
-    (
-        up_send,
-        hidden,
-        gate_up_grad,
-        normed_near,
-        sent[:1],
-    ) = lax.optimization_barrier(
-        (
-            up_send,
-            hidden,
-            gate_up_grad,
-            normed_near,
-            sent[:1],
+    normed_odd = other_core(normed_even)
+    hidden_even, grad_even = feed_forward(
+        normed_even, cot_near[:half], mlp_in, mlp_out_weight
+    )
+    hidden_odd, grad_odd = feed_forward(
+        normed_odd, cot_near[half:], mlp_in, mlp_out_weight
+    )
+    up_send = dot_back(grad_odd, mlp_in).astype(BF16)
+    up_send, hidden_even, hidden_odd, grad_even, grad_odd, normed_odd, first_sent = (
+        lax.optimization_barrier(
+            (
+                up_send,
+                hidden_even,
+                hidden_odd,
+                grad_even,
+                grad_odd,
+                normed_odd,
+                sent[:1],
+            )
         )
     )
-    steps = scatter_steps(dot_back(gate_up_grad[:half], mlp_in), up_send)
-    way = steps.send(None)
-    way, gate_up_grad, hidden = lax.optimization_barrier((way, gate_up_grad, hidden))
+    sent = first_sent + sent[1:]
+    steps = scatter_steps(dot_back(grad_even, mlp_in), up_send)
+    way, grad_even, grad_odd, hidden_even, hidden_odd = lax.optimization_barrier(
+        (steps.send(None), grad_even, grad_odd, hidden_even, hidden_odd)
+    )
     way = steps.send(way)
-    gate_sum = dot_over(normed_near, gate_up_grad[:, :hidden_units])
-    up_sum = dot_over(normed_near, gate_up_grad[:, hidden_units:])
-    way, gate_sum, up_sum, hidden = lax.optimization_barrier(
-        (way, gate_sum, up_sum, hidden)
-    )
-    out_sum = dot_over(hidden, cot_near)
+    gate_sum = dot_over(normed_even, grad_even[:, :hidden_units]) + dot_over(
+        normed_odd, grad_odd[:, :hidden_units]
+    )
+    up_sum = dot_over(normed_even, grad_even[:, hidden_units:]) + dot_over(
+        normed_odd, grad_odd[:, hidden_units:]
+    )
+    way, gate_sum, up_sum, hidden_even, hidden_odd = lax.optimization_barrier(
+        (way, gate_sum, up_sum, hidden_even, hidden_odd)
+    )
+    out_sum = dot_over(hidden_even, cot_near[:half]) + dot_over(
+        hidden_odd, cot_near[half:]
+    )
     normed_two_grad = run_steps(steps, way)
     middle_grad = cot_low.astype(F32) + norm_back(
         normed_two_grad, gains[1], inv_two, unit_two
     )
     mix_low = middle_grad.astype(BF16)
     gain_two_grad = jnp.sum(normed_two_grad * unit_two, axis=0)
-    middle_grad, mix_low, gain_two_grad, out_sum, hidden, sent = (
-        lax.optimization_barrier(
-            (middle_grad, mix_low, gain_two_grad, out_sum, hidden, sent)
+    (
+        middle_grad,
+        mix_low,
+        gain_two_grad,
+        out_sum,
+        hidden_even,
+        hidden_odd,
+        sent,
+    ) = lax.optimization_barrier(
+        (
+            middle_grad,
+            mix_low,
+            gain_two_grad,
+            out_sum,
+            hidden_even,
+            hidden_odd,
+            sent,
         )
     )
 
@@ -1016,17 +1113,23 @@
     way, sent = lax.optimization_barrier((steps.send(None), sent))
     way = steps.send(way)
     normed_far = far_gather(jnp.concatenate(sent)) if recompute else ()
-    feed_send = dot(hidden[half:], mlp_out_weight).astype(BF16)
-    feed_keep = dot(hidden[:half], mlp_out_weight)
+    feed_send = dot(hidden_odd, mlp_out_weight).astype(BF16)
+    feed_keep = dot(hidden_even, mlp_out_weight)
     way, feed_send, feed_keep = lax.optimization_barrier((way, feed_send, feed_keep))
     mix_even = run_steps(steps, way)
-    mix_near = jnp.concatenate([mix_even, other_core(mix_even)])
-    mix_near, cot_far = lax.optimization_barrier((mix_near, cot_far))
-    mixed_grad = from_near(dot_back(mix_near, out_win))
+    mix_odd = other_core(mix_even)
+    even_grad = dot_back(mix_even, out_win)
+    mix_odd, even_grad, cot_far = lax.optimization_barrier(
+        (mix_odd, even_grad, cot_far)
+    )
+    mix_near = jnp.concatenate([mix_even, mix_odd])
+    mixed_grad = jnp.concatenate([even_grad, dot_back(mix_odd, out_win)])
     out_grad = lax.dynamic_slice_in_dim(
         dot_over(mixed_near, mix_near).astype(BF16), offset, own
     )
-    gate_half, state_grad = gate_backward(mixed_grad, states, gate_rows, head, chunk)
+    gate_half, state_grad = gate_backward(
+        mixed_grad, states, gate_rows, head, chunk, size
+    )
     state_grad, out_grad = lax.optimization_barrier((state_grad, out_grad))
     out_grad = line_step(out_grad, 0)
 

time: 629 us -> 611 us (0.971)
  Pallas kernels: 191 us -> 180 us
  waiting for transfers between devices: 92.3 us -> 83.6 us
    pallas_call x4 -> x2, Pallas kernels: 25.7 us -> 13.3 us  [move_rows(): pl.pallas_call(move_kernel, grid_spec=pltpu.PrefetchScalarGridSpec(num_sc...]
    ppermute x43, waiting for transfers between devices: 74.2 us -> 67.4 us  [swap(): lax.ppermute(block, axis, [(i, i ^ bit) for i in range(lax.axis_size(axis...]
    dot_general x6 -> x9, matrix products: 28.3 us -> 31.5 us  [dot_over(): lax.dot_general(left, right, (((0,), (0,)), ((), ())), preferred_element_...]
    dot_general x7 -> x8, matrix products: 33.5 us -> 35.4 us  [dot(): return jnp.dot(left, right, preferred_element_type=F32)]
    dot_general x6 -> x8, matrix products: 28.1 us -> 26.6 us  [dot_back(): lax.dot_general(left, right, (((1,), (1,)), ((), ())), preferred_element_...]
    unnamed x107 -> x122, local copies, waits for them, and re-layouts: 22.3 us -> 22.1 us
  transfers between devices with their start and end apart: 58 -> 58, of which waited for: 22 -> 23; matrix products, arithmetic and copies ran while one was open for 31% -> 32% of each run, Pallas kernels for 30% -> 29%
where the time goes in v4:
time: 611 us; the launch traced here: 601 us
  Pallas kernels  180 us (29%)
  matrix products  93.4 us (15%)
  waiting for transfers between devices  83.6 us (14%)
  starting transfers between devices  82.7 us (14%)
  other arithmetic  62.9 us (10%)
  local copies, waits for them, and re-layouts  61.4 us (10%)
  blocking collectives  21.5 us (4%)
  between operations  16 us (3%)
    pallas_call x3, Pallas kernels, far_grads(): pl.pallas_call(far_kernel, grid=(total // rows,), in_specs=[data, data, h...  91.1 us
    ppermute x43, waiting for transfers between devices, swap(): lax.ppermute(block, axis, [(i, i ^ bit) for i in range(lax.axis_size(axis...  67.4 us
    ppermute x43, starting transfers between devices, swap(): lax.ppermute(block, axis, [(i, i ^ bit) for i in range(lax.axis_size(axis...  57.8 us
    dot_general x8, matrix products, dot(): return jnp.dot(left, right, preferred_element_type=F32)  35.4 us
    dot_general x9, matrix products, dot_over(): lax.dot_general(left, right, (((0,), (0,)), ((), ())), preferred_element_...  31.5 us
    dot_general x8, matrix products, dot_back(): lax.dot_general(left, right, (((1,), (1,)), ((), ())), preferred_element_...  26.6 us
    unnamed x122, local copies, waits for them, and re-layouts  22.1 us
    all_to_all x1, blocking collectives, exchange(): lax.all_to_all(blocks, 'wide', split_axis=0, concat_axis=0, tiled=True)  21.5 us
  transfers between devices with their start and end apart: 58, of which 23 were waited for; matrix products, arithmetic and copies ran while one was open for 32% of the time, Pallas kernels for 29%

profile of v4, /device:TPU:0, one launch (start us, length us, event | category | flops | bytes accessed | tf_op | source)
XLA Modules:
  0.0 601.1 jit_solution(4597742325700167597)
XLA Ops:
  14.8 6.5 %split_columns.2 = bf16[8,128,512]{2,1,0:T(8,128)(2,1)} custom-call(s32[9]{0:T(128)} %stack.138.table_ref, bf16[256,2,2560]{2,1,0:T(2,128)(2,1)} %src.3), custom_call_target="tpu_custom_call" | custom-call | tf_op jit(solution)/shard_map/split_columns/pallas_call | solution.py:573
  21.2 6.7 %split_columns.3 = bf16[8,128,512]{2,1,0:T(8,128)(2,1)} custom-call(s32[9]{0:T(128)} %stack.138.table_ref, bf16[256,2,2560]{2,1,0:T(2,128)(2,1)} %src.3), custom_call_target="tpu_custom_call" | custom-call | tf_op jit(solution)/shard_map/split_columns/pallas_call | solution.py:573
  28.0 21.5 %all_to_all.25 = bf16[8,128,512]{2,1,0:T(8,128)(2,1)} all-to-all(bf16[8,128,512]{2,1,0:T(8,128)(2,1)S(1)} %copy-done.21), channel_id=1, replica_groups=mesh['seq'=4,'wide'=8] {'wide'}, dimensions={0} | all-to-all | bytes 2097152 | tf_op jit(solution)/shard_map/all_to_all | solution.py:785
  55.3 6.9 %copy.85 = bf16[256,8,2,768]{3,1,2,0:T(8,128)(2,1)} copy(bf16[256,8,2,768]{3,2,1,0:T(2,128)(2,1)} %bitcast.344) | data formatting | bytes 12582912
  63.7 10.0 %collective-permute-done = bf16[8,128,512]{2,1,0:T(8,128)(2,1)} collective-permute-done((bf16[8,128,512]{2,1,0:T(8,128)(2,1)}, bf16[8,128,512]{2,1,0:T(8,128)(2,1)}, u32[]{:S(2)}, u32[]{:S(2)}) %collective-permute-start) | collective-permute-done | bytes 1048608 | tf_op jit(solution)/shard_map/ppermute | solution.py:693
  82.5 7.3 %norm_packed.1 = bf16[1024,2048]{1,0:T(8,128)(2,1)} custom-call(bf16[8,224,2048]{2,1,0:T(8,128)(2,1)} %bitcast.333, f32[1,2048]{1,0:T(1,128)} %bitcast.383), custom_call_target="tpu_custom_call" | custom-call | tf_op jit(solution)/shard_map/norm_packed/pallas_call | solution.py:655
  107.2 6.5 %fusion.73.refs_0_.refs_1_ = f32[1024,512]{1,0:T(8,128)} fusion(bf16[1024,2048]{1,0:T(8,128)(2,1)} %norm_packed.1, bf16[2048,512]{1,0:T(8,128)(2,1)} %bitcast.340), kind=kOutput, calls=%fused_computation.209 | convolution fusion | flops 2147483648 | bytes 8388608 | tf_op jit(solution)/shard_map/dot_general | solution.py:19
  113.7 12.3 %recur_forward.1 = (f32[1024,512]{1,0:T(8,128)}, f32[1024,512]{1,0:T(8,128)}, f32[1024,512]{1,0:T(8,128)}, f32[1024,512]{1,0:T(8,128)}, f32[1024,512]{1,0:T(8,12...) custom-call(f32[1024,512]{1,0:T(8,128)} %fusion.73.refs_0_.refs_1_, ...), custom_call_target="tpu_custom_call" | custom-call | tf_op jit(solution)/shard_map/recur_forward/pallas_call | solution.py:289
  134.6 7.2 %mix_forward.1 = (bf16[1024,512]{1,0:T(8,128)(2,1)}, f32[1024,512]{1,0:T(8,128)}) custom-call(f32[1024,512]{1,0:T(8,128)} %fusion.74.refs_0_.refs_1_, f32[1024,512]{1,0:T(8,128)} %fusion.74.refs_0_.refs_1_, f32[1024,512]{1,0:T(8,128)} %get-tuple-element.173.refs_2_.states_ref), custom_call_target="tpu_custom_call" | custom-call | tf_op jit(solution)/shard_map/mix_forward/pallas_call | solution.py:251
  184.1 7.3 %move_rows.2 = bf16[1024,2048]{1,0:T(8,128)(2,1)} custom-call(s32[8]{0:T(128)} %stack.153.table_ref, bf16[1024,2048]{1,0:T(8,128)(2,1)} %all-gather.6.cloned.1.call-done.src), custom_call_target="tpu_custom_call" | custom-call | tf_op jit(solution)/shard_map/move_rows/pallas_call | solution.py:804
  197.3 5.3 collective-permute-done.14
  207.1 8.8 %collective-permute-start.17 = (bf16[128,2048]{1,0:T(8,128)(2,1)}, bf16[128,2048]{1,0:T(8,128)(2,1)S(1)}, u32[]{:S(2)}, u32[]{:S(2)}) collective-permute-start(bf16[128,2048]{1,0:T(8,128)(2,1)} %copy-done.33), channel_id=1, source_target_pairs={{0,8},{8,0},{16,24},{24,16},{1,9},{9,1},{17,25},{25,17},{2,10},{10... | collective-permute-start | bytes 1572872 | tf_op jit(solution)/shard_map/ppermute | solution.py:693
  215.9 5.9 fusion.76
  224.8 6.4 %fusion.75 = f32[512,1536]{1,0:T(8,128)S(1)} fusion(bf16[512,2048]{1,0:T(8,128)(2,1)S(1)} %collective-permute-done.16, bf16[2048,1536]{1,0:T(8,128)(2,1)} %bitcast.313), kind=kOutput, calls=%fused_computation.211 | convolution fusion | flops 3221225472 | bytes 11534336 | tf_op jit(solution)/shard_map/dot_general | solution.py:19
  256.5 4.4 convolution_add_fusion.1.own_up_ref
  261.0 10.0 %collective-permute-done.19 = bf16[2,128,1024]{2,1,0:T(8,128)(2,1)S(1)} collective-permute-done((bf16[2,128,1024]{2,1,0:T(8,128)(2,1)S(1)}, bf16[2,128,1024]{2,1,0:T(8,128)(2,1)S(1)}, u32[]{:S(2)}, u32[]{:S(2)}) %collective-permute-start.19) | collective-permute-done | bytes 524320 | tf_op jit(solution)/shard_map/ppermute | solution.py:693
  277.2 4.5 convolution_add_fusion.own_out_ref
  281.8 4.8 collective-permute-done.22
  293.1 10.9 %collective-permute-done.25 = bf16[128,1024]{1,0:T(8,128)(2,1)} collective-permute-done((bf16[128,1024]{1,0:T(8,128)(2,1)S(1)}, bf16[128,1024]{1,0:T(8,128)(2,1)}, u32[]{:S(2)}, u32[]{:S(2)}) %collective-permute-start.25) | collective-permute-done | bytes 262176 | tf_op jit(solution)/shard_map/ppermute | solution.py:693
  320.2 5.6 collective-permute-done.28
  335.1 8.3 %gate_backward.1 = (bf16[1024,512]{1,0:T(8,128)(2,1)}, f32[1024,512]{1,0:T(8,128)}) custom-call(f32[1024,512]{1,0:T(8,128)} %pad_maximum_fusion.3.mgrad_ref, f32[1024,512]{1,0:T(8,128)} %get-tuple-element.173.refs_2_.states_ref, f32[1024,512]{1,0:T(8,128)} %get-tuple-element.238.gperm_ref), custom_call_target="tpu_custom_call" | custom-call | tf_op jit(solution)/shard_map/gate_backward/pallas_call | solution.py:373
  343.4 4.6 fusion
  351.5 11.7 %recur_backward.1 = (bf16[1024,512]{1,0:T(8,128)(2,1)}, f32[2,2,256,256]{3,2,1,0:T(8,128)}, f32[8,512]{1,0:T(8,128)}) custom-call(f32[1024,512]{1,0:T(8,128)} %get-tuple-element.240.sgrad_ref, f32[1024,512]{1,0:T(8,128)} %get-tuple-element.173.refs_2_.states_ref, f32[1024,512]{1,0:T(8,128)} %get-tuple-element.241.decay_ref, ...), custom_call_target="tpu_custom_call" | custom-call | tf_op jit(solution)/shard_map/recur_backward/pallas_call | solution.py:524
  380.0 6.1 %move_rows.3 = bf16[1024,640]{1,0:T(8,128)(2,1)} custom-call(s32[8]{0:T(128)} %stack.153.table_ref, bf16[1024,640]{1,0:T(8,128)(2,1)} %pad_maximum_fusion.8.src), custom_call_target="tpu_custom_call" | custom-call | tf_op jit(solution)/shard_map/move_rows/pallas_call | solution.py:804
  386.1 5.1 convolution_convert_fusion.3
  402.3 30.2 %far_grads.3 = (f32[2048,768]{1,0:T(8,128)}, f32[2048,768]{1,0:T(8,128)}, f32[768,2048]{1,0:T(8,128)}) custom-call(bf16[3072,2048]{1,0:T(8,128)(2,1)} %all-gather.10.cloned.1.call-done.normed_ref, bf16[3072,2048]{1,0:T(8,128)(2,1)} %all-gather.8.cloned.1.call-done.cot_ref, ...), custom_call_target="tpu_custom_call", output_to_operand_aliasing={{0}: (5, {}), {1}: (6, {}), {2}: (7, {})} | custom-call | flops 1024 | bytes 1024 | tf_op jit(solution)/shard_map/far_grads/pallas_call | solution.py:626
  454.7 30.6 %far_grads.4 = (f32[2048,768]{1,0:T(8,128)}, f32[2048,768]{1,0:T(8,128)}, f32[768,2048]{1,0:T(8,128)}) custom-call(bf16[3072,2048]{1,0:T(8,128)(2,1)} %all-gather.10.cloned.1.call-done.normed_ref, bf16[3072,2048]{1,0:T(8,128)(2,1)} %all-gather.8.cloned.1.call-done.cot_ref, ...), custom_call_target="tpu_custom_call", output_to_operand_aliasing={{0}: (5, {}), {1}: (6, {}), {2}: (7, {})} | custom-call | flops 1024 | bytes 1024 | tf_op jit(solution)/shard_map/far_grads/pallas_call | solution.py:626
  485.3 6.0 %collective-permute-done.36 = bf16[320,2048]{1,0:T(8,128)(2,1)} collective-permute-done((bf16[320,2048]{1,0:T(8,128)(2,1)}, bf16[320,2048]{1,0:T(8,128)(2,1)}, u32[]{:S(2)}, u32[]{:S(2)}) %collective-permute-start.36) | collective-permute-done | bytes 1310752 | tf_op jit(solution)/shard_map/ppermute | solution.py:757
  514.8 30.3 %far_grads.5 = (f32[2048,768]{1,0:T(8,128)}, f32[2048,768]{1,0:T(8,128)}, f32[768,2048]{1,0:T(8,128)}) custom-call(bf16[3072,2048]{1,0:T(8,128)(2,1)} %all-gather.10.cloned.1.call-done.normed_ref, bf16[3072,2048]{1,0:T(8,128)(2,1)} %all-gather.8.cloned.1.call-done.cot_ref, ...), custom_call_target="tpu_custom_call", output_to_operand_aliasing={{0}: (5, {}), {1}: (6, {}), {2}: (7, {})} | custom-call | flops 1024 | bytes 1024 | tf_op jit(solution)/shard_map/far_grads/pallas_call | solution.py:626
  565.4 10.2 %join_halves.3 = f32[2048,2,768]{2,1,0:T(2,128)} custom-call(f32[2048,768]{1,0:T(8,128)} %get-tuple-element.313.first, f32[2048,768]{1,0:T(8,128)} %get-tuple-element.314.second), custom_call_target="tpu_custom_call" | custom-call | tf_op jit(solution)/shard_map/join_halves/pallas_call | solution.py:677
  580.7 6.2 %all-reduce.7.cloned.1.call-done = (bf16[256,2560]{1,0:T(8,128)(2,1)}, bf16[2,10,256,32]{2,3,1,0:T(8,128)(2,1)}) async-done(((bf16[256,2560]{1,0:T(8,128)(2,1)}, bf16[2,10,256,32]{2,3,1,0:T(8,128)(2,1)}), (bf16[256,2560]{1,0:T(8,128)(2,1)}, bf16[2,10,256,32]{2,3,1,0:T(8,128)(2,1)})) %all-reduce.7.cloned.1.call-update) | async-done | bytes 1638416 | tf_op jit(solution)/shard_map/psum | solution.py:1226
  588.8 5.1 join_halves.2
  (385 shorter events, 272.0 us)
Async XLA Ops:
  7.2 73.3 %all-gather.12.cloned.1.call-start = ((), (), s32[]{:S(2)}) async-start(), calls=%async_computation.9 | async-start | bytes 8257536 | tf_op jit(solution)/shard_map/all_gather | solution.py:914
  51.0 41.1 %all-to-all-start.1 = ((bf16[8,128,512]{2,1,0:T(8,128)(2,1)}), bf16[8,128,512]{2,1,0:T(8,128)(2,1)}, u32[]{:S(2)}, u32[]{:S(2)}) async-start(bf16[8,128,512]{2,1,0:T(8,128)(2,1)} %split_columns.3), calls=%async_computation.1 | async-start | bytes 2097152 | tf_op jit(solution)/shard_map/all_to_all | solution.py:785
  55.2 90.1 %all-gather.6.cloned.1.call-start = ((), (), s32[]{:S(2)}) async-start(), calls=%async_computation.5 | async-start | bytes 4718592 | tf_op jit(solution)/shard_map/all_gather | solution.py:991
  92.1 238.6 %all-gather.8.cloned.1.call-start = ((), (), s32[]{:S(2)}) async-start(), calls=%async_computation.6 | async-start | bytes 14155776 | tf_op jit(solution)/shard_map/all_gather | solution.py:893
  92.1 33.9 %collective-permute-start.1 = (bf16[8,128,512]{2,1,0:T(8,128)(2,1)}, bf16[8,128,512]{2,1,0:T(8,128)(2,1)}, u32[]{:S(2)}, u32[]{:S(2)}) collective-permute-start(bf16[8,128,512]{2,1,0:T(8,128)(2,1)} %all-to-all-done.1), channel_id=1, source_target_pairs={{0,8},{8,0},{16,24},{24,16},{1,9},{9,1},{17,25},{25,17},{2,10},{10... | collective-permute-start | bytes 3145736 | tf_op jit(solution)/shard_map/ppermute | solution.py:693
  95.9 30.1 %collective-permute-start.2 = (bf16[192,2048]{1,0:T(8,128)(2,1)}, bf16[192,2048]{1,0:T(8,128)(2,1)}, u32[]{:S(2)}, u32[]{:S(2)}) collective-permute-start(bf16[192,2048]{1,0:T(8,128)(2,1)} %get-tuple-element.349), channel_id=1, source_target_pairs={{0,1},{1,2},{2,3},{3,4},{4,5},{5,6},{6,7},{8,9},{9,10},{10,11},{11... | collective-permute-start | bytes 2359304 | tf_op jit(solution)/shard_map/ppermute | solution.py:976
  98.7 27.3 %collective-permute-start.3 = (bf16[192,2048]{1,0:T(8,128)(2,1)}, bf16[192,2048]{1,0:T(8,128)(2,1)}, u32[]{:S(2)}, u32[]{:S(2)}) collective-permute-start(bf16[192,2048]{1,0:T(8,128)(2,1)} %get-tuple-element.348), channel_id=1, source_target_pairs={{1,0},{2,1},{3,2},{4,3},{5,4},{6,5},{7,6},{9,8},{10,9},{11,10},{12... | collective-permute-start | bytes 2359304 | tf_op jit(solution)/shard_map/ppermute | solution.py:982
  147.0 44.4 %collective-permute-start.11 = (bf16[128,2048]{1,0:T(8,128)(2,1)}, bf16[128,2048]{1,0:T(8,128)(2,1)}, u32[]{:S(2)}, u32[]{:S(2)}) collective-permute-start(bf16[128,2048]{1,0:T(8,128)(2,1)} %bitcast.353), channel_id=1, source_target_pairs={{0,8},{8,0},{16,24},{24,16},{1,9},{9,1},{17,25},{25,17},{2,10},{10... | collective-permute-start | bytes 1572872 | tf_op jit(solution)/shard_map/ppermute | solution.py:693
  147.6 43.7 %collective-permute-start.12 = (bf16[128,2048]{1,0:T(8,128)(2,1)}, bf16[128,2048]{1,0:T(8,128)(2,1)}, u32[]{:S(2)}, u32[]{:S(2)}) collective-permute-start(bf16[128,2048]{1,0:T(8,128)(2,1)} %bitcast.354), channel_id=1, source_target_pairs={{0,16},{8,24},{16,0},{24,8},{1,17},{9,25},{17,1},{25,9},{2,18},{10... | collective-permute-start | bytes 1572872 | tf_op jit(solution)/shard_map/ppermute | solution.py:693
  150.0 41.3 %collective-permute-start.13 = (bf16[128,2048]{1,0:T(8,128)(2,1)}, bf16[128,2048]{1,0:T(8,128)(2,1)}, u32[]{:S(2)}, u32[]{:S(2)}) collective-permute-start(bf16[128,2048]{1,0:T(8,128)(2,1)} %bitcast.355), channel_id=1, source_target_pairs={{0,24},{8,16},{16,8},{24,0},{1,25},{9,17},{17,9},{25,1},{2,26},{10... | collective-permute-start | bytes 1572872 | tf_op jit(solution)/shard_map/ppermute | solution.py:693
  207.0 188.0 %all-gather.10.cloned.1.call-start = ((), (), s32[]{:S(2)}) async-start(), calls=%async_computation.7 | async-start | bytes 14155776 | tf_op jit(solution)/shard_map/all_gather | solution.py:893
  207.1 31.0 %collective-permute-start.17 = (bf16[128,2048]{1,0:T(8,128)(2,1)}, bf16[128,2048]{1,0:T(8,128)(2,1)S(1)}, u32[]{:S(2)}, u32[]{:S(2)}) collective-permute-start(bf16[128,2048]{1,0:T(8,128)(2,1)} %copy-done.33), channel_id=1, source_target_pairs={{0,8},{8,0},{16,24},{24,16},{1,9},{9,1},{17,25},{25,17},{2,10},{10... | collective-permute-start | bytes 1572872 | tf_op jit(solution)/shard_map/ppermute | solution.py:693
  239.0 50.4 %collective-permute-start.23 = (bf16[128,2048]{1,0:T(8,128)(2,1)S(1)}, bf16[128,2048]{1,0:T(8,128)(2,1)}, u32[]{:S(2)}, u32[]{:S(2)}) collective-permute-start(bf16[128,2048]{1,0:T(8,128)(2,1)S(1)} %copy-done.34), channel_id=1, source_target_pairs={{0,16},{8,24},{16,0},{24,8},{1,17},{9,25},{17,1},{25,9},{2,18},{10... | collective-permute-start | bytes 1572872 | tf_op jit(solution)/shard_map/ppermute | solution.py:693
  241.3 48.1 %collective-permute-start.24 = (bf16[128,2048]{1,0:T(8,128)(2,1)S(1)}, bf16[128,2048]{1,0:T(8,128)(2,1)}, u32[]{:S(2)}, u32[]{:S(2)}) collective-permute-start(bf16[128,2048]{1,0:T(8,128)(2,1)S(1)} %copy-done.34), channel_id=1, source_target_pairs={{0,24},{8,16},{16,8},{24,0},{1,25},{9,17},{17,9},{25,1},{2,26},{10... | collective-permute-start | bytes 1572872 | tf_op jit(solution)/shard_map/ppermute | solution.py:693
  246.3 24.7 %collective-permute-start.19 = (bf16[2,128,1024]{2,1,0:T(8,128)(2,1)S(1)}, bf16[2,128,1024]{2,1,0:T(8,128)(2,1)S(1)}, u32[]{:S(2)}, u32[]{:S(2)}) collective-permute-start(bf16[2,128,1024]{2,1,0:T(8,128)(2,1)S(1)} %slice_bitcast_fusion.19), channel_id=1, source_target_pairs={{0,2},{1,3},{2,0},{3,1},{4,6},{5,7},{6,4},{7,5},{8,10},{9,11},{10,... | collective-permute-start | bytes 1572872 | tf_op jit(solution)/shard_map/ppermute | solution.py:693
  247.1 25.0 %collective-permute-start.20 = (bf16[2,128,1024]{2,1,0:T(8,128)(2,1)S(1)}, bf16[2,128,1024]{2,1,0:T(8,128)(2,1)S(1)}, u32[]{:S(2)}, u32[]{:S(2)}) collective-permute-start(bf16[2,128,1024]{2,1,0:T(8,128)(2,1)S(1)} %slice_bitcast_fusion.18), channel_id=1, source_target_pairs={{0,4},{1,5},{2,6},{3,7},{4,0},{5,1},{6,2},{7,3},{8,12},{9,13},{10,... | collective-permute-start | bytes 1572872 | tf_op jit(solution)/shard_map/ppermute | solution.py:693
  349.2 42.0 %collective-permute-start.30 = (bf16[320,2048]{1,0:T(8,128)(2,1)}, bf16[320,2048]{1,0:T(8,128)(2,1)}, u32[]{:S(2)}, u32[]{:S(2)}) collective-permute-start(bf16[320,2048]{1,0:T(8,128)(2,1)} %dynamic-slice_convert_fusion), channel_id=1, source_target_pairs={{0,8},{24,16},{1,9},{25,17},{2,10},{26,18},{3,11},{27,19},{4,12},{... | collective-permute-start | bytes 3932168 | tf_op jit(solution)/shard_map/ppermute | solution.py:757
  394.9 40.9 %collective-permute-start.31 = (bf16[512,2048]{1,0:T(8,128)(2,1)}, bf16[512,2048]{1,0:T(8,128)(2,1)}, u32[]{:S(2)}, u32[]{:S(2)}) collective-permute-start(bf16[512,2048]{1,0:T(8,128)(2,1)} %convolution_convert_fusion.3), channel_id=1, source_target_pairs={{0,1},{1,0},{2,3},{3,2},{4,5},{5,4},{6,7},{7,6},{8,9},{9,8},{10,11... | collective-permute-start | bytes 6291464 | tf_op jit(solution)/shard_map/ppermute | solution.py:693
  395.0 37.6 %collective-permute-start.32 = (bf16[320,2048]{1,0:T(8,128)(2,1)}, bf16[320,2048]{1,0:T(8,128)(2,1)}, u32[]{:S(2)}, u32[]{:S(2)}) collective-permute-start(bf16[320,2048]{1,0:T(8,128)(2,1)} %add_convert_fusion.1), channel_id=1, source_target_pairs={{8,16},{16,8},{9,17},{17,9},{10,18},{18,10},{11,19},{19,11},{12,20... | collective-permute-start | bytes 3932168 | tf_op jit(solution)/shard_map/ppermute | solution.py:757
  398.0 37.8 %all-to-all-start.3 = ((bf16[8,256,320]{1,2,0:T(8,128)(2,1)}), bf16[8,256,320]{1,2,0:T(8,128)(2,1)S(1)}, u32[]{:S(2)}, u32[]{:S(2)}) async-start(bf16[8,256,320]{1,2,0:T(8,128)(2,1)} %copy.62), calls=%async_computation.3 | async-start | bytes 2621440 | tf_op jit(solution)/shard_map/all_to_all | solution.py:785
  401.8 111.3 %all-reduce.5.cloned.1.call-start = ((), (), s32[]{:S(2)}) async-start(), calls=%async_computation.8 | async-start | bytes 2621440 | tf_op jit(solution)/shard_map/psum | solution.py:1176
  401.9 92.0 %collective-permute-start.35 = (bf16[512,2048]{1,0:T(8,128)(2,1)}, bf16[512,2048]{1,0:T(8,128)(2,1)}, u32[]{:S(2)}, u32[]{:S(2)}) collective-permute-start(bf16[512,2048]{1,0:T(8,128)(2,1)} %convolution_convert_fusion), channel_id=1, source_target_pairs={{0,1},{1,0},{2,3},{3,2},{4,5},{5,4},{6,7},{7,6},{8,9},{9,8},{10,11... | collective-permute-start | bytes 6291464 | tf_op jit(solution)/shard_map/ppermute | solution.py:693
  435.9 55.5 %collective-permute-start.36 = (bf16[320,2048]{1,0:T(8,128)(2,1)}, bf16[320,2048]{1,0:T(8,128)(2,1)}, u32[]{:S(2)}, u32[]{:S(2)}) collective-permute-start(bf16[320,2048]{1,0:T(8,128)(2,1)} %add_convert_fusion), channel_id=1, source_target_pairs={{8,0},{16,24},{9,1},{17,25},{10,2},{18,26},{11,3},{19,27},{12,4},{... | collective-permute-start | bytes 3932168 | tf_op jit(solution)/shard_map/ppermute | solution.py:757
  446.3 47.6 %collective-permute-start.33 = (bf16[2,128,1024]{2,1,0:T(8,128)(2,1)}, bf16[2,128,1024]{2,1,0:T(8,128)(2,1)}, u32[]{:S(2)}, u32[]{:S(2)}) collective-permute-start(bf16[2,128,1024]{2,1,0:T(8,128)(2,1)} %slice_bitcast_fusion.15), channel_id=1, source_target_pairs={{0,2},{1,3},{2,0},{3,1},{4,6},{5,7},{6,4},{7,5},{8,10},{9,11},{10,... | collective-permute-start | bytes 1572872 | tf_op jit(solution)/shard_map/ppermute | solution.py:693
  448.8 45.0 %collective-permute-start.34 = (bf16[2,128,1024]{2,1,0:T(8,128)(2,1)}, bf16[2,128,1024]{2,1,0:T(8,128)(2,1)}, u32[]{:S(2)}, u32[]{:S(2)}) collective-permute-start(bf16[2,128,1024]{2,1,0:T(8,128)(2,1)} %slice_bitcast_fusion.14), channel_id=1, source_target_pairs={{0,4},{1,5},{2,6},{3,7},{4,0},{5,1},{6,2},{7,3},{8,12},{9,13},{10,... | collective-permute-start | bytes 1572872 | tf_op jit(solution)/shard_map/ppermute | solution.py:693
  451.2 42.7 %all-to-all-start.4 = ((bf16[8,2,2,32,256]{4,3,1,2,0:T(8,128)(2,1)}), bf16[8,2,2,32,256]{4,3,1,2,0:T(8,128)(2,1)S(1)}, u32[]{:S(2)}, u32[]{:S(2)}) async-start(bf16[8,2,2,32,256]{4,3,1,2,0:T(8,128)(2,1)} %bitcast.310), calls=%async_computation.4 | async-start | bytes 1048576 | tf_op jit(solution)/shard_map/all_to_all | solution.py:785
  454.7 132.2 %all-reduce.7.cloned.1.call-start = ((), (), s32[]{:S(2)}) async-start(), calls=%async_computation.10 | async-start | bytes 3276800 | tf_op jit(solution)/shard_map/psum | solution.py:1226
  503.6 41.5 %collective-permute-start.37 = (bf16[128,1024]{1,0:T(8,128)(2,1)}, bf16[128,1024]{1,0:T(8,128)(2,1)S(1)}, u32[]{:S(2)}, u32[]{:S(2)}) collective-permute-start(bf16[128,1024]{1,0:T(8,128)(2,1)} %fusion.56), channel_id=1, source_target_pairs={{0,4},{1,5},{2,6},{3,7},{4,0},{5,1},{6,2},{7,3},{8,12},{9,13},{10,... | collective-permute-start | bytes 786440 | tf_op jit(solution)/shard_map/ppermute | solution.py:693
  507.9 37.2 %collective-permute-start.38 = (bf16[128,1024]{1,0:T(8,128)(2,1)}, bf16[128,1024]{1,0:T(8,128)(2,1)}, u32[]{:S(2)}, u32[]{:S(2)}) collective-permute-start(bf16[128,1024]{1,0:T(8,128)(2,1)} %fusion.57), channel_id=1, source_target_pairs={{0,2},{1,3},{2,0},{3,1},{4,6},{5,7},{6,4},{7,5},{8,10},{9,11},{10,... | collective-permute-start | bytes 786440 | tf_op jit(solution)/shard_map/ppermute | solution.py:693
  509.4 35.7 %collective-permute-start.39 = (bf16[2,128,1024]{2,1,0:T(8,128)(2,1)}, bf16[2,128,1024]{2,1,0:T(8,128)(2,1)}, u32[]{:S(2)}, u32[]{:S(2)}) collective-permute-start(bf16[2,128,1024]{2,1,0:T(8,128)(2,1)} %slice_bitcast_fusion.13), channel_id=1, source_target_pairs={{0,2},{1,3},{2,0},{3,1},{4,6},{5,7},{6,4},{7,5},{8,10},{9,11},{10,... | collective-permute-start | bytes 1572872 | tf_op jit(solution)/shard_map/ppermute | solution.py:693
  510.0 35.2 %collective-permute-start.40 = (bf16[2,128,1024]{2,1,0:T(8,128)(2,1)}, bf16[2,128,1024]{2,1,0:T(8,128)(2,1)}, u32[]{:S(2)}, u32[]{:S(2)}) collective-permute-start(bf16[2,128,1024]{2,1,0:T(8,128)(2,1)} %slice_bitcast_fusion.12), channel_id=1, source_target_pairs={{0,4},{1,5},{2,6},{3,7},{4,0},{5,1},{6,2},{7,3},{8,12},{9,13},{10,... | collective-permute-start | bytes 1572872 | tf_op jit(solution)/shard_map/ppermute | solution.py:693
  553.4 25.3 %collective-permute-start.42 = (bf16[128,1024]{1,0:T(8,128)(2,1)}, bf16[128,1024]{1,0:T(8,128)(2,1)S(1)}, u32[]{:S(2)}, u32[]{:S(2)}) collective-permute-start(bf16[128,1024]{1,0:T(8,128)(2,1)} %fusion.59), channel_id=1, source_target_pairs={{0,2},{1,3},{2,0},{3,1},{4,6},{5,7},{6,4},{7,5},{8,10},{9,11},{10,... | collective-permute-start | bytes 786440 | tf_op jit(solution)/shard_map/ppermute | solution.py:693
  (77 other events, 740.6 us)
Sparse Core Ops, SparseCore 0:
  14.3 66.1 all-gather.11
  92.2 44.6 all-gather.5
  207.1 100.9 all-gather.7
  309.8 75.2 all-gather.9
  439.1 73.6 all-reduce.4
  515.1 71.8 all-reduce.6

commit v5 on v4

--- a/solution.py
+++ b/solution.py
@@ -112,7 +112,7 @@
         ext[rows8(s + halo), :] = v
         return 0
 
-    lax.fori_loop(0, steps, load, 0, unroll=4)
+    lax.fori_loop(0, steps, load, 0, unroll=8)
     for back in range(1, halo + 1):
         v = ext[rows8(halo + steps - back), :]
         ext[rows8(halo - back), :] = roll_down(v, tail[back - 1 : back, :])
@@ -133,7 +133,7 @@
         low_ref[block(i), :] = out.astype(BF16)
         return 0
 
-    lax.fori_loop(0, steps // big, conv, 0)
+    lax.fori_loop(0, steps // big, conv, 0, unroll=2)
     low = low_ref[...]
     pre0[...] = dot_back(low, gw_ref[0, 0])
     pre1[...] = dot_back(low, gw_ref[1, 0])
@@ -150,7 +150,7 @@
         pre0[block(i), :] = scale * g * low_ref[block(i), :].astype(F32)
         return 0
 
-    lax.fori_loop(0, steps // big, gates, 0)
+    lax.fori_loop(0, steps // big, gates, 0, unroll=2)
 
     def scan(s, hp):
         h, p = hp
@@ -162,7 +162,7 @@
         return h, p
 
     zero = jnp.zeros((SUB, width), F32)
-    h, p = lax.fori_loop(0, steps, scan, (zero, zero + 1.0), unroll=8)
+    h, p = lax.fori_loop(0, steps, scan, (zero, zero + 1.0), unroll=16)
     for shift in (1, 2, 4):
         keep = sub_iota(width) >= shift
         h = h + p * jnp.where(keep, pltpu.roll(h, shift, 0), 0.0)
@@ -439,7 +439,7 @@
         return a * c, a * q
 
     zero = jnp.zeros((SUB, width), F32)
-    u, q = lax.fori_loop(0, steps, scan, (zero, zero + 1.0), unroll=8)
+    u, q = lax.fori_loop(0, steps, scan, (zero, zero + 1.0), unroll=16)
     for shift in (1, 2, 4):
         keep = sub_iota(width) < SUB - shift
         u = u + q * jnp.where(keep, pltpu.roll(u, SUB - shift, 0), 0.0)
@@ -474,7 +474,7 @@
         return sum_r + pr, sum_i + pi, sum_d + dgrad * r
 
     lowf[...] = low_ref[...].astype(F32)
-    sum_r, sum_i, sum_d = lax.fori_loop(0, steps, gates, (zero, zero, zero), unroll=4)
+    sum_r, sum_i, sum_d = lax.fori_loop(0, steps, gates, (zero, zero, zero), unroll=8)
     low = low_ref[...]
     pr = pre[0].astype(BF16)
     pi = pre[1].astype(BF16)
@@ -502,7 +502,7 @@
         strided_store(gout, s, steps, out)
         return (*new, new_bias)
 
-    acc = lax.fori_loop(0, steps, conv, (zero,) * (taps + 1), unroll=4)
+    acc = lax.fori_loop(0, steps, conv, (zero,) * (taps + 1), unroll=8)
     for n in range(width // LANES):
         pgrad_ref[:, n * LANES : (n + 1) * LANES] = gout[n].astype(BF16)
     for n, v in enumerate((*acc, sum_r, sum_i, sum_d)):

time: 611 us -> 611 us (level)
  transfers between devices with their start and end apart: 58 -> 58, of which waited for: 23 -> 24; matrix products, arithmetic and copies ran while one was open for 32% -> 32% of each run, Pallas kernels for 29% -> 29%
where the time goes in v5:
time: 611 us; the launch traced here: 601 us
  Pallas kernels  179 us (29%)
  matrix products  93.2 us (15%)
  waiting for transfers between devices  84.3 us (14%)
  starting transfers between devices  82.4 us (13%)
  other arithmetic  62.9 us (10%)
  local copies, waits for them, and re-layouts  61.4 us (10%)
  blocking collectives  21.5 us (4%)
  between operations  16 us (3%)
    pallas_call x3, Pallas kernels, far_grads(): pl.pallas_call(far_kernel, grid=(total // rows,), in_specs=[data, data, h...  91.1 us
    ppermute x43, waiting for transfers between devices, swap(): lax.ppermute(block, axis, [(i, i ^ bit) for i in range(lax.axis_size(axis...  67.1 us
    ppermute x43, starting transfers between devices, swap(): lax.ppermute(block, axis, [(i, i ^ bit) for i in range(lax.axis_size(axis...  57.8 us
    dot_general x8, matrix products, dot(): return jnp.dot(left, right, preferred_element_type=F32)  35.4 us
    dot_general x9, matrix products, dot_over(): lax.dot_general(left, right, (((0,), (0,)), ((), ())), preferred_element_...  31.3 us
    dot_general x8, matrix products, dot_back(): lax.dot_general(left, right, (((1,), (1,)), ((), ())), preferred_element_...  26.6 us
    unnamed x122, local copies, waits for them, and re-layouts  22.2 us
    all_to_all x1, blocking collectives, exchange(): lax.all_to_all(blocks, 'wide', split_axis=0, concat_axis=0, tiled=True)  21.5 us
  transfers between devices with their start and end apart: 58, of which 24 were waited for; matrix products, arithmetic and copies ran while one was open for 32% of the time, Pallas kernels for 29%

profile of v5, /device:TPU:0, one launch (start us, length us, event | category | flops | bytes accessed | tf_op | source)
XLA Modules:
  0.0 600.6 jit_solution(1728848573565960731)
XLA Ops:
  14.8 6.5 %split_columns.2 = bf16[8,128,512]{2,1,0:T(8,128)(2,1)} custom-call(s32[9]{0:T(128)} %stack.138.table_ref, bf16[256,2,2560]{2,1,0:T(2,128)(2,1)} %src.3), custom_call_target="tpu_custom_call" | custom-call | tf_op jit(solution)/shard_map/split_columns/pallas_call | solution.py:573
  21.2 6.7 %split_columns.3 = bf16[8,128,512]{2,1,0:T(8,128)(2,1)} custom-call(s32[9]{0:T(128)} %stack.138.table_ref, bf16[256,2,2560]{2,1,0:T(2,128)(2,1)} %src.3), custom_call_target="tpu_custom_call" | custom-call | tf_op jit(solution)/shard_map/split_columns/pallas_call | solution.py:573
  28.0 21.5 %all_to_all.25 = bf16[8,128,512]{2,1,0:T(8,128)(2,1)} all-to-all(bf16[8,128,512]{2,1,0:T(8,128)(2,1)S(1)} %copy-done.21), channel_id=1, replica_groups=mesh['seq'=4,'wide'=8] {'wide'}, dimensions={0} | all-to-all | bytes 2097152 | tf_op jit(solution)/shard_map/all_to_all | solution.py:785
  55.3 6.9 %copy.85 = bf16[256,8,2,768]{3,1,2,0:T(8,128)(2,1)} copy(bf16[256,8,2,768]{3,2,1,0:T(2,128)(2,1)} %bitcast.344) | data formatting | bytes 12582912
  63.7 10.0 %collective-permute-done = bf16[8,128,512]{2,1,0:T(8,128)(2,1)} collective-permute-done((bf16[8,128,512]{2,1,0:T(8,128)(2,1)}, bf16[8,128,512]{2,1,0:T(8,128)(2,1)}, u32[]{:S(2)}, u32[]{:S(2)}) %collective-permute-start) | collective-permute-done | bytes 1048608 | tf_op jit(solution)/shard_map/ppermute | solution.py:693
  82.5 7.3 %norm_packed.1 = bf16[1024,2048]{1,0:T(8,128)(2,1)} custom-call(bf16[8,224,2048]{2,1,0:T(8,128)(2,1)} %bitcast.333, f32[1,2048]{1,0:T(1,128)} %bitcast.383), custom_call_target="tpu_custom_call" | custom-call | tf_op jit(solution)/shard_map/norm_packed/pallas_call | solution.py:655
  107.2 6.5 %fusion.73.refs_0_.refs_1_ = f32[1024,512]{1,0:T(8,128)} fusion(bf16[1024,2048]{1,0:T(8,128)(2,1)} %norm_packed.1, bf16[2048,512]{1,0:T(8,128)(2,1)} %bitcast.340), kind=kOutput, calls=%fused_computation.209 | convolution fusion | flops 2147483648 | bytes 8388608 | tf_op jit(solution)/shard_map/dot_general | solution.py:19
  113.7 11.7 %recur_forward.1 = (f32[1024,512]{1,0:T(8,128)}, f32[1024,512]{1,0:T(8,128)}, f32[1024,512]{1,0:T(8,128)}, f32[1024,512]{1,0:T(8,128)}, f32[1024,512]{1,0:T(8,12...) custom-call(f32[1024,512]{1,0:T(8,128)} %fusion.73.refs_0_.refs_1_, ...), custom_call_target="tpu_custom_call" | custom-call | tf_op jit(solution)/shard_map/recur_forward/pallas_call | solution.py:289
  134.0 7.2 %mix_forward.1 = (bf16[1024,512]{1,0:T(8,128)(2,1)}, f32[1024,512]{1,0:T(8,128)}) custom-call(f32[1024,512]{1,0:T(8,128)} %fusion.74.refs_0_.refs_1_, f32[1024,512]{1,0:T(8,128)} %fusion.74.refs_0_.refs_1_, f32[1024,512]{1,0:T(8,128)} %get-tuple-element.173.refs_2_.states_ref), custom_call_target="tpu_custom_call" | custom-call | tf_op jit(solution)/shard_map/mix_forward/pallas_call | solution.py:251
  183.5 7.3 %move_rows.2 = bf16[1024,2048]{1,0:T(8,128)(2,1)} custom-call(s32[8]{0:T(128)} %stack.153.table_ref, bf16[1024,2048]{1,0:T(8,128)(2,1)} %all-gather.6.cloned.1.call-done.src), custom_call_target="tpu_custom_call" | custom-call | tf_op jit(solution)/shard_map/move_rows/pallas_call | solution.py:804
  196.7 5.3 collective-permute-done.14
  206.5 8.9 %collective-permute-start.17 = (bf16[128,2048]{1,0:T(8,128)(2,1)}, bf16[128,2048]{1,0:T(8,128)(2,1)S(1)}, u32[]{:S(2)}, u32[]{:S(2)}) collective-permute-start(bf16[128,2048]{1,0:T(8,128)(2,1)} %copy-done.33), channel_id=1, source_target_pairs={{0,8},{8,0},{16,24},{24,16},{1,9},{9,1},{17,25},{25,17},{2,10},{10... | collective-permute-start | bytes 1572872 | tf_op jit(solution)/shard_map/ppermute | solution.py:693
  215.4 5.9 fusion.76
  224.3 6.4 %fusion.75 = f32[512,1536]{1,0:T(8,128)S(1)} fusion(bf16[512,2048]{1,0:T(8,128)(2,1)S(1)} %collective-permute-done.16, bf16[2048,1536]{1,0:T(8,128)(2,1)} %bitcast.313), kind=kOutput, calls=%fused_computation.211 | convolution fusion | flops 3221225472 | bytes 11534336 | tf_op jit(solution)/shard_map/dot_general | solution.py:19
  256.0 4.4 convolution_add_fusion.1.own_up_ref
  260.4 10.0 %collective-permute-done.19 = bf16[2,128,1024]{2,1,0:T(8,128)(2,1)S(1)} collective-permute-done((bf16[2,128,1024]{2,1,0:T(8,128)(2,1)S(1)}, bf16[2,128,1024]{2,1,0:T(8,128)(2,1)S(1)}, u32[]{:S(2)}, u32[]{:S(2)}) %collective-permute-start.19) | collective-permute-done | bytes 524320 | tf_op jit(solution)/shard_map/ppermute | solution.py:693
  276.7 4.5 convolution_add_fusion.own_out_ref
  281.2 4.8 collective-permute-done.22
  292.5 11.0 %collective-permute-done.25 = bf16[128,1024]{1,0:T(8,128)(2,1)} collective-permute-done((bf16[128,1024]{1,0:T(8,128)(2,1)S(1)}, bf16[128,1024]{1,0:T(8,128)(2,1)}, u32[]{:S(2)}, u32[]{:S(2)}) %collective-permute-start.25) | collective-permute-done | bytes 262176 | tf_op jit(solution)/shard_map/ppermute | solution.py:693
  319.6 5.5 collective-permute-done.28
  334.4 8.3 %gate_backward.1 = (bf16[1024,512]{1,0:T(8,128)(2,1)}, f32[1024,512]{1,0:T(8,128)}) custom-call(f32[1024,512]{1,0:T(8,128)} %pad_maximum_fusion.3.mgrad_ref, f32[1024,512]{1,0:T(8,128)} %get-tuple-element.173.refs_2_.states_ref, f32[1024,512]{1,0:T(8,128)} %get-tuple-element.238.gperm_ref), custom_call_target="tpu_custom_call" | custom-call | tf_op jit(solution)/shard_map/gate_backward/pallas_call | solution.py:373
  342.7 4.5 fusion
  350.7 11.5 %recur_backward.1 = (bf16[1024,512]{1,0:T(8,128)(2,1)}, f32[2,2,256,256]{3,2,1,0:T(8,128)}, f32[8,512]{1,0:T(8,128)}) custom-call(f32[1024,512]{1,0:T(8,128)} %get-tuple-element.240.sgrad_ref, f32[1024,512]{1,0:T(8,128)} %get-tuple-element.173.refs_2_.states_ref, f32[1024,512]{1,0:T(8,128)} %get-tuple-element.241.decay_ref, ...), custom_call_target="tpu_custom_call" | custom-call | tf_op jit(solution)/shard_map/recur_backward/pallas_call | solution.py:524
  379.0 6.1 %move_rows.3 = bf16[1024,640]{1,0:T(8,128)(2,1)} custom-call(s32[8]{0:T(128)} %stack.153.table_ref, bf16[1024,640]{1,0:T(8,128)(2,1)} %pad_maximum_fusion.8.src), custom_call_target="tpu_custom_call" | custom-call | tf_op jit(solution)/shard_map/move_rows/pallas_call | solution.py:804
  385.1 5.1 convolution_convert_fusion.3
  401.7 30.2 %far_grads.3 = (f32[2048,768]{1,0:T(8,128)}, f32[2048,768]{1,0:T(8,128)}, f32[768,2048]{1,0:T(8,128)}) custom-call(bf16[3072,2048]{1,0:T(8,128)(2,1)} %all-gather.10.cloned.1.call-done.normed_ref, bf16[3072,2048]{1,0:T(8,128)(2,1)} %all-gather.8.cloned.1.call-done.cot_ref, ...), custom_call_target="tpu_custom_call", output_to_operand_aliasing={{0}: (5, {}), {1}: (6, {}), {2}: (7, {})} | custom-call | flops 1024 | bytes 1024 | tf_op jit(solution)/shard_map/far_grads/pallas_call | solution.py:626
  453.9 30.6 %far_grads.4 = (f32[2048,768]{1,0:T(8,128)}, f32[2048,768]{1,0:T(8,128)}, f32[768,2048]{1,0:T(8,128)}) custom-call(bf16[3072,2048]{1,0:T(8,128)(2,1)} %all-gather.10.cloned.1.call-done.normed_ref, bf16[3072,2048]{1,0:T(8,128)(2,1)} %all-gather.8.cloned.1.call-done.cot_ref, ...), custom_call_target="tpu_custom_call", output_to_operand_aliasing={{0}: (5, {}), {1}: (6, {}), {2}: (7, {})} | custom-call | flops 1024 | bytes 1024 | tf_op jit(solution)/shard_map/far_grads/pallas_call | solution.py:626
  484.5 6.3 %collective-permute-done.36 = bf16[320,2048]{1,0:T(8,128)(2,1)} collective-permute-done((bf16[320,2048]{1,0:T(8,128)(2,1)}, bf16[320,2048]{1,0:T(8,128)(2,1)}, u32[]{:S(2)}, u32[]{:S(2)}) %collective-permute-start.36) | collective-permute-done | bytes 1310752 | tf_op jit(solution)/shard_map/ppermute | solution.py:757
  513.9 30.3 %far_grads.5 = (f32[2048,768]{1,0:T(8,128)}, f32[2048,768]{1,0:T(8,128)}, f32[768,2048]{1,0:T(8,128)}) custom-call(bf16[3072,2048]{1,0:T(8,128)(2,1)} %all-gather.10.cloned.1.call-done.normed_ref, bf16[3072,2048]{1,0:T(8,128)(2,1)} %all-gather.8.cloned.1.call-done.cot_ref, ...), custom_call_target="tpu_custom_call", output_to_operand_aliasing={{0}: (5, {}), {1}: (6, {}), {2}: (7, {})} | custom-call | flops 1024 | bytes 1024 | tf_op jit(solution)/shard_map/far_grads/pallas_call | solution.py:626
  564.9 10.2 %join_halves.3 = f32[2048,2,768]{2,1,0:T(2,128)} custom-call(f32[2048,768]{1,0:T(8,128)} %get-tuple-element.313.first, f32[2048,768]{1,0:T(8,128)} %get-tuple-element.314.second), custom_call_target="tpu_custom_call" | custom-call | tf_op jit(solution)/shard_map/join_halves/pallas_call | solution.py:677
  580.3 6.2 %all-reduce.7.cloned.1.call-done = (bf16[256,2560]{1,0:T(8,128)(2,1)}, bf16[2,10,256,32]{2,3,1,0:T(8,128)(2,1)}) async-done(((bf16[256,2560]{1,0:T(8,128)(2,1)}, bf16[2,10,256,32]{2,3,1,0:T(8,128)(2,1)}), (bf16[256,2560]{1,0:T(8,128)(2,1)}, bf16[2,10,256,32]{2,3,1,0:T(8,128)(2,1)})) %all-reduce.7.cloned.1.call-update) | async-done | bytes 1638416 | tf_op jit(solution)/shard_map/psum | solution.py:1226
  588.3 5.1 join_halves.2
  (385 shorter events, 272.1 us)
Async XLA Ops:
  7.2 73.3 %all-gather.12.cloned.1.call-start = ((), (), s32[]{:S(2)}) async-start(), calls=%async_computation.9 | async-start | bytes 8257536 | tf_op jit(solution)/shard_map/all_gather | solution.py:914
  51.0 41.1 %all-to-all-start.1 = ((bf16[8,128,512]{2,1,0:T(8,128)(2,1)}), bf16[8,128,512]{2,1,0:T(8,128)(2,1)}, u32[]{:S(2)}, u32[]{:S(2)}) async-start(bf16[8,128,512]{2,1,0:T(8,128)(2,1)} %split_columns.3), calls=%async_computation.1 | async-start | bytes 2097152 | tf_op jit(solution)/shard_map/all_to_all | solution.py:785
  55.2 89.6 %all-gather.6.cloned.1.call-start = ((), (), s32[]{:S(2)}) async-start(), calls=%async_computation.5 | async-start | bytes 4718592 | tf_op jit(solution)/shard_map/all_gather | solution.py:991
  92.1 237.9 %all-gather.8.cloned.1.call-start = ((), (), s32[]{:S(2)}) async-start(), calls=%async_computation.6 | async-start | bytes 14155776 | tf_op jit(solution)/shard_map/all_gather | solution.py:893
  92.1 33.3 %collective-permute-start.1 = (bf16[8,128,512]{2,1,0:T(8,128)(2,1)}, bf16[8,128,512]{2,1,0:T(8,128)(2,1)}, u32[]{:S(2)}, u32[]{:S(2)}) collective-permute-start(bf16[8,128,512]{2,1,0:T(8,128)(2,1)} %all-to-all-done.1), channel_id=1, source_target_pairs={{0,8},{8,0},{16,24},{24,16},{1,9},{9,1},{17,25},{25,17},{2,10},{10... | collective-permute-start | bytes 3145736 | tf_op jit(solution)/shard_map/ppermute | solution.py:693
  95.9 29.5 %collective-permute-start.2 = (bf16[192,2048]{1,0:T(8,128)(2,1)}, bf16[192,2048]{1,0:T(8,128)(2,1)}, u32[]{:S(2)}, u32[]{:S(2)}) collective-permute-start(bf16[192,2048]{1,0:T(8,128)(2,1)} %get-tuple-element.349), channel_id=1, source_target_pairs={{0,1},{1,2},{2,3},{3,4},{4,5},{5,6},{6,7},{8,9},{9,10},{10,11},{11... | collective-permute-start | bytes 2359304 | tf_op jit(solution)/shard_map/ppermute | solution.py:976
  98.7 26.7 %collective-permute-start.3 = (bf16[192,2048]{1,0:T(8,128)(2,1)}, bf16[192,2048]{1,0:T(8,128)(2,1)}, u32[]{:S(2)}, u32[]{:S(2)}) collective-permute-start(bf16[192,2048]{1,0:T(8,128)(2,1)} %get-tuple-element.348), channel_id=1, source_target_pairs={{1,0},{2,1},{3,2},{4,3},{5,4},{6,5},{7,6},{9,8},{10,9},{11,10},{12... | collective-permute-start | bytes 2359304 | tf_op jit(solution)/shard_map/ppermute | solution.py:982
  146.5 44.3 %collective-permute-start.11 = (bf16[128,2048]{1,0:T(8,128)(2,1)}, bf16[128,2048]{1,0:T(8,128)(2,1)}, u32[]{:S(2)}, u32[]{:S(2)}) collective-permute-start(bf16[128,2048]{1,0:T(8,128)(2,1)} %bitcast.353), channel_id=1, source_target_pairs={{0,8},{8,0},{16,24},{24,16},{1,9},{9,1},{17,25},{25,17},{2,10},{10... | collective-permute-start | bytes 1572872 | tf_op jit(solution)/shard_map/ppermute | solution.py:693
  147.0 43.8 %collective-permute-start.12 = (bf16[128,2048]{1,0:T(8,128)(2,1)}, bf16[128,2048]{1,0:T(8,128)(2,1)}, u32[]{:S(2)}, u32[]{:S(2)}) collective-permute-start(bf16[128,2048]{1,0:T(8,128)(2,1)} %bitcast.354), channel_id=1, source_target_pairs={{0,16},{8,24},{16,0},{24,8},{1,17},{9,25},{17,1},{25,9},{2,18},{10... | collective-permute-start | bytes 1572872 | tf_op jit(solution)/shard_map/ppermute | solution.py:693
  149.4 41.4 %collective-permute-start.13 = (bf16[128,2048]{1,0:T(8,128)(2,1)}, bf16[128,2048]{1,0:T(8,128)(2,1)}, u32[]{:S(2)}, u32[]{:S(2)}) collective-permute-start(bf16[128,2048]{1,0:T(8,128)(2,1)} %bitcast.355), channel_id=1, source_target_pairs={{0,24},{8,16},{16,8},{24,0},{1,25},{9,17},{17,9},{25,1},{2,26},{10... | collective-permute-start | bytes 1572872 | tf_op jit(solution)/shard_map/ppermute | solution.py:693
  206.4 188.1 %all-gather.10.cloned.1.call-start = ((), (), s32[]{:S(2)}) async-start(), calls=%async_computation.7 | async-start | bytes 14155776 | tf_op jit(solution)/shard_map/all_gather | solution.py:893
  206.5 31.0 %collective-permute-start.17 = (bf16[128,2048]{1,0:T(8,128)(2,1)}, bf16[128,2048]{1,0:T(8,128)(2,1)S(1)}, u32[]{:S(2)}, u32[]{:S(2)}) collective-permute-start(bf16[128,2048]{1,0:T(8,128)(2,1)} %copy-done.33), channel_id=1, source_target_pairs={{0,8},{8,0},{16,24},{24,16},{1,9},{9,1},{17,25},{25,17},{2,10},{10... | collective-permute-start | bytes 1572872 | tf_op jit(solution)/shard_map/ppermute | solution.py:693
  238.5 50.4 %collective-permute-start.23 = (bf16[128,2048]{1,0:T(8,128)(2,1)S(1)}, bf16[128,2048]{1,0:T(8,128)(2,1)}, u32[]{:S(2)}, u32[]{:S(2)}) collective-permute-start(bf16[128,2048]{1,0:T(8,128)(2,1)S(1)} %copy-done.34), channel_id=1, source_target_pairs={{0,16},{8,24},{16,0},{24,8},{1,17},{9,25},{17,1},{25,9},{2,18},{10... | collective-permute-start | bytes 1572872 | tf_op jit(solution)/shard_map/ppermute | solution.py:693
  240.8 48.1 %collective-permute-start.24 = (bf16[128,2048]{1,0:T(8,128)(2,1)S(1)}, bf16[128,2048]{1,0:T(8,128)(2,1)}, u32[]{:S(2)}, u32[]{:S(2)}) collective-permute-start(bf16[128,2048]{1,0:T(8,128)(2,1)S(1)} %copy-done.34), channel_id=1, source_target_pairs={{0,24},{8,16},{16,8},{24,0},{1,25},{9,17},{17,9},{25,1},{2,26},{10... | collective-permute-start | bytes 1572872 | tf_op jit(solution)/shard_map/ppermute | solution.py:693
  246.5 25.0 %collective-permute-start.20 = (bf16[2,128,1024]{2,1,0:T(8,128)(2,1)S(1)}, bf16[2,128,1024]{2,1,0:T(8,128)(2,1)S(1)}, u32[]{:S(2)}, u32[]{:S(2)}) collective-permute-start(bf16[2,128,1024]{2,1,0:T(8,128)(2,1)S(1)} %slice_bitcast_fusion.18), channel_id=1, source_target_pairs={{0,4},{1,5},{2,6},{3,7},{4,0},{5,1},{6,2},{7,3},{8,12},{9,13},{10,... | collective-permute-start | bytes 1572872 | tf_op jit(solution)/shard_map/ppermute | solution.py:693
  348.4 41.8 %collective-permute-start.30 = (bf16[320,2048]{1,0:T(8,128)(2,1)}, bf16[320,2048]{1,0:T(8,128)(2,1)}, u32[]{:S(2)}, u32[]{:S(2)}) collective-permute-start(bf16[320,2048]{1,0:T(8,128)(2,1)} %dynamic-slice_convert_fusion), channel_id=1, source_target_pairs={{0,8},{24,16},{1,9},{25,17},{2,10},{26,18},{3,11},{27,19},{4,12},{... | collective-permute-start | bytes 3932168 | tf_op jit(solution)/shard_map/ppermute | solution.py:757
  369.4 25.1 %all-to-all-start.2 = ((bf16[8,256,320]{1,2,0:T(8,128)(2,1)}), bf16[8,256,320]{1,2,0:T(8,128)(2,1)S(1)}, u32[]{:S(2)}, u32[]{:S(2)}) async-start(bf16[8,256,320]{1,2,0:T(8,128)(2,1)} %copy.61), calls=%async_computation.2 | async-start | bytes 2621440 | tf_op jit(solution)/shard_map/all_to_all | solution.py:785
  394.5 40.8 %collective-permute-start.31 = (bf16[512,2048]{1,0:T(8,128)(2,1)}, bf16[512,2048]{1,0:T(8,128)(2,1)}, u32[]{:S(2)}, u32[]{:S(2)}) collective-permute-start(bf16[512,2048]{1,0:T(8,128)(2,1)} %convolution_convert_fusion.3), channel_id=1, source_target_pairs={{0,1},{1,0},{2,3},{3,2},{4,5},{5,4},{6,7},{7,6},{8,9},{9,8},{10,11... | collective-permute-start | bytes 6291464 | tf_op jit(solution)/shard_map/ppermute | solution.py:693
  394.5 37.4 %collective-permute-start.32 = (bf16[320,2048]{1,0:T(8,128)(2,1)}, bf16[320,2048]{1,0:T(8,128)(2,1)}, u32[]{:S(2)}, u32[]{:S(2)}) collective-permute-start(bf16[320,2048]{1,0:T(8,128)(2,1)} %add_convert_fusion.1), channel_id=1, source_target_pairs={{8,16},{16,8},{9,17},{17,9},{10,18},{18,10},{11,19},{19,11},{12,20... | collective-permute-start | bytes 3932168 | tf_op jit(solution)/shard_map/ppermute | solution.py:757
  397.5 37.7 %all-to-all-start.3 = ((bf16[8,256,320]{1,2,0:T(8,128)(2,1)}), bf16[8,256,320]{1,2,0:T(8,128)(2,1)S(1)}, u32[]{:S(2)}, u32[]{:S(2)}) async-start(bf16[8,256,320]{1,2,0:T(8,128)(2,1)} %copy.62), calls=%async_computation.3 | async-start | bytes 2621440 | tf_op jit(solution)/shard_map/all_to_all | solution.py:785
  401.1 111.2 %all-reduce.5.cloned.1.call-start = ((), (), s32[]{:S(2)}) async-start(), calls=%async_computation.8 | async-start | bytes 2621440 | tf_op jit(solution)/shard_map/psum | solution.py:1176
  401.2 92.2 %collective-permute-start.35 = (bf16[512,2048]{1,0:T(8,128)(2,1)}, bf16[512,2048]{1,0:T(8,128)(2,1)}, u32[]{:S(2)}, u32[]{:S(2)}) collective-permute-start(bf16[512,2048]{1,0:T(8,128)(2,1)} %convolution_convert_fusion), channel_id=1, source_target_pairs={{0,1},{1,0},{2,3},{3,2},{4,5},{5,4},{6,7},{7,6},{8,9},{9,8},{10,11... | collective-permute-start | bytes 6291464 | tf_op jit(solution)/shard_map/ppermute | solution.py:693
  435.2 55.6 %collective-permute-start.36 = (bf16[320,2048]{1,0:T(8,128)(2,1)}, bf16[320,2048]{1,0:T(8,128)(2,1)}, u32[]{:S(2)}, u32[]{:S(2)}) collective-permute-start(bf16[320,2048]{1,0:T(8,128)(2,1)} %add_convert_fusion), channel_id=1, source_target_pairs={{8,0},{16,24},{9,1},{17,25},{10,2},{18,26},{11,3},{19,27},{12,4},{... | collective-permute-start | bytes 3932168 | tf_op jit(solution)/shard_map/ppermute | solution.py:757
  445.6 47.7 %collective-permute-start.33 = (bf16[2,128,1024]{2,1,0:T(8,128)(2,1)}, bf16[2,128,1024]{2,1,0:T(8,128)(2,1)}, u32[]{:S(2)}, u32[]{:S(2)}) collective-permute-start(bf16[2,128,1024]{2,1,0:T(8,128)(2,1)} %slice_bitcast_fusion.15), channel_id=1, source_target_pairs={{0,2},{1,3},{2,0},{3,1},{4,6},{5,7},{6,4},{7,5},{8,10},{9,11},{10,... | collective-permute-start | bytes 1572872 | tf_op jit(solution)/shard_map/ppermute | solution.py:693
  448.0 45.4 %collective-permute-start.34 = (bf16[2,128,1024]{2,1,0:T(8,128)(2,1)}, bf16[2,128,1024]{2,1,0:T(8,128)(2,1)}, u32[]{:S(2)}, u32[]{:S(2)}) collective-permute-start(bf16[2,128,1024]{2,1,0:T(8,128)(2,1)} %slice_bitcast_fusion.14), channel_id=1, source_target_pairs={{0,4},{1,5},{2,6},{3,7},{4,0},{5,1},{6,2},{7,3},{8,12},{9,13},{10,... | collective-permute-start | bytes 1572872 | tf_op jit(solution)/shard_map/ppermute | solution.py:693
  450.4 43.0 %all-to-all-start.4 = ((bf16[8,2,2,32,256]{4,3,1,2,0:T(8,128)(2,1)}), bf16[8,2,2,32,256]{4,3,1,2,0:T(8,128)(2,1)S(1)}, u32[]{:S(2)}, u32[]{:S(2)}) async-start(bf16[8,2,2,32,256]{4,3,1,2,0:T(8,128)(2,1)} %bitcast.310), calls=%async_computation.4 | async-start | bytes 1048576 | tf_op jit(solution)/shard_map/all_to_all | solution.py:785
  453.9 132.5 %all-reduce.7.cloned.1.call-start = ((), (), s32[]{:S(2)}) async-start(), calls=%async_computation.10 | async-start | bytes 3276800 | tf_op jit(solution)/shard_map/psum | solution.py:1226
  503.1 41.1 %collective-permute-start.37 = (bf16[128,1024]{1,0:T(8,128)(2,1)}, bf16[128,1024]{1,0:T(8,128)(2,1)S(1)}, u32[]{:S(2)}, u32[]{:S(2)}) collective-permute-start(bf16[128,1024]{1,0:T(8,128)(2,1)} %fusion.56), channel_id=1, source_target_pairs={{0,4},{1,5},{2,6},{3,7},{4,0},{5,1},{6,2},{7,3},{8,12},{9,13},{10,... | collective-permute-start | bytes 786440 | tf_op jit(solution)/shard_map/ppermute | solution.py:693
  507.4 36.8 %collective-permute-start.38 = (bf16[128,1024]{1,0:T(8,128)(2,1)}, bf16[128,1024]{1,0:T(8,128)(2,1)}, u32[]{:S(2)}, u32[]{:S(2)}) collective-permute-start(bf16[128,1024]{1,0:T(8,128)(2,1)} %fusion.57), channel_id=1, source_target_pairs={{0,2},{1,3},{2,0},{3,1},{4,6},{5,7},{6,4},{7,5},{8,10},{9,11},{10,... | collective-permute-start | bytes 786440 | tf_op jit(solution)/shard_map/ppermute | solution.py:693
  508.9 35.4 %collective-permute-start.39 = (bf16[2,128,1024]{2,1,0:T(8,128)(2,1)}, bf16[2,128,1024]{2,1,0:T(8,128)(2,1)}, u32[]{:S(2)}, u32[]{:S(2)}) collective-permute-start(bf16[2,128,1024]{2,1,0:T(8,128)(2,1)} %slice_bitcast_fusion.13), channel_id=1, source_target_pairs={{0,2},{1,3},{2,0},{3,1},{4,6},{5,7},{6,4},{7,5},{8,10},{9,11},{10,... | collective-permute-start | bytes 1572872 | tf_op jit(solution)/shard_map/ppermute | solution.py:693
  509.5 34.8 %collective-permute-start.40 = (bf16[2,128,1024]{2,1,0:T(8,128)(2,1)}, bf16[2,128,1024]{2,1,0:T(8,128)(2,1)}, u32[]{:S(2)}, u32[]{:S(2)}) collective-permute-start(bf16[2,128,1024]{2,1,0:T(8,128)(2,1)} %slice_bitcast_fusion.12), channel_id=1, source_target_pairs={{0,4},{1,5},{2,6},{3,7},{4,0},{5,1},{6,2},{7,3},{8,12},{9,13},{10,... | collective-permute-start | bytes 1572872 | tf_op jit(solution)/shard_map/ppermute | solution.py:693
  552.7 25.5 %collective-permute-start.42 = (bf16[128,1024]{1,0:T(8,128)(2,1)}, bf16[128,1024]{1,0:T(8,128)(2,1)S(1)}, u32[]{:S(2)}, u32[]{:S(2)}) collective-permute-start(bf16[128,1024]{1,0:T(8,128)(2,1)} %fusion.59), channel_id=1, source_target_pairs={{0,2},{1,3},{2,0},{3,1},{4,6},{5,7},{6,4},{7,5},{8,10},{9,11},{10,... | collective-permute-start | bytes 786440 | tf_op jit(solution)/shard_map/ppermute | solution.py:693
  (77 other events, 741.4 us)
Sparse Core Ops, SparseCore 0:
  14.3 66.1 all-gather.11
  92.2 44.6 all-gather.5
  206.5 100.9 all-gather.7
  309.3 75.8 all-gather.9
  438.4 73.8 all-reduce.4
  514.6 71.8 all-reduce.6
